TPU v7x, 32 devices: a whole 2x2x4 slice. The times are simulated.
32 devices in a mesh: dp: 4 (over y, x), blk: 2 (over core), sp: 4 (over z).
Axes of the slice: x: 2, y: 2, z: 4, core: 2. Of those that a mesh axis runs over, the one named last changes fastest.
Arguments:
- tokens: bfloat16 [4096, 2048], P(('dp', 'blk', 'sp')), may hold values from -24 to 24
- query_weight: bfloat16 [2048, 2048], P(('dp', 'blk', 'sp')), may hold values from -1 to 1
- key_weight: bfloat16 [2048, 2048], P(('dp', 'blk', 'sp')), may hold values from -1 to 1
- value_weight: bfloat16 [2048, 2048], P(('dp', 'blk', 'sp')), may hold values from -0.125 to 0.125
- output_weight: bfloat16 [2048, 2048], P(('dp', 'blk', 'sp')), may hold values from -0.5 to 0.5
- router_weight: bfloat16 [2048, 64], P(('dp', 'blk', 'sp')), may hold values from -16 to 16
- attention_gain: bfloat16 [2048], P(('dp', 'blk', 'sp')), may hold values from 0.099609375 to 1.8984375
- query_gain: bfloat16 [2048], P(('dp', 'blk', 'sp')), may hold values from 0.6 to 1.4
- key_gain: bfloat16 [2048], P(('dp', 'blk', 'sp')), may hold values from 0.6 to 1.4
- feature_gain: bfloat16 [2048], P(('dp', 'blk', 'sp')), may hold values from 0.099609375 to 1.8984375
- gate_weight: bfloat16 [64, 2048, 1024], P(('dp', 'sp'), None, 'blk'), may hold values from -0.125 to 0.125
- up_weight: bfloat16 [64, 2048, 1024], P(('dp', 'sp'), None, 'blk'), may hold values from -0.125 to 0.125
- down_weight: bfloat16 [64, 1024, 2048], P(('dp', 'sp'), 'blk'), may hold values from -6 to 6
- routes: int32 [4096, 8], P(('dp', 'blk', 'sp')), may hold values from 0 to 63, all different within a row; in each aligned block of 128 rows (0 to 127, 128 to 255, ...) at most 24 rows name the same one
- cotangent: bfloat16 [4096, 2048], P(('dp', 'blk', 'sp')), may hold values from -6 to 6
Outputs:
- block_output: bfloat16 [4096, 2048], P(('dp', 'blk', 'sp'))
- input_gradient: float32 [4096, 2048], P(('dp', 'blk', 'sp'))
- query_gradient: float32 [2048, 2048], P(('dp', 'blk', 'sp'))
- key_gradient: float32 [2048, 2048], P(('dp', 'blk', 'sp'))
- value_gradient: float32 [2048, 2048], P(('dp', 'blk', 'sp'))
- output_gradient: float32 [2048, 2048], P(('dp', 'blk', 'sp'))
- router_gradient: float32 [2048, 64], P(('dp', 'blk', 'sp'))
- gradient_attention: float32 [2048], P(('dp', 'blk', 'sp'))
- gradient_queries: float32 [2048], P(('dp', 'blk', 'sp'))
- gradient_keys: float32 [2048], P(('dp', 'blk', 'sp'))
- gradient_features: float32 [2048], P(('dp', 'blk', 'sp'))
- gate_gradient: float32 [64, 2048, 1024], P(('dp', 'sp'), None, 'blk')
- up_gradient: float32 [64, 2048, 1024], P(('dp', 'sp'), None, 'blk')
- down_gradient: float32 [64, 1024, 2048], P(('dp', 'sp'), 'blk')
Inputs may be any that keep to these rules, and one draw needn't show every extreme that they name: `routes`: each row names 8 different experts. In the rows of one device no expert is named more than 24 times, a bound that some block reaches.
All inputs are finite; a program needn't handle non-finite values.
Results may differ from a plain program's by a relative error of at most 0.02.
Values may be sent and summed in bfloat16 or wider, within the bound.
A program may use at most 384 MiB of HBM per device.

v0:
```python
import math

import jax
import jax.numpy as jnp
from jax import lax
from jax.sharding import PartitionSpec as P

HEADS = 16
HEAD_DIM = 128
EXPERTS = 64
TOPK = 8
CAP = 24


NORM_EPSILON = 1e-05
ROPE_BASE = 10000.0
MASKED = -1e30


def norm_apply(values, norm_gain):
    return (
        values
        * lax.rsqrt(jnp.mean(values * values, axis=-1, keepdims=True) + NORM_EPSILON)
        * norm_gain
    )


def rope_tables(positions, head_size):
    half_size = head_size // 2
    frequencies = jnp.exp(
        -math.log(ROPE_BASE) * 2.0 * jnp.arange(half_size, dtype=jnp.float32) / head_size
    )
    angles = positions.astype(jnp.float32)[:, None] * frequencies[None, :]
    return (jnp.cos(angles), jnp.sin(angles))


def rotate(values, cosine, sine):
    half_size = values.shape[-1] // 2
    first_half = values[..., :half_size]
    second_half = values[..., half_size:]
    cosine_row = cosine[:, None, :]
    sine_row = sine[:, None, :]
    return jnp.concatenate(
        [
            first_half * cosine_row - second_half * sine_row,
            second_half * cosine_row + first_half * sine_row,
        ],
        axis=-1,
    )


def rank_slots(route_rows):
    flat_experts = route_rows.reshape(-1)
    onehot = (flat_experts[:, None] == jnp.arange(EXPERTS, dtype=jnp.int32)[None, :]).astype(
        jnp.int32
    )
    return (flat_experts, jnp.sum(jnp.cumsum(onehot, axis=0) * onehot, axis=1) - 1)


def body(
    tokens,
    query_weight,
    key_weight,
    value_weight,
    output_weight,
    router_weight,
    attention_gain,
    query_gain,
    key_gain,
    feature_gain,
    gate_weight,
    up_weight,
    down_weight,
    routes,
    cotangent,
):
    sp_size = lax.axis_size("sp")
    blk_size = lax.axis_size("blk")
    dp_size = lax.axis_size("dp")
    tok_rows = tokens.shape[0]
    model_width = tokens.shape[1]
    heads_here = HEADS // sp_size
    head_width = heads_here * HEAD_DIM
    experts_here = gate_weight.shape[0]
    capacity = CAP
    score_scale = 1.0 / math.sqrt(HEAD_DIM)
    (
        query_full,
        key_full,
        value_full,
        output_full,
        router_full,
        gain_attention,
        gain_query,
        gain_key,
        gain_feature,
    ) = (
        lax.all_gather(query_weight, ("dp", "blk", "sp"), axis=0, tiled=True),
        lax.all_gather(key_weight, ("dp", "blk", "sp"), axis=0, tiled=True),
        lax.all_gather(value_weight, ("dp", "blk", "sp"), axis=0, tiled=True),
        lax.all_gather(output_weight, ("dp", "blk", "sp"), axis=0, tiled=True),
        lax.all_gather(router_weight, ("dp", "blk", "sp"), axis=0, tiled=True),
        lax.all_gather(attention_gain, ("dp", "blk", "sp"), axis=0, tiled=True),
        lax.all_gather(query_gain, ("dp", "blk", "sp"), axis=0, tiled=True),
        lax.all_gather(key_gain, ("dp", "blk", "sp"), axis=0, tiled=True),
        lax.all_gather(feature_gain, ("dp", "blk", "sp"), axis=0, tiled=True),
    )
    gain_attention = gain_attention.astype(jnp.float32)
    gain_query = gain_query.astype(jnp.float32)
    gain_key = gain_key.astype(jnp.float32)
    gain_feature = gain_feature.astype(jnp.float32)
    tokens_f = tokens.astype(jnp.float32)
    normed_f, attention_pull = jax.vjp(norm_apply, tokens_f, gain_attention)
    normed = normed_f.astype(jnp.bfloat16)
    query_lin = jnp.dot(normed, query_full, preferred_element_type=jnp.float32)
    key_lin = jnp.dot(normed, key_full, preferred_element_type=jnp.float32)
    value_rows = jnp.dot(normed, value_full, preferred_element_type=jnp.float32).astype(
        jnp.bfloat16
    )
    seq_start = (lax.axis_index("blk") * sp_size + lax.axis_index("sp")) * tok_rows
    cosine, sine = rope_tables(seq_start + jnp.arange(tok_rows, dtype=jnp.int32), HEAD_DIM)

    def rotated(linear, norm_gain):
        normalized = norm_apply(linear, norm_gain).reshape(
            tok_rows, model_width // HEAD_DIM, HEAD_DIM
        )
        return rotate(normalized, cosine, sine).reshape(tok_rows, model_width)

    query_rot, query_pull = jax.vjp(rotated, query_lin, gain_query)
    key_rot, key_pull = jax.vjp(rotated, key_lin, gain_key)
    query_heads, key_heads, value_heads = (
        lax.all_to_all(
            query_rot.astype(jnp.bfloat16).reshape(tok_rows, sp_size, head_width),
            "sp",
            split_axis=1,
            concat_axis=0,
            tiled=True,
        ),
        lax.all_to_all(
            key_rot.astype(jnp.bfloat16).reshape(tok_rows, sp_size, head_width),
            "sp",
            split_axis=1,
            concat_axis=0,
            tiled=True,
        ),
        lax.all_to_all(
            value_rows.reshape(tok_rows, sp_size, head_width),
            "sp",
            split_axis=1,
            concat_axis=0,
            tiled=True,
        ),
    )
    head_rows = sp_size * tok_rows
    keys_all, values_all = (
        lax.all_gather(key_heads, "blk", axis=0, tiled=True),
        lax.all_gather(value_heads, "blk", axis=0, tiled=True),
    )
    key_rows = keys_all.shape[0]
    keys_all = keys_all.reshape(key_rows, heads_here, HEAD_DIM)
    values_all = values_all.reshape(key_rows, heads_here, HEAD_DIM)
    block_rows = math.gcd(512, head_rows)
    blocks = head_rows // block_rows
    query_base = lax.axis_index("blk") * head_rows
    key_places = jnp.arange(key_rows, dtype=jnp.int32)
    query_blocks = query_heads.reshape(blocks, block_rows, heads_here, HEAD_DIM)
    block_starts = jnp.arange(blocks, dtype=jnp.int32) * block_rows

    def masked_scores(block_queries, block_start):
        scores = (
            jnp.einsum("qhd,khd->hqk", block_queries, keys_all, preferred_element_type=jnp.float32)
            * score_scale
        )
        query_places = query_base + block_start + jnp.arange(block_rows, dtype=jnp.int32)
        causal = key_places[None, :] <= query_places[:, None]
        return jnp.where(causal[None], scores, MASKED)

    def attend_block(block_input):
        block_queries, block_start = block_input
        scores = masked_scores(block_queries, block_start)
        row_peak = jnp.max(scores, axis=-1, keepdims=True)
        exponent = jnp.exp(scores - row_peak)
        row_total = jnp.sum(exponent, axis=-1, keepdims=True)
        attn_weights = (exponent / row_total).astype(jnp.bfloat16)
        context = jnp.einsum(
            "hqk,khd->qhd", attn_weights, values_all, preferred_element_type=jnp.float32
        )
        return (context.astype(jnp.bfloat16), (row_peak + jnp.log(row_total))[..., 0])

    context_blocks, logsum = lax.map(attend_block, (query_blocks, block_starts))
    context_rows = lax.all_to_all(
        context_blocks.reshape(head_rows, 1, head_width),
        "sp",
        split_axis=0,
        concat_axis=1,
        tiled=True,
    ).reshape(tok_rows, model_width)
    attended = jnp.dot(context_rows, output_full, preferred_element_type=jnp.float32)
    residual = tokens_f + attended
    features_f, feature_pull = jax.vjp(norm_apply, residual, gain_feature)
    features = features_f.astype(jnp.bfloat16)
    logits = jnp.dot(features, router_full, preferred_element_type=jnp.float32)
    router_probs = jax.nn.softmax(logits, axis=-1)
    flat_experts, slot_rank = rank_slots(routes)
    slot_index = flat_experts * capacity + slot_rank
    token_of = jnp.arange(tok_rows * TOPK, dtype=jnp.int32) // TOPK
    slot_token = jnp.zeros((EXPERTS * capacity,), jnp.int32).at[slot_index].set(token_of)
    slot_used = jnp.zeros((EXPERTS * capacity,), jnp.bool_).at[slot_index].set(True)
    slot_rows = jnp.where(slot_used[:, None], features[slot_token], jnp.zeros((), jnp.bfloat16))

    def spread_halves(per_slot):
        grouped = per_slot.reshape(dp_size, 1, sp_size, experts_here, capacity, model_width)
        grouped = jnp.broadcast_to(
            grouped, (dp_size, blk_size, sp_size, experts_here, capacity, model_width)
        )
        return grouped.reshape(dp_size * blk_size * sp_size, experts_here, capacity, model_width)

    def join_halves(returned):
        grouped = returned.reshape(
            dp_size, blk_size, sp_size, experts_here, capacity, model_width
        ).astype(jnp.float32)
        return jnp.sum(grouped, axis=1).reshape(EXPERTS * capacity, model_width)

    send_rows = spread_halves(slot_rows)
    arrived = lax.all_to_all(
        send_rows, ("dp", "blk", "sp"), split_axis=0, concat_axis=0, tiled=True
    )
    gate_values = jnp.einsum(
        "secd,edf->secf", arrived, gate_weight, preferred_element_type=jnp.float32
    )
    up_values = jnp.einsum("secd,edf->secf", arrived, up_weight, preferred_element_type=jnp.float32)
    hidden = (jax.nn.silu(gate_values) * up_values).astype(jnp.bfloat16)
    part_out = jnp.einsum(
        "secf,efd->secd", hidden, down_weight, preferred_element_type=jnp.float32
    ).astype(jnp.bfloat16)
    returned = lax.all_to_all(
        part_out, ("dp", "blk", "sp"), split_axis=0, concat_axis=0, tiled=True
    )
    expert_out = join_halves(returned)
    route_rows = expert_out[slot_index].reshape(tok_rows, TOPK, model_width)
    route_probs = jnp.take_along_axis(router_probs, routes, axis=1)
    block_output = (residual + jnp.sum(route_probs[:, :, None] * route_rows, axis=1)).astype(
        jnp.bfloat16
    )
    out_grad = cotangent.astype(jnp.float32)
    route_grad = (
        (route_probs[:, :, None] * out_grad[:, None, :])
        .astype(jnp.bfloat16)
        .reshape(tok_rows * TOPK, model_width)
    )
    prob_route = jnp.sum(out_grad[:, None, :] * route_rows, axis=-1)
    expert_ids = jnp.arange(EXPERTS, dtype=jnp.int32)
    prob_grad = jnp.sum(
        jnp.where(routes[:, :, None] == expert_ids[None, None, :], prob_route[:, :, None], 0.0),
        axis=1,
    )
    logit_grad = (
        router_probs * (prob_grad - jnp.sum(prob_grad * router_probs, axis=-1, keepdims=True))
    ).astype(jnp.bfloat16)
    router_grad_full = jnp.dot(features.T, logit_grad, preferred_element_type=jnp.float32)
    gradient_slots = (
        jnp.zeros((EXPERTS * capacity, model_width), jnp.bfloat16).at[slot_index].set(route_grad)
    )
    gradient_send = spread_halves(gradient_slots)
    gradient_arrived, rows_arrived = (
        lax.all_to_all(gradient_send, ("dp", "blk", "sp"), split_axis=0, concat_axis=0, tiled=True),
        lax.all_to_all(send_rows, ("dp", "blk", "sp"), split_axis=0, concat_axis=0, tiled=True),
    )
    gate_values = jnp.einsum(
        "secd,edf->secf", rows_arrived, gate_weight, preferred_element_type=jnp.float32
    )
    up_values = jnp.einsum(
        "secd,edf->secf", rows_arrived, up_weight, preferred_element_type=jnp.float32
    )
    sigmoid_values = jax.nn.sigmoid(gate_values)
    silu_values = gate_values * sigmoid_values
    hidden = (silu_values * up_values).astype(jnp.bfloat16)
    hidden_grad = jnp.einsum(
        "secd,efd->secf", gradient_arrived, down_weight, preferred_element_type=jnp.float32
    ).astype(jnp.bfloat16)
    down_grad_local = jnp.einsum(
        "secf,secd->efd", hidden, gradient_arrived, preferred_element_type=jnp.float32
    )
    hidden_wide = hidden_grad.astype(jnp.float32)
    gate_grad = (
        hidden_wide * up_values * sigmoid_values * (1.0 + gate_values * (1.0 - sigmoid_values))
    ).astype(jnp.bfloat16)
    up_grad = (hidden_wide * silu_values).astype(jnp.bfloat16)
    gate_grad_local = jnp.einsum(
        "secd,secf->edf", rows_arrived, gate_grad, preferred_element_type=jnp.float32
    )
    up_grad_local = jnp.einsum(
        "secd,secf->edf", rows_arrived, up_grad, preferred_element_type=jnp.float32
    )
    input_parts = (
        jnp.einsum("secf,edf->secd", gate_grad, gate_weight, preferred_element_type=jnp.float32)
        + jnp.einsum("secf,edf->secd", up_grad, up_weight, preferred_element_type=jnp.float32)
    ).astype(jnp.bfloat16)
    returned_grads = lax.all_to_all(
        input_parts, ("dp", "blk", "sp"), split_axis=0, concat_axis=0, tiled=True
    )
    slot_input_grad = join_halves(returned_grads)
    expert_input_grad = slot_input_grad[slot_index].reshape(tok_rows, TOPK, model_width)
    feature_grad = jnp.dot(logit_grad, router_full.T, preferred_element_type=jnp.float32) + jnp.sum(
        expert_input_grad, axis=1
    )
    residual_part, feature_gain_grad = feature_pull(feature_grad)
    residual_grad = out_grad + residual_part
    attended_grad = residual_grad.astype(jnp.bfloat16)
    output_grad_full = jnp.dot(context_rows.T, attended_grad, preferred_element_type=jnp.float32)
    context_grad = jnp.dot(attended_grad, output_full.T, preferred_element_type=jnp.float32).astype(
        jnp.bfloat16
    )
    context_heads_grad = lax.all_to_all(
        context_grad.reshape(tok_rows, sp_size, head_width),
        "sp",
        split_axis=1,
        concat_axis=0,
        tiled=True,
    )
    context_heads_grad = context_heads_grad.reshape(blocks, block_rows, heads_here, HEAD_DIM)

    def backward_block(carry, block_input):
        key_total, value_total = carry
        block_queries, block_grads, block_logsum, block_start = block_input
        scores = masked_scores(block_queries, block_start)
        attn_weights = jnp.exp(scores - block_logsum[..., None])
        prob_dots = jnp.einsum(
            "qhd,khd->hqk", block_grads, values_all, preferred_element_type=jnp.float32
        )
        row_delta = jnp.sum(attn_weights * prob_dots, axis=-1, keepdims=True)
        score_grad = (attn_weights * (prob_dots - row_delta)).astype(jnp.bfloat16)
        query_grad = (
            jnp.einsum("hqk,khd->qhd", score_grad, keys_all, preferred_element_type=jnp.float32)
            * score_scale
        )
        key_total = (
            key_total
            + jnp.einsum(
                "hqk,qhd->khd", score_grad, block_queries, preferred_element_type=jnp.float32
            )
            * score_scale
        )
        value_total = value_total + jnp.einsum(
            "hqk,qhd->khd",
            attn_weights.astype(jnp.bfloat16),
            block_grads,
            preferred_element_type=jnp.float32,
        )
        return ((key_total, value_total), query_grad.astype(jnp.bfloat16))

    zero_keys = jnp.zeros((key_rows, heads_here, HEAD_DIM), jnp.float32)
    (key_total, value_total), query_grads = lax.scan(
        backward_block,
        (zero_keys, zero_keys),
        (query_blocks, context_heads_grad, logsum, block_starts),
    )
    key_mine, value_mine = (
        lax.psum_scatter(key_total, "blk", scatter_dimension=0, tiled=True),
        lax.psum_scatter(value_total, "blk", scatter_dimension=0, tiled=True),
    )
    query_back, key_back, value_back = (
        lax.all_to_all(
            query_grads.reshape(head_rows, 1, head_width),
            "sp",
            split_axis=0,
            concat_axis=1,
            tiled=True,
        ),
        lax.all_to_all(
            key_mine.astype(jnp.bfloat16).reshape(head_rows, 1, head_width),
            "sp",
            split_axis=0,
            concat_axis=1,
            tiled=True,
        ),
        lax.all_to_all(
            value_mine.astype(jnp.bfloat16).reshape(head_rows, 1, head_width),
            "sp",
            split_axis=0,
            concat_axis=1,
            tiled=True,
        ),
    )
    query_lin_grad, query_gain_grad = query_pull(
        query_back.reshape(tok_rows, model_width).astype(jnp.float32)
    )
    key_lin_grad, key_gain_grad = key_pull(
        key_back.reshape(tok_rows, model_width).astype(jnp.float32)
    )
    query_lin_low = query_lin_grad.astype(jnp.bfloat16)
    key_lin_low = key_lin_grad.astype(jnp.bfloat16)
    value_low = value_back.reshape(tok_rows, model_width)
    query_grad_full = jnp.dot(normed.T, query_lin_low, preferred_element_type=jnp.float32)
    key_grad_full = jnp.dot(normed.T, key_lin_low, preferred_element_type=jnp.float32)
    value_grad_full = jnp.dot(normed.T, value_low, preferred_element_type=jnp.float32)
    normed_grad = jnp.dot(query_lin_low, query_full.T, preferred_element_type=jnp.float32)
    normed_grad = normed_grad + jnp.dot(key_lin_low, key_full.T, preferred_element_type=jnp.float32)
    normed_grad = normed_grad + jnp.dot(value_low, value_full.T, preferred_element_type=jnp.float32)
    tokens_part, attention_gain_grad = attention_pull(normed_grad)
    input_gradient = residual_grad + tokens_part
    summed = (
        lax.psum_scatter(query_grad_full, ("dp", "blk", "sp"), scatter_dimension=0, tiled=True),
        lax.psum_scatter(key_grad_full, ("dp", "blk", "sp"), scatter_dimension=0, tiled=True),
        lax.psum_scatter(value_grad_full, ("dp", "blk", "sp"), scatter_dimension=0, tiled=True),
        lax.psum_scatter(output_grad_full, ("dp", "blk", "sp"), scatter_dimension=0, tiled=True),
        lax.psum_scatter(router_grad_full, ("dp", "blk", "sp"), scatter_dimension=0, tiled=True),
        lax.psum_scatter(attention_gain_grad, ("dp", "blk", "sp"), scatter_dimension=0, tiled=True),
        lax.psum_scatter(query_gain_grad, ("dp", "blk", "sp"), scatter_dimension=0, tiled=True),
        lax.psum_scatter(key_gain_grad, ("dp", "blk", "sp"), scatter_dimension=0, tiled=True),
        lax.psum_scatter(feature_gain_grad, ("dp", "blk", "sp"), scatter_dimension=0, tiled=True),
    )
    return (
        block_output,
        input_gradient,
        summed[0],
        summed[1],
        summed[2],
        summed[3],
        summed[4],
        summed[5],
        summed[6],
        summed[7],
        summed[8],
        gate_grad_local,
        up_grad_local,
        down_grad_local,
    )


def solution(mesh):
    in_specs = (
        P(("dp", "blk", "sp"), None),
        P(("dp", "blk", "sp"), None),
        P(("dp", "blk", "sp"), None),
        P(("dp", "blk", "sp"), None),
        P(("dp", "blk", "sp"), None),
        P(("dp", "blk", "sp"), None),
        P(("dp", "blk", "sp")),
        P(("dp", "blk", "sp")),
        P(("dp", "blk", "sp")),
        P(("dp", "blk", "sp")),
        P(("dp", "sp"), None, "blk"),
        P(("dp", "sp"), None, "blk"),
        P(("dp", "sp"), "blk", None),
        P(("dp", "blk", "sp"), None),
        P(("dp", "blk", "sp"), None),
    )
    out_specs = (
        P(("dp", "blk", "sp"), None),
        P(("dp", "blk", "sp"), None),
        P(("dp", "blk", "sp"), None),
        P(("dp", "blk", "sp"), None),
        P(("dp", "blk", "sp"), None),
        P(("dp", "blk", "sp"), None),
        P(("dp", "blk", "sp"), None),
        P(("dp", "blk", "sp")),
        P(("dp", "blk", "sp")),
        P(("dp", "blk", "sp")),
        P(("dp", "blk", "sp")),
        P(("dp", "sp"), None, "blk"),
        P(("dp", "sp"), None, "blk"),
        P(("dp", "sp"), "blk", None),
    )
    return jax.shard_map(body, mesh=mesh, in_specs=in_specs, out_specs=out_specs, check_vma=False)
```

profile of v0, /device:TPU:0, one launch (start us, length us, event | category | flops | bytes accessed | tf_op | source)
XLA Modules:
  0.0 3349.1 jit_solution(2714634614352808484)
XLA Ops:
  12.9 42.6 %all-reduce.13 = (bf16[2048]{0:T(1024)(128)(2,1)S(1)}, bf16[2048]{0:T(1024)(128)(2,1)S(1)}, bf16[2048]{0:T(1024)(128)(2,1)S(1)}, bf16[2048]{0:T(1024)(128)(2,1)S(1)}) all-reduce(bf16[2048]{0:T(1024)(128)(2,1)S(1)} %dynamic-update-slice, ...), channel_id=1, replica_groups=mesh['dp'=4,'blk'=2,'sp'=4] {'dp','blk','sp'}, use_global_device_ids=true, to_apply=%add.4 | all-reduce | flops 8192 | bytes 32768
  57.0 34.3 %all-gather.11.cloned.1.call-done = bf16[2048,2048]{1,0:T(8,128)(2,1)} async-done(((bf16[64,2048]{1,0:T(8,128)(2,1)}), bf16[2048,2048]{1,0:T(8,128)(2,1)}) %all-gather.11.cloned.1.call-update) | async-done | bytes 8388624 | tf_op jit(solution)/shard_map/all_gather | solution.py:98
  97.8 72.5 %all-gather.13.cloned.1.call-done = bf16[2048,2048]{1,0:T(8,128)(2,1)} async-done(((bf16[64,2048]{1,0:T(8,128)(2,1)}), bf16[2048,2048]{1,0:T(8,128)(2,1)}) %all-gather.13.cloned.1.call-update) | async-done | bytes 8388624 | tf_op jit(solution)/shard_map/all_gather | solution.py:99
  179.1 22.2 all_to_all.135
  202.4 51.8 %all-gather.7.cloned.1.call-done = bf16[2048,2048]{1,0:T(8,128)(2,1)} async-done(((bf16[64,2048]{1,0:T(8,128)(2,1)}), bf16[2048,2048]{1,0:T(8,128)(2,1)}) %all-gather.7.cloned.1.call-update) | async-done | bytes 8388624 | tf_op jit(solution)/shard_map/all_gather | solution.py:100
  258.9 18.3 all_to_all.136
  278.1 18.0 reduce-window.6
  302.4 16.6 all-to-all-done.1
  346.5 16.0 all-to-all-done.3
  402.2 341.2 %all_gather.43 = bf16[2048,64]{1,0:T(8,128)(2,1)S(1)} all-gather(bf16[64,64]{1,0:T(8,128)(2,1)S(1)} %copy-done.69), channel_id=1, replica_groups=mesh['dp'=4,'blk'=2,'sp'=4] {'dp','blk','sp'}, dimensions={0}, use_global_device_ids=true | all-gather | bytes 270336 | tf_op jit(solution)/shard_map/all_gather | solution.py:102
  803.2 243.5 %all-to-all-done.6 = bf16[32,4,24,2048]{3,2,1,0:T(8,128)(2,1)} async-done(((bf16[32,4,24,2048]{3,2,1,0:T(8,128)(2,1)}), bf16[32,4,24,2048]{3,2,1,0:T(8,128)(2,1)}, u32[]{:S(2)}, u32[]{:S(2)}) %all-to-all-start.6) | async-done | bytes 12582944 | tf_op jit(solution)/shard_map/all_to_all | solution.py:266
  1046.6 16.4 fusion.32
  1091.4 15.6 fusion.9
  1107.1 19.0 fusion
  1136.8 225.6 %all-to-all-done.5 = bf16[32,4,24,2048]{3,2,1,0:T(8,128)(2,1)} async-done(((bf16[32,4,24,2048]{3,2,1,0:T(8,128)(2,1)}), bf16[32,4,24,2048]{3,2,1,0:T(8,128)(2,1)}, u32[]{:S(2)}, u32[]{:S(2)}) %all-to-all-start.5) | async-done | bytes 12582944 | tf_op jit(solution)/shard_map/all_to_all | solution.py:236
  1406.0 238.8 %all-to-all-done.7 = bf16[32,4,24,2048]{3,2,1,0:T(8,128)(2,1)} async-done(((bf16[32,4,24,2048]{3,2,1,0:T(8,128)(2,1)}), bf16[32,4,24,2048]{3,2,1,0:T(8,128)(2,1)}, u32[]{:S(2)}, u32[]{:S(2)}) %all-to-all-start.7) | async-done | bytes 12582944 | tf_op jit(solution)/shard_map/all_to_all | solution.py:299
  1697.2 15.0 all-to-all-done.8
  1746.1 20.8 all_to_all.137
  1851.8 15.7 fusion.26
  1907.1 41.3 %all-reduce.12 = (f32[2048]{0:T(1024)S(1)}, f32[2048]{0:T(1024)S(1)}, f32[2048]{0:T(1024)S(1)}, f32[2048]{0:T(1024)S(1)}) all-reduce(f32[2048]{0:T(1024)S(1)} %get-tuple-element.79, f32[2048]{0:T(1024)S(1)} %copy-done.66, f32[2048]{0:T(1024)S(1)} %copy-done.65, ...), channel_id=9, replica_groups=mesh['dp'=4,'blk'=2,'sp'=4] {'dp','blk','sp'}, use_global_device_ids=true, to_apply=%region_34.35.clone | all-reduce | flops 8192 | bytes 65536
  1952.1 294.6 %reduce-scatter.18.cloned.1.call-done = f32[64,2048]{1,0:T(8,128)} async-done(((f32[2048,2048]{1,0:T(8,128)}), f32[64,2048]{1,0:T(8,128)}) %reduce-scatter.18.cloned.1.call-update) | async-done | bytes 524304 | tf_op jit(solution)/shard_map/reduce_scatter | solution.py:406
  2246.7 365.2 %reduce-scatter.16.cloned.1.call-done = f32[64,2048]{1,0:T(8,128)} async-done(((f32[2048,2048]{1,0:T(8,128)}), f32[64,2048]{1,0:T(8,128)}) %reduce-scatter.16.cloned.1.call-update) | async-done | bytes 524304 | tf_op jit(solution)/shard_map/reduce_scatter | solution.py:405
  2611.9 365.0 %reduce-scatter.14.cloned.1.call-done = f32[64,2048]{1,0:T(8,128)} async-done(((f32[2048,2048]{1,0:T(8,128)}), f32[64,2048]{1,0:T(8,128)}) %reduce-scatter.14.cloned.1.call-update) | async-done | bytes 524304 | tf_op jit(solution)/shard_map/reduce_scatter | solution.py:404
  2976.9 365.2 %reduce-scatter.12.cloned.1.call-done = f32[64,2048]{1,0:T(8,128)} async-done(((f32[2048,2048]{1,0:T(8,128)}), f32[64,2048]{1,0:T(8,128)}) %reduce-scatter.12.cloned.1.call-update) | async-done | bytes 524304 | tf_op jit(solution)/shard_map/reduce_scatter | solution.py:403
  (384 shorter events, 457.7 us)
Async XLA Ops:
  7.2 84.1 %all-gather.11.cloned.1.call-start = ((), (), s32[]{:S(2)}) async-start(), calls=%async_computation.21 | async-start | bytes 8650752 | tf_op jit(solution)/shard_map/all_gather | solution.py:98
  7.9 162.3 %all-gather.13.cloned.1.call-start = ((), (), s32[]{:S(2)}) async-start(), calls=%async_computation.22 | async-start | bytes 8650752 | tf_op jit(solution)/shard_map/all_gather | solution.py:99
  8.7 245.5 %all-gather.7.cloned.1.call-start = ((), (), s32[]{:S(2)}) async-start(), calls=%async_computation.19 | async-start | bytes 8650752 | tf_op jit(solution)/shard_map/all_gather | solution.py:100
  9.4 310.3 %all-gather.15.cloned.1.call-start = ((), (), s32[]{:S(2)}) async-start(), calls=%async_computation.23 | async-start | bytes 1572864 | tf_op jit(solution)/shard_map/all_gather | solution.py:156
  202.3 119.0 %all-gather.9.cloned.1.call-start = ((), (), s32[]{:S(2)}) async-start(), calls=%async_computation.20 | async-start | bytes 1572864 | tf_op jit(solution)/shard_map/all_gather | solution.py:157
  277.2 99.0 %all-gather.17.cloned.1.call-start = ((), (), s32[]{:S(2)}) async-start(), calls=%async_computation.24 | async-start | bytes 8650752 | tf_op jit(solution)/shard_map/all_gather | solution.py:101
  297.4 21.6 all-to-all-start.1
  333.8 28.8 all-to-all-start.3
  382.2 361.2 %copy-start = (bf16[128,2048]{1,0:T(8,128)(2,1)}, bf16[128,2048]{1,0:T(8,128)(2,1)S(1)}, u32[]{:S(2)}) copy-start(bf16[128,2048]{1,0:T(8,128)(2,1)S(1)} %multiply_convert_fusion.1) | copy-start | bytes 1572868
  397.9 365.1 %all-to-all-start.4 = ((bf16[32,4,24,2048]{3,2,1,0:T(8,128)(2,1)}), bf16[32,4,24,2048]{3,2,1,0:T(8,128)(2,1)}, u32[]{:S(2)}, u32[]{:S(2)}) async-start(bf16[32,4,24,2048]{3,2,1,0:T(8,128)(2,1)} %bitcast.229), calls=%async_computation.4 | async-start | bytes 25165824 | tf_op jit(solution)/shard_map/all_to_all | solution.py:225
  402.2 350.1 %copy-start.19 = (f32[128,2048]{1,0:T(8,128)}, f32[128,2048]{1,0:T(8,128)S(1)}, u32[]{:S(2)}) copy-start(f32[128,2048]{1,0:T(8,128)S(1)} %convert_element_type.194) | copy-start | bytes 3145732
  771.5 275.2 %all-to-all-start.6 = ((bf16[32,4,24,2048]{3,2,1,0:T(8,128)(2,1)}), bf16[32,4,24,2048]{3,2,1,0:T(8,128)(2,1)}, u32[]{:S(2)}, u32[]{:S(2)}) async-start(bf16[32,4,24,2048]{3,2,1,0:T(8,128)(2,1)} %bitcast.230), calls=%async_computation.6 | async-start | bytes 25165824 | tf_op jit(solution)/shard_map/all_to_all | solution.py:266
  1080.1 282.3 %all-to-all-start.5 = ((bf16[32,4,24,2048]{3,2,1,0:T(8,128)(2,1)}), bf16[32,4,24,2048]{3,2,1,0:T(8,128)(2,1)}, u32[]{:S(2)}, u32[]{:S(2)}) async-start(bf16[32,4,24,2048]{3,2,1,0:T(8,128)(2,1)} %copy.281), calls=%async_computation.5 | async-start | bytes 25165824 | tf_op jit(solution)/shard_map/all_to_all | solution.py:236
  1362.3 282.4 %all-to-all-start.7 = ((bf16[32,4,24,2048]{3,2,1,0:T(8,128)(2,1)}), bf16[32,4,24,2048]{3,2,1,0:T(8,128)(2,1)}, u32[]{:S(2)}, u32[]{:S(2)}) async-start(bf16[32,4,24,2048]{3,2,1,0:T(8,128)(2,1)} %copy.287), calls=%async_computation.7 | async-start | bytes 25165824 | tf_op jit(solution)/shard_map/all_to_all | solution.py:299
  1686.9 25.2 all-to-all-start.8
  1696.7 46.4 %reduce-scatter.10.cloned.1.call-start = ((), (), s32[]{:S(2)}) async-start(), calls=%async_computation.26 | async-start | bytes 3145728 | tf_op jit(solution)/shard_map/reduce_scatter | solution.py:360
  1718.9 68.1 %reduce-scatter.8.cloned.1.call-start = ((), (), s32[]{:S(2)}) async-start(), calls=%async_computation.25 | async-start | bytes 3145728 | tf_op jit(solution)/shard_map/reduce_scatter | solution.py:359
  1732.6 219.5 %reduce-scatter.20.cloned.1.call-start = ((), (), s32[]{:S(2)}) async-start(), calls=%async_computation.31 | async-start | bytes 1081344 | tf_op jit(solution)/shard_map/reduce_scatter | solution.py:407
  1734.0 512.7 %reduce-scatter.18.cloned.1.call-start = ((), (), s32[]{:S(2)}) async-start(), calls=%async_computation.30 | async-start | bytes 17301504 | tf_op jit(solution)/shard_map/reduce_scatter | solution.py:406
  1743.1 868.8 %reduce-scatter.16.cloned.1.call-start = ((), (), s32[]{:S(2)}) async-start(), calls=%async_computation.29 | async-start | bytes 17301504 | tf_op jit(solution)/shard_map/reduce_scatter | solution.py:405
  1783.5 19.5 all-to-all-start.9
  1803.0 19.4 all-to-all-start.10
  1806.5 1170.4 %reduce-scatter.14.cloned.1.call-start = ((), (), s32[]{:S(2)}) async-start(), calls=%async_computation.28 | async-start | bytes 17301504 | tf_op jit(solution)/shard_map/reduce_scatter | solution.py:404
  1839.9 1502.3 %reduce-scatter.12.cloned.1.call-start = ((), (), s32[]{:S(2)}) async-start(), calls=%async_computation.27 | async-start | bytes 17301504 | tf_op jit(solution)/shard_map/reduce_scatter | solution.py:403
  (86 other events, 2100.2 us)
Sparse Core Ops, SparseCore 0:
  10.9 80.3 all-gather.10
  94.2 75.9 all-gather.12
  173.2 80.9 all-gather.6
  256.2 7.6 all-gather.14
  277.4 7.1 all-gather.8
  287.4 88.8 all-gather.16
  1719.1 7.9 reduce-scatter.9
  1732.7 8.3 reduce-scatter.7
  1744.0 138.4 reduce-scatter.19
  1885.3 361.4 reduce-scatter.17
  2249.7 362.1 reduce-scatter.15
  2614.7 362.1 reduce-scatter.13
  2979.9 362.1 reduce-scatter.11
where the time goes:
time: 3360 us; the launch traced here: 3350 us
  waiting for transfers between devices  2350 us (70%)
  blocking collectives  486 us (14%)
  matrix products  230 us (7%)
  local copies, waits for them, and re-layouts  119 us (4%)
  other arithmetic  96.1 us (3%)
  starting transfers between devices  55.9 us (2%)
    reduce_scatter x1, waiting for transfers between devices, body(): lax.psum_scatter(value_grad_full, ('dp', 'blk', 'sp'), scatter_dimension=...  365 us
    reduce_scatter x1, waiting for transfers between devices, body(): lax.psum_scatter(query_grad_full, ('dp', 'blk', 'sp'), scatter_dimension=...  365 us
    reduce_scatter x1, waiting for transfers between devices, body(): lax.psum_scatter(key_grad_full, ('dp', 'blk', 'sp'), scatter_dimension=0,...  365 us
    all_gather x1, blocking collectives, body(): lax.all_gather(router_weight, ('dp', 'blk', 'sp'), axis=0, tiled=True)  341 us
    reduce_scatter x1, waiting for transfers between devices, body(): lax.psum_scatter(output_grad_full, ('dp', 'blk', 'sp'), scatter_dimension...  295 us
    all_to_all x1, waiting for transfers between devices, body(): lax.all_to_all(gradient_send, ('dp', 'blk', 'sp'), split_axis=0, concat_a...  243 us
    all_to_all x1, waiting for transfers between devices, body(): lax.all_to_all(input_parts, ('dp', 'blk', 'sp'), split_axis=0, concat_axi...  239 us
    all_to_all x1, waiting for transfers between devices, body(): lax.all_to_all(part_out, ('dp', 'blk', 'sp'), split_axis=0, concat_axis=0...  226 us
  transfers between devices with their start and end apart: 22, of which 16 were waited for; matrix products, arithmetic and copies ran while one was open for 10% of the time, Pallas kernels for 0%

commit v1 on v0

--- a/solution.py
+++ b/solution.py
@@ -1,9 +1,14 @@
+import functools
 import math
 
 import jax
 import jax.numpy as jnp
 from jax import lax
+from jax.experimental import pallas as pl
+from jax.experimental.pallas import tpu as pltpu
 from jax.sharding import PartitionSpec as P
+
+DP, BLK, SP = AXES = ("dp", "blk", "sp")
 
 HEADS = 16
 HEAD_DIM = 128
@@ -55,6 +60,1677 @@
         jnp.int32
     )
     return (flat_experts, jnp.sum(jnp.cumsum(onehot, axis=0) * onehot, axis=1) - 1)
+
+
+MESH_ID = pl.DeviceIdType.MESH
+VMEM_BYTES = 56 * 1024 * 1024
+
+
+class Place:
+    def __init__(self):
+        self.dp = lax.axis_index(DP)
+        self.blk = lax.axis_index(BLK)
+        self.z = lax.axis_index(SP)
+        self.x = self.dp % 2
+        self.y = self.dp // 2
+        self.col = self.blk * 4 + self.z
+
+    def column(self, k):
+        if k == 0:
+            return self.dp
+        if k == 1:
+            return self.dp + 1 - 2 * self.x
+        if k == 2:
+            return self.dp + 2 - 4 * self.y
+        return 3 - self.dp
+
+    def at(self, k=0, blk=None, z=None):
+        return (self.column(k), self.blk if blk is None else blk, self.z if z is None else z)
+
+
+def entry_barrier(place, reach):
+    barrier = pltpu.get_barrier_semaphore()
+
+    def tell(target):
+        pl.semaphore_signal(barrier, inc=1, device_id=target, device_id_type=MESH_ID)
+
+    if reach == "all":
+        me = (place.dp * 2 + place.blk) * 4 + place.z
+
+        @pl.loop(1, 32)
+        def _(step):
+            other = (me + step) % 32
+            tell((other // 8, (other // 4) % 2, other % 4))
+
+        pl.semaphore_wait(barrier, 31)
+    elif reach == "column":
+
+        @pl.loop(1, 8)
+        def _(step):
+            other = (place.col + step) % 8
+            tell((place.dp, other // 4, other % 4))
+
+        pl.semaphore_wait(barrier, 7)
+    else:
+        planes = reach == "planes"
+        tell(place.at(0, 1 - place.blk))
+        if planes:
+            tell(place.at(1))
+            tell(place.at(2))
+
+        @pl.when(place.z > 0)
+        def _():
+            tell(place.at(z=place.z - 1))
+
+        @pl.when(place.z < 3)
+        def _():
+            tell(place.at(z=place.z + 1))
+
+        ends = (3 - place.z) // 3 + place.z // 3
+        pl.semaphore_wait(barrier, 3 + (2 if planes else 0) - ends)
+
+
+def remote(src, dst, send_sem, recv_sem, target):
+    return pltpu.make_async_remote_copy(
+        src_ref=src,
+        dst_ref=dst,
+        send_sem=send_sem,
+        recv_sem=recv_sem,
+        device_id=target,
+        device_id_type=MESH_ID,
+    )
+
+
+class GatherFlow:
+    SENDS = 40
+    RECVS = 37
+
+    def __init__(self, place, src, out, send, recv, full, direct=False):
+        self.p, self.src, self.out, self.send, self.recv, self.full = place, src, out, send, recv, full
+        self.direct = direct
+        self.half = src.shape[0] // 2
+
+    def slot(self, k, blk, s):
+        if self.full:
+            return (self.p.column(k) * 2 + blk) * 4 + s
+        return blk * 4 + s
+
+    def block(self, k, s, blk=None):
+        return self.out.at[self.slot(k, self.p.blk if blk is None else blk, s)]
+
+    def copies(self, k, s, own=False):
+        src = self.src if own else self.block(k, s)
+        return src, self.block(k, s)
+
+    def up(self, s, own=False):
+        src, dst = self.copies(0, s, own)
+        return remote(src, dst, self.send.at[s], self.recv.at[s], self.p.at(z=jnp.minimum(self.p.z + 1, 3)))
+
+    def down(self, s, own=False):
+        src, dst = self.copies(0, s, own)
+        return remote(src, dst, self.send.at[4 + s], self.recv.at[s], self.p.at(z=jnp.maximum(self.p.z - 1, 0)))
+
+    def across_x(self, s, own=False):
+        src, dst = self.copies(0, s, own)
+        return remote(src, dst, self.send.at[8 + s], self.recv.at[4 + s], self.p.at(1))
+
+    def across_y(self, s, own=False):
+        src, dst = self.copies(0, s, own)
+        return remote(src, dst, self.send.at[12 + s], self.recv.at[8 + s], self.p.at(2))
+
+    def turn_y(self, s):
+        ref = self.block(1, s).at[pl.ds(0, self.half)]
+        return remote(ref, ref, self.send.at[16 + s], self.recv.at[12 + s], self.p.at(2))
+
+    def turn_x(self, s):
+        ref = self.block(2, s).at[pl.ds(self.half, self.half)]
+        return remote(ref, ref, self.send.at[20 + s], self.recv.at[16 + s], self.p.at(1))
+
+    def core(self, k, s, own=False):
+        src, dst = self.copies(k, s, own)
+        return remote(
+            src, dst, self.send.at[24 + 4 * k + s], self.recv.at[20 + 4 * k + s], self.p.at(0, 1 - self.p.blk)
+        )
+
+    def got(self, sem, ref):
+        remote(ref, ref, self.send.at[0], self.recv.at[sem], self.p.at(0, 1 - self.p.blk)).wait_recv()
+
+    def own_copy(self):
+        return pltpu.make_async_copy(self.src, self.block(0, self.p.z), self.recv.at[36])
+
+    def spread(self, s, own=False):
+        if self.full:
+            self.across_x(s, own).start()
+            self.across_y(s, own).start()
+        self.core(0, s, own).start()
+
+    def straight(self, step):
+        z = self.p.z
+        return remote(
+            self.src, self.block(0, z), self.send.at[step - 1], self.recv.at[z], self.p.at(z=(z + step) % 4)
+        )
+
+    def begin(self):
+        z = self.p.z
+        if self.direct:
+            for step in (1, 2, 3):
+                self.straight(step).start()
+            self.spread(z, True)
+            self.own_copy().start()
+            return
+
+        @pl.when(z < 3)
+        def _():
+            self.up(z, True).start()
+
+        @pl.when(z > 0)
+        def _():
+            self.down(z, True).start()
+
+        self.spread(z, True)
+        self.own_copy().start()
+
+    def along(self, d):
+        z = self.p.z
+
+        @pl.when(z >= d)
+        def _():
+            s = z - d
+            self.got(s, self.block(0, s))
+
+            if not self.direct:
+
+                @pl.when(z < 3)
+                def _():
+                    self.up(s).start()
+
+            self.spread(s)
+
+        @pl.when(z + d <= 3)
+        def _():
+            s = z + d
+            self.got(s, self.block(0, s))
+
+            if not self.direct:
+
+                @pl.when(z > 0)
+                def _():
+                    self.down(s).start()
+
+            self.spread(s)
+
+    def each(self, d, act):
+        z = self.p.z
+        if d == 0:
+            act(z)
+            return
+
+        @pl.when(z >= d)
+        def _():
+            act(z - d)
+
+        @pl.when(z + d <= 3)
+        def _():
+            act(z + d)
+
+    def turn(self, d):
+        if not self.full:
+            return
+
+        def act(s):
+            self.got(4 + s, self.block(1, s))
+            self.turn_y(s).start()
+            self.core(1, s).start()
+            self.got(8 + s, self.block(2, s))
+            self.turn_x(s).start()
+            self.core(2, s).start()
+
+        self.each(d, act)
+
+    def corner(self, d):
+        if not self.full:
+            return
+
+        def act(s):
+            self.got(12 + s, self.block(3, s).at[pl.ds(0, self.half)])
+            self.got(16 + s, self.block(3, s).at[pl.ds(self.half, self.half)])
+            self.core(3, s).start()
+
+        self.each(d, act)
+
+    def settle_plane(self, s):
+        for k in range(4 if self.full else 1):
+            self.got(20 + 4 * k + s, self.block(k, s, 1 - self.p.blk))
+            self.core(k, s).wait_send()
+        if self.full:
+            self.across_x(s).wait_send()
+            self.across_y(s).wait_send()
+            self.turn_x(s).wait_send()
+            self.turn_y(s).wait_send()
+
+    def finish(self):
+        z = self.p.z
+
+        @pl.loop(0, 4)
+        def _(s):
+            self.settle_plane(s)
+            if not self.direct:
+
+                @pl.when((s <= z) & (z < 3))
+                def _():
+                    self.up(s).wait_send()
+
+                @pl.when((s >= z) & (z > 0))
+                def _():
+                    self.down(s).wait_send()
+
+        if self.direct:
+            for step in (1, 2, 3):
+                self.straight(step).wait_send()
+        self.own_copy().wait()
+
+    def steps(self):
+        return [
+            self.begin,
+            lambda: self.along(1),
+            lambda: self.turn(0),
+            lambda: self.along(2),
+            lambda: self.turn(1),
+            lambda: self.along(3),
+            lambda: self.corner(0),
+            lambda: self.turn(2),
+            lambda: self.corner(1),
+            lambda: self.turn(3),
+            lambda: self.corner(2),
+            lambda: self.corner(3),
+            self.finish,
+        ]
+
+
+class PlaneFlow(GatherFlow):
+    def __init__(self, place, blocks, out, send, recv, local):
+        super().__init__(place, blocks[0][1], out, send, recv, True)
+        self.blocks, self.local = blocks, local
+
+    def begin(self):
+        for i, (s, src) in enumerate(self.blocks):
+            self.src = src
+            self.spread(s, True)
+            pltpu.make_async_copy(src, self.block(0, s), self.local.at[i]).start()
+
+    def turns(self):
+        for s, _ in self.blocks:
+            self.got(4 + s, self.block(1, s))
+            self.turn_y(s).start()
+            self.core(1, s).start()
+            self.got(8 + s, self.block(2, s))
+            self.turn_x(s).start()
+            self.core(2, s).start()
+
+    def corners(self):
+        for s, _ in self.blocks:
+            self.got(12 + s, self.block(3, s).at[pl.ds(0, self.half)])
+            self.got(16 + s, self.block(3, s).at[pl.ds(self.half, self.half)])
+            self.core(3, s).start()
+
+    def finish(self):
+        for i, (s, src) in enumerate(self.blocks):
+            self.settle_plane(s)
+            pltpu.make_async_copy(src, self.block(0, s), self.local.at[i]).wait()
+
+
+def run_flows(flows):
+    lists = [flow.steps() for flow in flows]
+    for position in range(max(len(steps) for steps in lists)):
+        for steps in lists:
+            if position < len(steps):
+                steps[position]()
+
+
+def gather_call(arrays, fulls, name, collective_id):
+    count = len(arrays)
+
+    def kernel(*refs):
+        srcs, outs = refs[:count], refs[count : 2 * count]
+        sems = refs[2 * count :]
+        place = Place()
+        entry_barrier(place, "planes" if any(fulls) else "line")
+        run_flows(
+            [
+                GatherFlow(place, srcs[i], outs[i], sems[2 * i], sems[2 * i + 1], fulls[i])
+                for i in range(count)
+            ]
+        )
+
+    scratch = []
+    for _ in arrays:
+        scratch += [pltpu.SemaphoreType.DMA((GatherFlow.SENDS,)), pltpu.SemaphoreType.DMA((GatherFlow.RECVS,))]
+    return pl.pallas_call(
+        kernel,
+        out_shape=[
+            jax.ShapeDtypeStruct((32 if full else 8,) + a.shape, a.dtype) for a, full in zip(arrays, fulls)
+        ],
+        in_specs=[pl.BlockSpec(memory_space=pl.ANY)] * count,
+        out_specs=[pl.BlockSpec(memory_space=pl.ANY)] * count,
+        scratch_shapes=scratch,
+        compiler_params=pltpu.CompilerParams(collective_id=collective_id, has_side_effects=True),
+        name=name,
+    )(*arrays)
+
+
+def add_rows(dst, terms, rows):
+    @pl.loop(0, rows // 16)
+    def _(i):
+        at = pl.ds(pl.multiple_of(i * 16, 16), 16)
+        total = terms[0][at, :].astype(jnp.float32)
+        for term in terms[1:]:
+            total = total + term[at, :].astype(jnp.float32)
+        dst[at, :] = total.astype(dst.dtype)
+
+
+class ScatterFlow:
+    SENDS = 16 + 8 + 8 + 4 + 4
+    RECVS = 16 + 8 + 8 + 4 + 4
+    LOCALS = 20
+
+    def __init__(self, place, part, out, scratch, full, plane_only=False):
+        self.p, self.part, self.out, self.full, self.plane_only = place, part, out, full, plane_only
+        if full:
+            (self.acc, self.near, self.half_in, self.side_in, self.line_in, self.sum, self.send, self.recv, self.local) = scratch
+        else:
+            (self.acc, self.near, self.line_in, self.sum, self.send, self.recv, self.local) = scratch
+        self.columns = 4 if full else 1
+        self.rows = part.shape[1]
+        self.half = self.rows // 2
+
+    @staticmethod
+    def scratch(rows, width, dtype, full):
+        columns = 4 if full else 1
+        shapes = [
+            pltpu.VMEM((columns, 4, rows, width), dtype),
+            pltpu.VMEM((columns, 4, rows, width), dtype),
+        ]
+        if full:
+            shapes += [pltpu.VMEM((2, 4, rows // 2, width), dtype), pltpu.VMEM((2, 4, rows, width), dtype)]
+        return shapes + [
+            pltpu.VMEM((2, 4, rows, width), dtype),
+            pltpu.VMEM((rows, width), jnp.float32),
+            pltpu.SemaphoreType.DMA((ScatterFlow.SENDS,)),
+            pltpu.SemaphoreType.DMA((ScatterFlow.RECVS,)),
+            pltpu.SemaphoreType.DMA((ScatterFlow.LOCALS,)),
+        ]
+
+    def slot(self, k, blk, s):
+        if self.full:
+            return (self.p.column(k) * 2 + blk) * 4 + s
+        return blk * 4 + s
+
+    def order(self, i):
+        z = self.p.z
+        return [3 * (1 - z // 2), (2 + 3 * z) % 5, 1 + z % 2, z][i]
+
+    def load(self, k, s):
+        return pltpu.make_async_copy(
+            self.part.at[self.slot(k, self.p.blk, s)], self.acc.at[k, s], self.local.at[4 * k + s]
+        )
+
+    def core(self, k, s):
+        return remote(
+            self.part.at[self.slot(k, 1 - self.p.blk, s)],
+            self.near.at[k, s],
+            self.send.at[4 * k + s],
+            self.recv.at[4 * k + s],
+            self.p.at(0, 1 - self.p.blk),
+        )
+
+    def half_x(self, s):
+        return remote(
+            self.acc.at[3, s, pl.ds(0, self.half)],
+            self.half_in.at[0, s],
+            self.send.at[16 + s],
+            self.recv.at[16 + s],
+            self.p.at(1),
+        )
+
+    def half_y(self, s):
+        return remote(
+            self.acc.at[3, s, pl.ds(self.half, self.half)],
+            self.half_in.at[1, s],
+            self.send.at[20 + s],
+            self.recv.at[20 + s],
+            self.p.at(2),
+        )
+
+    def side_x(self, s):
+        return remote(
+            self.acc.at[1, s], self.side_in.at[0, s], self.send.at[24 + s], self.recv.at[24 + s], self.p.at(1)
+        )
+
+    def side_y(self, s):
+        return remote(
+            self.acc.at[2, s], self.side_in.at[1, s], self.send.at[28 + s], self.recv.at[28 + s], self.p.at(2)
+        )
+
+    def line_up(self, s):
+        return remote(
+            self.acc.at[0, s],
+            self.line_in.at[0, s],
+            self.send.at[32 + s],
+            self.recv.at[32 + s],
+            self.p.at(z=jnp.minimum(self.p.z + 1, 3)),
+        )
+
+    def line_down(self, s):
+        return remote(
+            self.acc.at[0, s],
+            self.line_in.at[1, s],
+            self.send.at[36 + s],
+            self.recv.at[36 + s],
+            self.p.at(z=jnp.maximum(self.p.z - 1, 0)),
+        )
+
+    def begin(self):
+        for i in range(4):
+            s = self.order(i)
+            for k in reversed(range(self.columns)):
+                self.core(k, s).start()
+                self.load(k, s).start()
+
+    def arrive(self, k, s):
+        self.load(k, s).wait()
+        self.core(k, s).wait_recv()
+        return [self.acc.at[k, s], self.near.at[k, s]]
+
+    def stage1(self, i):
+        if not self.full:
+            return
+        s = self.order(i)
+        add_rows(self.acc.at[3, s], self.arrive(3, s), self.rows)
+        self.half_x(s).start()
+        self.half_y(s).start()
+
+    def stage2(self, i):
+        if not self.full:
+            return
+        s = self.order(i)
+        first, second = pl.ds(0, self.half), pl.ds(self.half, self.half)
+        terms = self.arrive(2, s)
+        late = [term.at[first] for term in terms] + [self.half_in.at[0, s]]
+        rest = [term.at[second] for term in terms]
+        add_rows(rest[0], rest, self.half)
+        self.half_x(s).wait_recv()
+        add_rows(late[0], late, self.half)
+        self.side_y(s).start()
+        terms = self.arrive(1, s)
+        late = [term.at[second] for term in terms] + [self.half_in.at[1, s]]
+        rest = [term.at[first] for term in terms]
+        add_rows(rest[0], rest, self.half)
+        self.half_y(s).wait_recv()
+        add_rows(late[0], late, self.half)
+        self.side_x(s).start()
+
+    def stage3(self, i):
+        s = self.order(i)
+        z = self.p.z
+        terms = self.arrive(0, s)
+        if self.full:
+            self.side_x(s).wait_recv()
+            self.side_y(s).wait_recv()
+            terms = terms + [self.side_in.at[0, s], self.side_in.at[1, s]]
+        add_rows(self.acc.at[0, s], terms, self.rows)
+        if self.plane_only:
+            self.keep_plane(i).start()
+        elif i < 3:
+
+            @pl.when(z == 0)
+            def _():
+                self.line_up(s).start()
+
+            @pl.when(z == 3)
+            def _():
+                self.line_down(s).start()
+
+    def chain(self, i):
+        s = self.order(i)
+        z = self.p.z
+
+        @pl.when((z > 0) & (z < s) & (z < 3))
+        def _():
+            self.line_up(s).wait_recv()
+            add_rows(self.acc.at[0, s], [self.acc.at[0, s], self.line_in.at[0, s]], self.rows)
+            self.line_up(s).start()
+
+        @pl.when((z < 3) & (z > s) & (z > 0))
+        def _():
+            self.line_down(s).wait_recv()
+            add_rows(self.acc.at[0, s], [self.acc.at[0, s], self.line_in.at[1, s]], self.rows)
+            self.line_down(s).start()
+
+    def final(self):
+        z = self.p.z
+        mine, above, below = self.acc.at[0, z], self.line_in.at[0, z], self.line_in.at[1, z]
+
+        @pl.when(z > 0)
+        def _():
+            self.line_up(z).wait_recv()
+
+        @pl.when(z < 3)
+        def _():
+            self.line_down(z).wait_recv()
+
+        @pl.when(z == 0)
+        def _():
+            add_rows(self.sum, [mine, below], self.rows)
+
+        @pl.when(z == 3)
+        def _():
+            add_rows(self.sum, [mine, above], self.rows)
+
+        @pl.when((z > 0) & (z < 3))
+        def _():
+            add_rows(self.sum, [mine, above, below], self.rows)
+
+        done = pltpu.make_async_copy(self.sum, self.out, self.local.at[0])
+        done.start()
+
+        @pl.loop(0, 4)
+        def _(s):
+            for k in range(self.columns):
+                self.core(k, s).wait_send()
+            if self.full:
+                self.half_x(s).wait_send()
+                self.half_y(s).wait_send()
+                self.side_x(s).wait_send()
+                self.side_y(s).wait_send()
+
+            @pl.when(s > z)
+            def _():
+                self.line_up(s).wait_send()
+
+            @pl.when(s < z)
+            def _():
+                self.line_down(s).wait_send()
+
+        done.wait()
+
+    def keep_plane(self, i):
+        s = self.order(i)
+        return pltpu.make_async_copy(self.acc.at[0, s], self.out.at[s], self.local.at[16 + i])
+
+    def settle_plane(self):
+        for i in range(4):
+            s = self.order(i)
+            self.keep_plane(i).wait()
+            for k in range(4):
+                self.core(k, s).wait_send()
+            self.half_x(s).wait_send()
+            self.half_y(s).wait_send()
+            self.side_x(s).wait_send()
+            self.side_y(s).wait_send()
+
+    def steps(self):
+        plan = [
+            (self.stage1, 0),
+            (self.stage1, 1),
+            (self.stage2, 0),
+            (self.stage1, 2),
+            (self.stage2, 1),
+            (self.stage3, 0),
+            (self.stage1, 3),
+            (self.stage2, 2),
+            (self.stage3, 1),
+            (self.chain, 0),
+            (self.stage2, 3),
+            (self.stage3, 2),
+            (self.chain, 1),
+            (self.chain, 2),
+            (self.stage3, 3),
+        ]
+        return [self.begin] + [functools.partial(act, i) for act, i in plan] + [self.final]
+
+
+def local_params():
+    return pltpu.CompilerParams(vmem_limit_bytes=VMEM_BYTES)
+
+
+def inner(left, right, left_dim=1, right_dim=0):
+    return lax.dot_general(
+        left, right, (((left_dim,), (right_dim,)), ((), ())), preferred_element_type=jnp.float32
+    )
+
+
+def pick_rows(picks, features, grads, experts):
+    pairs, picked, pair_rows = picks.shape
+    width = features.shape[-1]
+    per = picked // experts
+
+    def kernel(pick_ref, feature_ref, grad_ref, row_ref, grad_row_ref):
+        for src, dst in ((feature_ref, row_ref), (grad_ref, grad_row_ref)):
+            rows = inner(pick_ref[0], src[0]).astype(dst.dtype)
+            for e in range(experts):
+                dst[e] = rows[e * per : (e + 1) * per]
+
+    shape = jax.ShapeDtypeStruct((experts, pairs * per, width), features.dtype)
+    source = pl.BlockSpec((1, pair_rows, width), lambda p: (p, 0, 0))
+    target = pl.BlockSpec((experts, per, width), lambda p: (0, p, 0))
+    return pl.pallas_call(
+        kernel,
+        out_shape=[shape, shape],
+        grid=(pairs,),
+        in_specs=[pl.BlockSpec((1, picked, pair_rows), lambda p: (p, 0, 0)), source, source],
+        out_specs=[target, target],
+        compiler_params=local_params(),
+        name="pick_rows",
+    )(picks, features, grads)
+
+
+def put_rows_back(places, out_rows, input_rows):
+    pairs, pair_rows, picked = places.shape
+    experts, _, width = out_rows.shape
+    per = picked // experts
+
+    def kernel(place_ref, out_ref, input_ref, out_sum, input_sum):
+        for src, dst in ((out_ref, out_sum), (input_ref, input_sum)):
+            rows = jnp.concatenate([src[e] for e in range(experts)], axis=0)
+            dst[0] = inner(place_ref[0], rows).astype(dst.dtype)
+
+    shape = jax.ShapeDtypeStruct((pairs, pair_rows, width), out_rows.dtype)
+    source = pl.BlockSpec((experts, per, width), lambda p: (0, p, 0))
+    target = pl.BlockSpec((1, pair_rows, width), lambda p: (p, 0, 0))
+    return pl.pallas_call(
+        kernel,
+        out_shape=[shape, shape],
+        grid=(pairs,),
+        in_specs=[pl.BlockSpec((1, pair_rows, picked), lambda p: (p, 0, 0)), source, source],
+        out_specs=[target, target],
+        compiler_params=local_params(),
+        name="put_rows_back",
+    )(places, out_rows, input_rows)
+
+
+def run_experts(rows, grads, probs, gate_weight, up_weight, down_weight):
+    experts, slots, width = rows.shape
+    hidden = gate_weight.shape[2]
+    parts = 2
+    part = slots // parts
+
+    def kernel(x, c, p, wg, wu, wd, weighted, gate_back, up_back, out, back, prob_back):
+        gate = inner(x[0], wg[0])
+        up = inner(x[0], wu[0])
+        plain = inner(c[0], wd[0], 1, 1)
+        prob = p[0]
+        sig = jax.nn.sigmoid(gate)
+        act = gate * sig
+        hid = act * up
+        prob_back[0] = jnp.sum(hid * plain, axis=1, keepdims=True)
+        low = (hid * prob).astype(jnp.bfloat16)
+        weighted[0] = low
+        grad = plain * prob
+        gate_low = (grad * up * sig * (1.0 + gate * (1.0 - sig))).astype(jnp.bfloat16)
+        up_low = (grad * act).astype(jnp.bfloat16)
+        gate_back[0] = gate_low
+        up_back[0] = up_low
+        out[0] = inner(low, wd[0]).astype(jnp.bfloat16)
+        back[0] = (inner(gate_low, wg[0], 1, 1) + inner(up_low, wu[0], 1, 1)).astype(jnp.bfloat16)
+
+    def block(size):
+        return pl.BlockSpec((1, part, size), lambda e, i: (e, i, 0))
+
+    def whole(shape):
+        return pl.BlockSpec((1,) + shape[1:], lambda e, i: (e, 0, 0))
+
+    narrow = jax.ShapeDtypeStruct((experts, slots, hidden), rows.dtype)
+    wide = jax.ShapeDtypeStruct(rows.shape, rows.dtype)
+    column = jax.ShapeDtypeStruct((experts, slots, 1), jnp.float32)
+    return pl.pallas_call(
+        kernel,
+        out_shape=[narrow, narrow, narrow, wide, wide, column],
+        grid=(experts, parts),
+        in_specs=[
+            block(width),
+            block(width),
+            block(1),
+            whole(gate_weight.shape),
+            whole(up_weight.shape),
+            whole(down_weight.shape),
+        ],
+        out_specs=[block(hidden)] * 3 + [block(width)] * 2 + [block(1)],
+        compiler_params=local_params(),
+        name="run_experts",
+    )(rows, grads, probs, gate_weight, up_weight, down_weight)
+
+
+class ColumnsFlow:
+    SENDS = 24 + 1 + 8
+    RECVS = 8 + 1 + 8
+    LOCALS = 4
+
+    def __init__(self, place, sources, rows_in, wide, tall, send, recv, local):
+        self.p, self.sources, self.rows_in, self.wide, self.tall = place, sources, rows_in, wide, tall
+        self.send, self.recv, self.local = send, recv, local
+        self.rows = rows_in.shape[0]
+        self.share = wide.shape[1] // len(sources)
+
+    def wide_rows(self, col):
+        return pl.ds(pl.multiple_of((self.p.dp * 8 + col) * self.rows, self.rows), self.rows)
+
+    def piece(self, i, to, start):
+        share = self.share
+        src = self.sources[i].at[:, pl.ds(pl.multiple_of(to * share, share), share)]
+        dst = self.wide.at[self.wide_rows(self.p.col), pl.ds(i * share, share)]
+        return src, dst
+
+    def scatter(self, step, i):
+        to = (self.p.col + step) % 8
+        src, dst = self.piece(i, to, step)
+        return remote(
+            src, dst, self.send.at[3 * step + i], self.recv.at[self.p.col], (self.p.dp, to // 4, to % 4)
+        )
+
+    def keep(self, i):
+        src, dst = self.piece(i, self.p.col, 0)
+        return pltpu.make_async_copy(src, dst, self.local.at[i])
+
+    def tall_rows(self, k):
+        return self.tall.at[pl.ds(pl.multiple_of(self.p.column(k) * self.rows, self.rows), self.rows)]
+
+    def swap(self):
+        group = self.p.dp * 2 + self.p.blk
+        dst = self.tall.at[pl.ds(pl.multiple_of(self.p.z * self.rows, self.rows), self.rows)]
+        return remote(
+            self.rows_in, dst, self.send.at[24], self.recv.at[8], (self.p.z, group // 4, group % 4)
+        )
+
+    def stay(self):
+        return pltpu.make_async_copy(self.rows_in, self.tall_rows(0), self.local.at[3])
+
+    def at_home(self):
+        group = self.p.dp * 2 + self.p.blk
+        return (self.p.z == self.p.dp) & (group == self.p.col)
+
+    def band(self, which, k):
+        if which == 0:
+            height = 8 * self.rows
+            return self.wide.at[pl.ds(pl.multiple_of(self.p.column(k) * height, height), height)]
+        return self.tall_rows(k)
+
+    def across(self, which, k):
+        ref = self.band(which, 0)
+        slot = 4 * which + k - 1
+        return remote(ref, ref, self.send.at[25 + slot], self.recv.at[9 + slot], self.p.at(k))
+
+    def part(self, which, k, first):
+        ref = self.band(which, k)
+        half = ref.shape[0] // 2
+        return ref.at[pl.ds(0 if first else half, half)]
+
+    def turn(self, which, k):
+        ref = self.part(which, k, k == 1)
+        slot = 4 * which + 1 + k
+        return remote(ref, ref, self.send.at[25 + slot], self.recv.at[9 + slot], self.p.at(3 - k))
+
+    def got(self, sem, ref):
+        remote(ref, ref, self.send.at[0], self.recv.at[sem], self.p.at(0, 1 - self.p.blk)).wait_recv()
+
+    def begin(self):
+        home = self.at_home()
+
+        @pl.when(home)
+        def _():
+            self.stay().start()
+
+        @pl.when(jnp.logical_not(home))
+        def _():
+            self.swap().start()
+
+        @pl.loop(1, 8)
+        def _(step):
+            for i in range(3):
+                self.scatter(step, i).start()
+
+        for i in range(3):
+            self.keep(i).start()
+
+    def settle(self):
+        home = self.at_home()
+
+        @pl.when(home)
+        def _():
+            self.stay().wait()
+
+        @pl.when(jnp.logical_not(home))
+        def _():
+            self.got(8, self.tall_rows(0))
+
+        self.across(1, 1).start()
+        self.across(1, 2).start()
+        for i in range(3):
+            self.keep(i).wait()
+
+        @pl.loop(1, 8)
+        def _(step):
+            col = (self.p.col + step) % 8
+            self.got(col, self.wide.at[self.wide_rows(col)])
+
+        self.across(0, 1).start()
+        self.across(0, 2).start()
+
+    def turns(self):
+        for which in (1, 0):
+            for k in (1, 2):
+                self.got(9 + 4 * which + k - 1, self.band(which, k))
+                self.turn(which, k).start()
+
+    def finish(self):
+        for which in (1, 0):
+            for k in (1, 2):
+                self.got(9 + 4 * which + 1 + k, self.part(which, 3, k == 1))
+                self.turn(which, k).wait_send()
+                self.across(which, k).wait_send()
+
+        @pl.when(jnp.logical_not(self.at_home()))
+        def _():
+            self.swap().wait_send()
+
+        @pl.loop(1, 8)
+        def _(step):
+            for i in range(3):
+                self.scatter(step, i).wait_send()
+
+
+class SumsFlow:
+    SENDS = 8 + 8 + 1
+    RECVS = 8 + 8 + 1
+    LOCALS = 10
+
+    def __init__(self, place, wide, tall, wide_out, tall_out, scratch):
+        self.p = place
+        self.parts = (wide, tall)
+        self.outs = (wide_out, tall_out)
+        self.acc, self.half_in, self.side_in = scratch[0:2], scratch[2:4], scratch[4:6]
+        self.send, self.recv, self.local = scratch[6:9]
+        self.rows = tall_out.shape[0]
+
+    @staticmethod
+    def scratch(wide, tall):
+        shapes = []
+        for kind in ((4, 1), (2, 2), (2, 1)):
+            for part in (wide, tall):
+                shapes.append(pltpu.VMEM((kind[0], part.shape[1] // kind[1], part.shape[2]), part.dtype))
+        return shapes + [
+            pltpu.SemaphoreType.DMA((SumsFlow.SENDS,)),
+            pltpu.SemaphoreType.DMA((SumsFlow.RECVS,)),
+            pltpu.SemaphoreType.DMA((SumsFlow.LOCALS,)),
+        ]
+
+    def load(self, which, k):
+        return pltpu.make_async_copy(
+            self.parts[which].at[self.p.column(k)], self.acc[which].at[k], self.local.at[4 * which + k]
+        )
+
+    def halves(self, ref):
+        half = ref.shape[0] // 2
+        return ref.at[pl.ds(0, half)], ref.at[pl.ds(half, half)]
+
+    def corner(self, which, k):
+        src = self.halves(self.acc[which].at[3])[k - 1]
+        slot = 4 * which + k - 1
+        return remote(src, self.half_in[which].at[k - 1], self.send.at[slot], self.recv.at[slot], self.p.at(k))
+
+    def side(self, which, k):
+        slot = 4 * which + 1 + k
+        return remote(
+            self.acc[which].at[k], self.side_in[which].at[k - 1], self.send.at[slot], self.recv.at[slot], self.p.at(k)
+        )
+
+    def deal(self, step):
+        to = (self.p.col + step) % 8
+        src = self.acc[0].at[0, pl.ds(pl.multiple_of(to * self.rows, self.rows), self.rows)]
+        return remote(
+            src, self.outs[0].at[self.p.col], self.send.at[8 + step], self.recv.at[8 + self.p.col], (self.p.dp, to // 4, to % 4)
+        )
+
+    def keep(self):
+        src = self.acc[0].at[0, pl.ds(pl.multiple_of(self.p.col * self.rows, self.rows), self.rows)]
+        return pltpu.make_async_copy(src, self.outs[0].at[self.p.col], self.local.at[8])
+
+    def swap(self):
+        return remote(
+            self.acc[1].at[0], self.outs[1], self.send.at[16], self.recv.at[16], (self.p.col // 2, self.p.col % 2, self.p.dp)
+        )
+
+    def stay(self):
+        return pltpu.make_async_copy(self.acc[1].at[0], self.outs[1], self.local.at[9])
+
+    def at_home(self):
+        return (self.p.col // 2 == self.p.dp) & (self.p.col % 2 == self.p.blk) & (self.p.z == self.p.dp)
+
+    def begin(self):
+        for which in (1, 0):
+            for k in (3, 2, 1, 0):
+                self.load(which, k).start()
+        for which in (1, 0):
+            self.load(which, 3).wait()
+            self.corner(which, 1).start()
+            self.corner(which, 2).start()
+
+    def sides(self):
+        for which in (1, 0):
+            for k, other in ((2, 1), (1, 2)):
+                self.load(which, k).wait()
+                self.corner(which, other).wait_recv()
+                target = self.halves(self.acc[which].at[k])[other - 1]
+                add_rows(target, [target, self.half_in[which].at[other - 1]], target.shape[0])
+                self.side(which, k).start()
+
+    def total(self):
+        for which in (1, 0):
+            self.load(which, 0).wait()
+            self.side(which, 1).wait_recv()
+            self.side(which, 2).wait_recv()
+            mine = self.acc[which].at[0]
+            add_rows(mine, [mine, self.side_in[which].at[0], self.side_in[which].at[1]], mine.shape[0])
+            if which == 1:
+                home = self.at_home()
+
+                @pl.when(home)
+                def _():
+                    self.stay().start()
+
+                @pl.when(jnp.logical_not(home))
+                def _():
+                    self.swap().start()
+
+        @pl.loop(1, 8)
+        def _(step):
+            self.deal(step).start()
+
+        self.keep().start()
+
+    def finish(self):
+        home = self.at_home()
+
+        @pl.when(home)
+        def _():
+            self.stay().wait()
+
+        @pl.when(jnp.logical_not(home))
+        def _():
+            self.swap().wait()
+
+        self.keep().wait()
+
+        @pl.loop(1, 8)
+        def _(step):
+            col = (self.p.col + step) % 8
+            landed = self.outs[0].at[col]
+            remote(
+                landed, landed, self.send.at[0], self.recv.at[8 + col], self.p.at(0, 1 - self.p.blk)
+            ).wait_recv()
+            self.deal(step).wait_send()
+
+        for which in (1, 0):
+            for k in (1, 2):
+                self.corner(which, k).wait_send()
+                self.side(which, k).wait_send()
+
+    def steps(self):
+        idle = lambda: None
+        return [self.begin, self.sides, idle, idle, self.total, idle, idle, idle, idle, idle, idle, idle, idle, idle, idle, idle, self.finish]
+
+
+class DealFlow:
+    def __init__(self, place, src, out, send, recv, local):
+        self.p, self.src, self.out, self.send, self.recv, self.local = place, src, out, send, recv, local
+        self.me = (place.dp * 2 + place.blk) * 4 + place.z
+
+    def copy(self, step):
+        to = (self.me + step) % 32
+        return remote(
+            self.src.at[to], self.out.at[self.me], self.send.at[step], self.recv.at[self.me], (to // 8, (to // 4) % 2, to % 4)
+        )
+
+    def keep(self):
+        return pltpu.make_async_copy(self.src.at[self.me], self.out.at[self.me], self.local.at[0])
+
+    def begin(self):
+        self.keep().start()
+
+        @pl.loop(1, 32)
+        def _(step):
+            self.copy(step).start()
+
+    def finish(self):
+        self.keep().wait()
+
+        @pl.loop(1, 32)
+        def _(step):
+            landed = self.out.at[(self.me + step) % 32]
+            remote(
+                landed,
+                landed,
+                self.send.at[0],
+                self.recv.at[(self.me + step) % 32],
+                self.p.at(0, 1 - self.p.blk),
+            ).wait_recv()
+            self.copy(step).wait_send()
+
+    @staticmethod
+    def scratch():
+        return [pltpu.SemaphoreType.DMA((32,)), pltpu.SemaphoreType.DMA((32,)), pltpu.SemaphoreType.DMA((1,))]
+
+    def steps(self, length=18):
+        return [self.begin] + [lambda: None] * (length - 2) + [self.finish]
+
+
+def hbm_call(kernel, shapes, scratch, name, collective_id, args, aliases=None):
+    return pl.pallas_call(
+        kernel,
+        out_shape=shapes,
+        in_specs=[pl.BlockSpec(memory_space=pl.ANY)] * len(args),
+        out_specs=[pl.BlockSpec(memory_space=pl.ANY)] * len(shapes),
+        scratch_shapes=scratch,
+        input_output_aliases=aliases or {},
+        compiler_params=pltpu.CompilerParams(
+            collective_id=collective_id, has_side_effects=True, vmem_limit_bytes=VMEM_BYTES
+        ),
+        name=name,
+    )(*args)
+
+
+def gather_sems():
+    return [pltpu.SemaphoreType.DMA((GatherFlow.SENDS,)), pltpu.SemaphoreType.DMA((GatherFlow.RECVS,))]
+
+
+def plane_sems(count):
+    return gather_sems() + [pltpu.SemaphoreType.DMA((count,))]
+
+
+def opening_call(tokens, small, cotangent, query_weight, key_weight, value_weight, output_weight):
+    width = tokens.shape[1]
+    rows = query_weight.shape[0]
+
+    def kernel(tok, sml, cot, wq, wk, wv, wo, tok_out, sml_out, cot_out, wide, tall, *sems):
+        place = Place()
+        entry_barrier(place, "all")
+        weights = ColumnsFlow(place, (wq, wk, wv), wo, wide, tall, *sems[7:10])
+        line = GatherFlow(place, tok, tok_out, sems[0], sems[1], False)
+        params = GatherFlow(place, sml, sml_out, sems[2], sems[3], True, True)
+        plane = PlaneFlow(place, [(place.z, cot)], cot_out, *sems[4:7])
+        params.begin()
+        weights.begin()
+        for d in range(1, 4):
+            params.along(d)
+        plane.begin()
+        for d in range(4):
+            params.turn(d)
+        plane.turns()
+        weights.settle()
+        line.begin()
+        for d in range(4):
+            params.corner(d)
+        plane.corners()
+        line.along(1)
+        params.finish()
+        line.along(2)
+        weights.turns()
+        line.along(3)
+        plane.finish()
+        line.finish()
+        weights.finish()
+
+    shapes = [
+        jax.ShapeDtypeStruct((8,) + tokens.shape, tokens.dtype),
+        jax.ShapeDtypeStruct((32,) + small.shape, small.dtype),
+        jax.ShapeDtypeStruct((32,) + cotangent.shape, cotangent.dtype),
+        jax.ShapeDtypeStruct((32 * rows, 3 * width // 8), tokens.dtype),
+        jax.ShapeDtypeStruct((4 * rows, width), tokens.dtype),
+    ]
+    scratch = gather_sems() * 2 + plane_sems(1)
+    scratch += [
+        pltpu.SemaphoreType.DMA((ColumnsFlow.SENDS,)),
+        pltpu.SemaphoreType.DMA((ColumnsFlow.RECVS,)),
+        pltpu.SemaphoreType.DMA((ColumnsFlow.LOCALS,)),
+    ]
+    return hbm_call(
+        kernel,
+        shapes,
+        scratch,
+        "opening",
+        1,
+        (tokens, small, cotangent, query_weight, key_weight, value_weight, output_weight),
+    )
+
+
+def attended_call(part, others, gathered):
+    line = ScatterFlow.scratch(part.shape[1], part.shape[2], part.dtype, False)
+
+    def kernel(part_ref, first, second, third, _, out, gathered_out, *scratch):
+        place = Place()
+        entry_barrier(place, "planes")
+        flow = ScatterFlow(place, part_ref, out, scratch[: len(line)], False)
+        blocks = [((place.z + 4 - j) % 4, src) for j, src in ((1, first), (2, second), (3, third))]
+        plane = PlaneFlow(place, blocks, gathered_out, *scratch[len(line) :])
+        flow.begin()
+        plane.begin()
+        flow.stage3(0)
+        flow.stage3(1)
+        flow.chain(0)
+        plane.turns()
+        flow.stage3(2)
+        flow.chain(1)
+        flow.chain(2)
+        flow.stage3(3)
+        flow.final()
+        plane.corners()
+        plane.finish()
+
+    shapes = [
+        jax.ShapeDtypeStruct(part.shape[1:], jnp.float32),
+        jax.ShapeDtypeStruct(gathered.shape, gathered.dtype),
+    ]
+    return hbm_call(
+        kernel, shapes, line + plane_sems(3), "attended", 5, (part,) + tuple(others) + (gathered,), {4: 1}
+    )
+
+
+def closing_call(normed_part, wide, tall):
+    line = ScatterFlow.scratch(normed_part.shape[1], normed_part.shape[2], normed_part.dtype, False)
+    sums = SumsFlow.scratch(wide, tall)
+    rows = tall.shape[1]
+
+    def kernel(part, wide_in, tall_in, out, wide_out, tall_out, *scratch):
+        place = Place()
+        entry_barrier(place, "all")
+        weights = SumsFlow(place, wide_in, tall_in, wide_out, tall_out, scratch[len(line) :])
+        flow = ScatterFlow(place, part, out, scratch[: len(line)], False)
+        weights.begin()
+        flow.begin()
+        flow.stage3(0)
+        flow.stage3(1)
+        weights.sides()
+        flow.chain(0)
+        flow.stage3(2)
+        flow.chain(1)
+        flow.chain(2)
+        flow.stage3(3)
+        weights.total()
+        flow.final()
+        weights.finish()
+
+    shapes = [
+        jax.ShapeDtypeStruct(normed_part.shape[1:], jnp.float32),
+        jax.ShapeDtypeStruct((8, rows, wide.shape[2]), wide.dtype),
+        jax.ShapeDtypeStruct((rows, tall.shape[2]), tall.dtype),
+    ]
+    return hbm_call(kernel, shapes, line + sums, "closing", 2, (normed_part, wide, tall))
+
+
+def residual_grad_call(grad, logit_grad, out_part):
+    sums = ScatterFlow.scratch(out_part.shape[1], out_part.shape[2], out_part.dtype, True)
+
+    def kernel(grad_ref, logit_ref, part_ref, grad_out, logit_out, out, *scratch):
+        place = Place()
+        entry_barrier(place, "planes")
+        line = GatherFlow(place, grad_ref, grad_out, scratch[0], scratch[1], False)
+        logits = GatherFlow(place, logit_ref, logit_out, scratch[2], scratch[3], True)
+        flow = ScatterFlow(place, part_ref, out, scratch[4:], True, True)
+        line.begin()
+        logits.begin()
+        flow.begin()
+        flow.stage1(0)
+        flow.stage1(1)
+        line.along(1)
+        logits.along(1)
+        logits.turn(0)
+        flow.stage2(0)
+        flow.stage1(2)
+        line.along(2)
+        logits.along(2)
+        logits.turn(1)
+        flow.stage1(3)
+        flow.stage2(1)
+        flow.stage3(0)
+        line.along(3)
+        logits.along(3)
+        logits.turn(2)
+        logits.turn(3)
+        flow.stage2(2)
+        flow.stage3(1)
+        for d in range(4):
+            logits.corner(d)
+        flow.stage2(3)
+        flow.stage3(2)
+        line.finish()
+        logits.finish()
+        flow.stage3(3)
+        flow.settle_plane()
+
+    shapes = [
+        jax.ShapeDtypeStruct((8,) + grad.shape, grad.dtype),
+        jax.ShapeDtypeStruct((32,) + logit_grad.shape, logit_grad.dtype),
+        jax.ShapeDtypeStruct((4,) + out_part.shape[1:], out_part.dtype),
+    ]
+    return hbm_call(kernel, shapes, gather_sems() * 2 + sums, "residual_grad", 7, (grad, logit_grad, out_part))
+
+
+class WeightGrads:
+    PARTS = 4
+
+    @staticmethod
+    def scratch(rows, hidden):
+        slots, part = rows.shape[1], rows.shape[2] // WeightGrads.PARTS
+        return [
+            pltpu.VMEM((2, 2, slots, part), rows.dtype),
+            pltpu.VMEM((2, 3, slots, hidden), rows.dtype),
+            pltpu.VMEM((2, 2, part, hidden), jnp.float32),
+            pltpu.VMEM((2, hidden, part), jnp.float32),
+            pltpu.SemaphoreType.DMA((2, 5)),
+            pltpu.SemaphoreType.DMA((2, 3)),
+        ]
+
+    def __init__(self, ins, outs, scratch):
+        self.ins, self.outs = ins, outs
+        self.wide, self.narrow, self.tall, self.flat, self.in_sems, self.out_sems = scratch
+        self.part = self.wide.shape[3]
+        self.units = ins[0].shape[0] * self.PARTS
+
+    def columns(self, unit):
+        return pl.ds(pl.multiple_of((unit % self.PARTS) * self.part, self.part), self.part)
+
+    def loads(self, unit, slot):
+        e = unit // self.PARTS
+        copies = []
+        for i in range(2):
+            copies.append((self.ins[i].at[e, :, self.columns(unit)], self.wide.at[slot, i]))
+        for i in range(3):
+            copies.append((self.ins[2 + i].at[e], self.narrow.at[slot, i]))
+        return [pltpu.make_async_copy(s, d, self.in_sems.at[slot, n]) for n, (s, d) in enumerate(copies)]
+
+    def stores(self, unit, slot):
+        e, columns = unit // self.PARTS, self.columns(unit)
+        copies = [
+            (self.tall.at[slot, 0], self.outs[0].at[e, columns]),
+            (self.tall.at[slot, 1], self.outs[1].at[e, columns]),
+            (self.flat.at[slot], self.outs[2].at[e, :, columns]),
+        ]
+        return [pltpu.make_async_copy(s, d, self.out_sems.at[slot, n]) for n, (s, d) in enumerate(copies)]
+
+    def begin(self):
+        for copy in self.loads(0, 0):
+            copy.start()
+
+    def run(self, unit):
+        slot = unit % 2
+
+        @pl.when(unit + 1 < self.units)
+        def _():
+            for copy in self.loads(unit + 1, 1 - slot):
+                copy.start()
+
+        for copy in self.loads(unit, slot):
+            copy.wait()
+
+        @pl.when(unit >= 2)
+        def _():
+            for copy in self.stores(unit - 2, slot):
+                copy.wait()
+
+        rows, grads = self.wide[slot, 0], self.wide[slot, 1]
+        self.tall[slot, 0] = inner(rows, self.narrow[slot, 1], 0, 0)
+        self.tall[slot, 1] = inner(rows, self.narrow[slot, 2], 0, 0)
+        self.flat[slot] = inner(self.narrow[slot, 0], grads, 0, 0)
+        for copy in self.stores(unit, slot):
+            copy.start()
+
+    def finish(self):
+        for unit in (self.units - 2, self.units - 1):
+            for copy in self.stores(unit, unit % 2):
+                copy.wait()
+
+
+def experts_back_call(part, dealt, rows, grads, weighted, gate_back, up_back):
+    sums = ScatterFlow.scratch(part.shape[1], part.shape[2], part.dtype, True)
+    experts, _, width = rows.shape
+    hidden = weighted.shape[2]
+
+    def kernel(part_ref, dealt_ref, *refs):
+        ins, (out, dealt_out), outs, scratch = refs[:5], refs[5:7], refs[7:10], refs[10:]
+        place = Place()
+        entry_barrier(place, "all")
+        deal = DealFlow(place, dealt_ref, dealt_out, *scratch[:3])
+        flow = ScatterFlow(place, part_ref, out, scratch[3 : 3 + len(sums)], True)
+        grads_here = WeightGrads(ins, outs, scratch[3 + len(sums) :])
+        deal.begin()
+        steps = flow.steps()
+        steps[0]()
+        grads_here.begin()
+
+        @pl.loop(0, grads_here.units)
+        def _(unit):
+            for i, step in enumerate(steps[1:-1]):
+                pl.when(unit == i)(step)
+            grads_here.run(unit)
+
+        steps[-1]()
+        grads_here.finish()
+        deal.finish()
+
+    shapes = [
+        jax.ShapeDtypeStruct(part.shape[1:], jnp.float32),
+        jax.ShapeDtypeStruct(dealt.shape, dealt.dtype),
+        jax.ShapeDtypeStruct((experts, width, hidden), jnp.float32),
+        jax.ShapeDtypeStruct((experts, width, hidden), jnp.float32),
+        jax.ShapeDtypeStruct((experts, hidden, width), jnp.float32),
+    ]
+    scratch = DealFlow.scratch() + sums + WeightGrads.scratch(rows, hidden)
+    return hbm_call(
+        kernel, shapes, scratch, "experts_back", 3, (part, dealt, rows, grads, weighted, gate_back, up_back)
+    )
+
+
+def column_sum(values, name, collective_id):
+    def kernel(src, out, landed, send, recv):
+        place = Place()
+        entry_barrier(place, "column")
+
+        def copy(step):
+            to = (place.col + step) % 8
+            return remote(
+                src, landed.at[place.col], send.at[step], recv.at[place.col], (place.dp, to // 4, to % 4)
+            )
+
+        @pl.loop(1, 8)
+        def _(step):
+            copy(step).start()
+
+        landed[place.col] = src[...]
+
+        @pl.loop(1, 8)
+        def _(step):
+            col = (place.col + step) % 8
+            remote(src, landed.at[col], send.at[0], recv.at[col], place.at(0, 1 - place.blk)).wait_recv()
+            copy(step).wait_send()
+
+        total = landed[0]
+        for col in range(1, 8):
+            total = total + landed[col]
+        out[...] = total
+
+    return pl.pallas_call(
+        kernel,
+        out_shape=jax.ShapeDtypeStruct(values.shape, values.dtype),
+        in_specs=[pl.BlockSpec(memory_space=pltpu.VMEM)],
+        out_specs=pl.BlockSpec(memory_space=pltpu.VMEM),
+        scratch_shapes=[
+            pltpu.VMEM((8,) + values.shape, values.dtype),
+            pltpu.SemaphoreType.DMA((8,)),
+            pltpu.SemaphoreType.DMA((8,)),
+        ],
+        compiler_params=pltpu.CompilerParams(collective_id=collective_id, has_side_effects=True),
+        name=name,
+    )(values)
+
+
+def deal_sum(values, collective_id):
+    def kernel(src, out, landed, send, recv, local):
+        place = Place()
+        entry_barrier(place, "all")
+        flow = DealFlow(place, src, landed, send, recv, local)
+        flow.begin()
+        flow.finish()
+        total = landed[0]
+        for index in range(1, 32):
+            total = total + landed[index]
+        out[...] = total
+
+    return pl.pallas_call(
+        kernel,
+        out_shape=jax.ShapeDtypeStruct(values.shape[1:], values.dtype),
+        in_specs=[pl.BlockSpec(memory_space=pltpu.VMEM)],
+        out_specs=pl.BlockSpec(memory_space=pltpu.VMEM),
+        scratch_shapes=[pltpu.VMEM(values.shape, values.dtype)] + DealFlow.scratch(),
+        compiler_params=pltpu.CompilerParams(collective_id=collective_id, has_side_effects=True),
+        name="gain_gradients",
+    )(values)
+
+
+def product(left, right, sums, batches=((), ()), out=jnp.float32):
+    return lax.dot_general(left, right, (sums, batches), preferred_element_type=out)
+
+
+def shift_line(rows, step):
+    size = lax.axis_size(SP)
+    return lax.ppermute(rows, SP, [(i, (i + step) % size) for i in range(size)])
+
+
+HEAD_BATCH = ((1,), (1,))
+BATCH = ((0,), (0,))
+
+
+def rotate_heads(values, cosine, sine):
+    rows, width = values.shape
+    heads = values.reshape(rows, width // HEAD_DIM, HEAD_DIM)
+    return rotate(heads, cosine, sine).reshape(rows, width)
+
+
+def body_fast(
+    tokens,
+    query_weight,
+    key_weight,
+    value_weight,
+    output_weight,
+    router_weight,
+    attention_gain,
+    query_gain,
+    key_gain,
+    feature_gain,
+    gate_weight,
+    up_weight,
+    down_weight,
+    routes,
+    cotangent,
+):
+    tok_rows, model_width = tokens.shape
+    column_size = 8
+    devices = 32
+    share = model_width // column_size
+    heads_here = share // HEAD_DIM
+    seq_rows = tok_rows * column_size
+    experts_here = gate_weight.shape[0]
+    own_rows = query_weight.shape[0]
+    score_scale = 1.0 / math.sqrt(HEAD_DIM)
+    column = lax.axis_index(BLK) * 4 + lax.axis_index(SP)
+    f32, bf16 = jnp.float32, jnp.bfloat16
+
+    gains = jnp.stack([attention_gain, query_gain, key_gain, feature_gain], axis=1)
+    named_here = routes.astype(bf16).reshape(own_rows, tok_rows * TOPK // own_rows)
+    filled = EXPERTS + 4 + named_here.shape[1]
+    small = jnp.concatenate(
+        [router_weight, gains, named_here, jnp.zeros((own_rows, 128 - filled), bf16)], axis=1
+    )
+    tokens_all, small_all, cotangent_all, wide_weight, tall_weight = opening_call(
+        tokens, small, cotangent, query_weight, key_weight, value_weight, output_weight
+    )
+    routes_all = small_all[:, :, EXPERTS + 4 : filled].astype(jnp.int32).reshape(devices, tok_rows, TOPK)
+    small_all = small_all.reshape(model_width, 128)
+    router_full = small_all[:, :EXPERTS]
+    gain_all = small_all[:, EXPERTS : EXPERTS + 4].astype(f32)
+    gain_attention, gain_feature = gain_all[:, 0], gain_all[:, 3]
+    gain_share = lax.dynamic_slice_in_dim(gain_all, column * share, share, axis=0)
+    gain_query, gain_key = gain_share[:, 1], gain_share[:, 2]
+
+    sequence = tokens_all.reshape(seq_rows, model_width).astype(f32)
+    normed_all = norm_apply(sequence, gain_attention).astype(bf16)
+    linear = jnp.dot(normed_all, wide_weight, preferred_element_type=f32)
+    query_lin, key_lin = linear[:, :share], linear[:, share : 2 * share]
+    values = linear[:, 2 * share :].astype(bf16)
+    squares = jnp.stack([jnp.sum(query_lin * query_lin, axis=1), jnp.sum(key_lin * key_lin, axis=1)])
+    squares = column_sum(squares.reshape(16, seq_rows // 8), "square_sums", 4).reshape(2, seq_rows)
+    own_cotangent, squares = lax.optimization_barrier((cotangent, squares))
+    cotangent_others = [shift_line(own_cotangent, j) for j in (1, 2, 3)]
+    scales = lax.rsqrt(squares / model_width + NORM_EPSILON)
+    query_r, key_r = scales[0][:, None], scales[1][:, None]
+    cosine, sine = rope_tables(jnp.arange(seq_rows, dtype=jnp.int32), HEAD_DIM)
+    query_u, key_u = query_lin * query_r, key_lin * key_r
+    queries = rotate_heads(query_u * gain_query, cosine, sine).astype(bf16)
+    keys = rotate_heads(key_u * gain_key, cosine, sine).astype(bf16)
+
+    def split(rows):
+        return rows.reshape(seq_rows, heads_here, HEAD_DIM)
+
+    scores = product(split(queries), split(keys), ((2,), (2,)), HEAD_BATCH)
+    places = jnp.arange(seq_rows, dtype=jnp.int32)
+    causal = places[None, :] <= places[:, None]
+    scores = jnp.where(causal[None], scores * score_scale, MASKED)
+    attn_weights = jax.nn.softmax(scores, axis=-1)
+    attn_low = attn_weights.astype(bf16)
+    context = product(attn_low, split(values), ((2,), (0,)), ((0,), (1,))).transpose(1, 0, 2)
+    context = context.astype(bf16).reshape(seq_rows, share)
+    attended_part = jnp.dot(context, tall_weight, preferred_element_type=f32).astype(bf16)
+    attended, cotangent_all = attended_call(
+        attended_part.reshape(column_size, tok_rows, model_width), cotangent_others, cotangent_all
+    )
+
+    tokens_f = tokens.astype(f32)
+    residual = tokens_f + attended
+    features_f, feature_pull = jax.vjp(norm_apply, residual, gain_feature)
+    features = features_f.astype(bf16)
+    logits = jnp.dot(features, router_full, preferred_element_type=f32)
+    router_probs = jax.nn.softmax(logits, axis=-1)
+    features_all, probs_all = gather_call(
+        [features, router_probs.reshape(tok_rows // 2, 2 * EXPERTS)], [True, True], "features_gather", 6
+    )
+
+    first_expert = (lax.axis_index(DP) * 4 + lax.axis_index(SP)) * experts_here
+    expert_ids = first_expert + jnp.arange(experts_here, dtype=jnp.int32)
+    named = jnp.any(routes_all[:, None] == expert_ids[None, :, None, None], axis=3)
+    named_low = named.astype(bf16)
+    earlier = (jnp.arange(tok_rows)[:, None] < jnp.arange(tok_rows)[None, :]).astype(bf16)
+    rank = product(named_low, earlier, ((2,), (0,))).astype(jnp.int32)
+    slot = jnp.arange(CAP, dtype=jnp.int32)
+    hot = (named[:, :, None, :] & (rank[:, :, None, :] == slot[None, None, :, None])).astype(bf16)
+    pairs = devices // 2
+    hot = hot.reshape(pairs, 2, experts_here, CAP, tok_rows)
+    zero = jnp.zeros_like(hot[:, 0])
+    picks = jnp.concatenate(
+        [jnp.concatenate([hot[:, 0], zero], axis=3), jnp.concatenate([zero, hot[:, 1]], axis=3)], axis=2
+    )
+    pair_rows = 2 * tok_rows
+    slots = devices * CAP
+    pick_matrix = picks.reshape(pairs, experts_here * 2 * CAP, pair_rows)
+    features_all = features_all.reshape(pairs, pair_rows, model_width)
+    cotangent_all = cotangent_all.reshape(pairs, pair_rows, model_width)
+    expert_rows, grad_rows = pick_rows(pick_matrix, features_all, cotangent_all, experts_here)
+    probs_all = probs_all.reshape(pairs, pair_rows, EXPERTS)
+    probs_here = lax.dynamic_slice_in_dim(probs_all, first_expert, experts_here, axis=2)
+    slot_probs = jnp.sum(picks.astype(f32) * probs_here.transpose(0, 2, 1)[:, :, None, :], axis=3)
+    slot_probs = slot_probs.transpose(1, 0, 2).reshape(experts_here, slots)[:, :, None]
+    weighted_hidden, gate_grad, up_grad, out_rows, input_rows, slot_grad = run_experts(
+        expert_rows, grad_rows, slot_probs, gate_weight, up_weight, down_weight
+    )
+    token_grad = jnp.sum(
+        picks.astype(f32) * slot_grad.reshape(experts_here, pairs, 2 * CAP).transpose(1, 0, 2)[:, :, :, None],
+        axis=2,
+    )
+    token_grad = token_grad.reshape(pairs, experts_here, 2, tok_rows).transpose(0, 2, 1, 3)
+    token_grad = token_grad.reshape(devices, experts_here, tok_rows)
+    token_grad = jnp.pad(token_grad, ((0, 0), (0, 8 - experts_here), (0, 0)))
+    out_part, input_part = put_rows_back(pick_matrix.transpose(0, 2, 1), out_rows, input_rows)
+    out_part = out_part.reshape(devices, tok_rows, model_width)
+    input_part = input_part.reshape(devices, tok_rows, model_width)
+    input_grad, prob_parts, gate_grad_local, up_grad_local, down_grad_local = experts_back_call(
+        input_part, token_grad, expert_rows, grad_rows, weighted_hidden, gate_grad, up_grad
+    )
+
+    prob_parts = prob_parts.reshape(4, 2, 4, 8, tok_rows)[:, :, :, :experts_here]
+    prob_grad = jnp.sum(prob_parts, axis=1).reshape(EXPERTS, tok_rows).T
+    logit_grad = (
+        router_probs * (prob_grad - jnp.sum(prob_grad * router_probs, axis=-1, keepdims=True))
+    ).astype(bf16)
+    feature_grad = jnp.dot(logit_grad, router_full.T, preferred_element_type=f32) + input_grad
+    residual_part, feature_gain_grad = feature_pull(feature_grad)
+    residual_grad = cotangent.astype(f32) + residual_part
+    attended_grad = residual_grad.astype(bf16)
+    grads_all, logit_all, out_sums = residual_grad_call(
+        attended_grad, logit_grad.reshape(tok_rows // 2, 2 * EXPERTS), out_part
+    )
+    mixture = jnp.zeros((tok_rows, model_width), f32)
+    for j in range(4):
+        there = (lax.axis_index(SP) + j) % 4
+        block = lax.dynamic_index_in_dim(out_sums, there, axis=0, keepdims=False)
+        mixture = mixture + (block if j == 0 else shift_line(block, j)).astype(f32)
+    block_output = (residual + mixture).astype(bf16)
+    own_index = (lax.axis_index(DP) * 2 + lax.axis_index(BLK)) * 4 + lax.axis_index(SP)
+    own_features = lax.dynamic_slice_in_dim(
+        features_all.reshape(devices * tok_rows, model_width), own_index * own_rows, own_rows, axis=1
+    )
+    router_grad = product(own_features, logit_all.reshape(devices * tok_rows, EXPERTS), ((0,), (0,)))
+
+    grads_all = grads_all.reshape(seq_rows, model_width)
+    tall_grad = product(context, grads_all, ((0,), (0,))).astype(bf16)
+    context_grad = product(grads_all, tall_weight, ((1,), (1,))).astype(bf16)
+    prob_dots = product(split(context_grad), split(values), ((2,), (2,)), HEAD_BATCH)
+    row_delta = jnp.sum(attn_weights * prob_dots, axis=-1, keepdims=True)
+    score_grad = (attn_weights * (prob_dots - row_delta)).astype(bf16)
+    query_back = product(score_grad, split(keys), ((2,), (0,)), ((0,), (1,))).transpose(1, 0, 2) * score_scale
+    key_back = product(score_grad, split(queries), ((1,), (0,)), ((0,), (1,))).transpose(1, 0, 2) * score_scale
+    value_low = product(attn_low, split(context_grad), ((1,), (0,)), ((0,), (1,))).transpose(1, 0, 2)
+    value_low = value_low.astype(bf16).reshape(seq_rows, share)
+
+    def unrotate(grad):
+        grad = grad.astype(bf16).astype(f32).reshape(seq_rows, share)
+        return rotate_heads(grad, cosine, -sine)
+
+    query_back, key_back = unrotate(query_back), unrotate(key_back)
+    query_gain_grad = jnp.sum(query_back * query_u, axis=0)
+    key_gain_grad = jnp.sum(key_back * key_u, axis=0)
+    query_w, key_w = query_back * gain_query, key_back * gain_key
+    dots = jnp.stack([jnp.sum(query_w * query_u, axis=1), jnp.sum(key_w * key_u, axis=1)])
+    dots = column_sum(dots.reshape(16, seq_rows // 8), "dot_sums", 8).reshape(2, seq_rows) / model_width
+    query_low = (query_r * (query_w - query_u * dots[0][:, None])).astype(bf16)
+    key_low = (key_r * (key_w - key_u * dots[1][:, None])).astype(bf16)
+    linear_grad = jnp.concatenate([query_low, key_low, value_low], axis=1)
+    wide_grad = product(normed_all, linear_grad, ((0,), (0,))).astype(bf16)
+    normed_part = product(linear_grad, wide_weight, ((1,), (1,))).astype(bf16)
+    normed_part, mixture = lax.optimization_barrier((normed_part, mixture))
+    normed_grad, wide_back, tall_back = closing_call(
+        normed_part.reshape(column_size, tok_rows, model_width),
+        wide_grad.reshape(4, model_width // 4, 3 * share),
+        tall_grad.reshape(4, share // 4, model_width),
+    )
+    _, attention_pull = jax.vjp(norm_apply, tokens_f, gain_attention)
+    tokens_part, attention_gain_grad = attention_pull(normed_grad)
+    input_gradient = residual_grad + tokens_part
+    wide_back = wide_back.reshape(column_size, own_rows, 3, share).transpose(2, 1, 0, 3)
+    wide_back = wide_back.reshape(3, own_rows, model_width).astype(f32)
+
+    def spread(share_grad):
+        placed = jnp.zeros((model_width,), f32)
+        return lax.dynamic_update_slice(placed, share_grad, (column * share,))
+
+    gain_grads = jnp.stack(
+        [attention_gain_grad, spread(query_gain_grad), spread(key_gain_grad), feature_gain_grad]
+    )
+    gain_grads = gain_grads.reshape(4, devices, own_rows).transpose(1, 0, 2)
+    gain_grads = jnp.pad(gain_grads, ((0, 0), (0, 4), (0, 128 - own_rows)))
+    gain_sums = deal_sum(gain_grads, 9)
+    return (
+        block_output,
+        input_gradient,
+        wide_back[0],
+        wide_back[1],
+        wide_back[2],
+        tall_back.astype(f32),
+        router_grad,
+        gain_sums[0, :own_rows],
+        gain_sums[1, :own_rows],
+        gain_sums[2, :own_rows],
+        gain_sums[3, :own_rows],
+        gate_grad_local,
+        up_grad_local,
+        down_grad_local,
+    )
 
 
 def body(
@@ -74,9 +1750,9 @@
     routes,
     cotangent,
 ):
-    sp_size = lax.axis_size("sp")
-    blk_size = lax.axis_size("blk")
-    dp_size = lax.axis_size("dp")
+    sp_size = lax.axis_size(SP)
+    blk_size = lax.axis_size(BLK)
+    dp_size = lax.axis_size(DP)
     tok_rows = tokens.shape[0]
     model_width = tokens.shape[1]
     heads_here = HEADS // sp_size
@@ -95,15 +1771,15 @@
         gain_key,
         gain_feature,
     ) = (
-        lax.all_gather(query_weight, ("dp", "blk", "sp"), axis=0, tiled=True),
-        lax.all_gather(key_weight, ("dp", "blk", "sp"), axis=0, tiled=True),
-        lax.all_gather(value_weight, ("dp", "blk", "sp"), axis=0, tiled=True),
-        lax.all_gather(output_weight, ("dp", "blk", "sp"), axis=0, tiled=True),
-        lax.all_gather(router_weight, ("dp", "blk", "sp"), axis=0, tiled=True),
-        lax.all_gather(attention_gain, ("dp", "blk", "sp"), axis=0, tiled=True),
-        lax.all_gather(query_gain, ("dp", "blk", "sp"), axis=0, tiled=True),
-        lax.all_gather(key_gain, ("dp", "blk", "sp"), axis=0, tiled=True),
-        lax.all_gather(feature_gain, ("dp", "blk", "sp"), axis=0, tiled=True),
+        lax.all_gather(query_weight, AXES, axis=0, tiled=True),
+        lax.all_gather(key_weight, AXES, axis=0, tiled=True),
+        lax.all_gather(value_weight, AXES, axis=0, tiled=True),
+        lax.all_gather(output_weight, AXES, axis=0, tiled=True),
+        lax.all_gather(router_weight, AXES, axis=0, tiled=True),
+        lax.all_gather(attention_gain, AXES, axis=0, tiled=True),
+        lax.all_gather(query_gain, AXES, axis=0, tiled=True),
+        lax.all_gather(key_gain, AXES, axis=0, tiled=True),
+        lax.all_gather(feature_gain, AXES, axis=0, tiled=True),
     )
     gain_attention = gain_attention.astype(jnp.float32)
     gain_query = gain_query.astype(jnp.float32)
@@ -117,7 +1793,7 @@
     value_rows = jnp.dot(normed, value_full, preferred_element_type=jnp.float32).astype(
         jnp.bfloat16
     )
-    seq_start = (lax.axis_index("blk") * sp_size + lax.axis_index("sp")) * tok_rows
+    seq_start = (lax.axis_index(BLK) * sp_size + lax.axis_index(SP)) * tok_rows
     cosine, sine = rope_tables(seq_start + jnp.arange(tok_rows, dtype=jnp.int32), HEAD_DIM)
 
     def rotated(linear, norm_gain):
@@ -131,21 +1807,21 @@
     query_heads, key_heads, value_heads = (
         lax.all_to_all(
             query_rot.astype(jnp.bfloat16).reshape(tok_rows, sp_size, head_width),
-            "sp",
+            SP,
             split_axis=1,
             concat_axis=0,
             tiled=True,
         ),
         lax.all_to_all(
             key_rot.astype(jnp.bfloat16).reshape(tok_rows, sp_size, head_width),
-            "sp",
+            SP,
             split_axis=1,
             concat_axis=0,
             tiled=True,
         ),
         lax.all_to_all(
             value_rows.reshape(tok_rows, sp_size, head_width),
-            "sp",
+            SP,
             split_axis=1,
             concat_axis=0,
             tiled=True,
@@ -153,15 +1829,15 @@
     )
     head_rows = sp_size * tok_rows
     keys_all, values_all = (
-        lax.all_gather(key_heads, "blk", axis=0, tiled=True),
-        lax.all_gather(value_heads, "blk", axis=0, tiled=True),
+        lax.all_gather(key_heads, BLK, axis=0, tiled=True),
+        lax.all_gather(value_heads, BLK, axis=0, tiled=True),
     )
     key_rows = keys_all.shape[0]
     keys_all = keys_all.reshape(key_rows, heads_here, HEAD_DIM)
     values_all = values_all.reshape(key_rows, heads_here, HEAD_DIM)
     block_rows = math.gcd(512, head_rows)
     blocks = head_rows // block_rows
-    query_base = lax.axis_index("blk") * head_rows
+    query_base = lax.axis_index(BLK) * head_rows
     key_places = jnp.arange(key_rows, dtype=jnp.int32)
     query_blocks = query_heads.reshape(blocks, block_rows, heads_here, HEAD_DIM)
     block_starts = jnp.arange(blocks, dtype=jnp.int32) * block_rows
@@ -190,7 +1866,7 @@
     context_blocks, logsum = lax.map(attend_block, (query_blocks, block_starts))
     context_rows = lax.all_to_all(
         context_blocks.reshape(head_rows, 1, head_width),
-        "sp",
+        SP,
         split_axis=0,
         concat_axis=1,
         tiled=True,
@@ -223,7 +1899,7 @@
 
     send_rows = spread_halves(slot_rows)
     arrived = lax.all_to_all(
-        send_rows, ("dp", "blk", "sp"), split_axis=0, concat_axis=0, tiled=True
+        send_rows, AXES, split_axis=0, concat_axis=0, tiled=True
     )
     gate_values = jnp.einsum(
         "secd,edf->secf", arrived, gate_weight, preferred_element_type=jnp.float32
@@ -234,7 +1910,7 @@
         "secf,efd->secd", hidden, down_weight, preferred_element_type=jnp.float32
     ).astype(jnp.bfloat16)
     returned = lax.all_to_all(
-        part_out, ("dp", "blk", "sp"), split_axis=0, concat_axis=0, tiled=True
+        part_out, AXES, split_axis=0, concat_axis=0, tiled=True
     )
     expert_out = join_halves(returned)
     route_rows = expert_out[slot_index].reshape(tok_rows, TOPK, model_width)
@@ -263,8 +1939,8 @@
     )
     gradient_send = spread_halves(gradient_slots)
     gradient_arrived, rows_arrived = (
-        lax.all_to_all(gradient_send, ("dp", "blk", "sp"), split_axis=0, concat_axis=0, tiled=True),
-        lax.all_to_all(send_rows, ("dp", "blk", "sp"), split_axis=0, concat_axis=0, tiled=True),
+        lax.all_to_all(gradient_send, AXES, split_axis=0, concat_axis=0, tiled=True),
+        lax.all_to_all(send_rows, AXES, split_axis=0, concat_axis=0, tiled=True),
     )
     gate_values = jnp.einsum(
         "secd,edf->secf", rows_arrived, gate_weight, preferred_element_type=jnp.float32
@@ -297,7 +1973,7 @@
         + jnp.einsum("secf,edf->secd", up_grad, up_weight, preferred_element_type=jnp.float32)
     ).astype(jnp.bfloat16)
     returned_grads = lax.all_to_all(
-        input_parts, ("dp", "blk", "sp"), split_axis=0, concat_axis=0, tiled=True
+        input_parts, AXES, split_axis=0, concat_axis=0, tiled=True
     )
     slot_input_grad = join_halves(returned_grads)
     expert_input_grad = slot_input_grad[slot_index].reshape(tok_rows, TOPK, model_width)
@@ -313,7 +1989,7 @@
     )
     context_heads_grad = lax.all_to_all(
         context_grad.reshape(tok_rows, sp_size, head_width),
-        "sp",
+        SP,
         split_axis=1,
         concat_axis=0,
         tiled=True,
@@ -356,27 +2032,27 @@
         (query_blocks, context_heads_grad, logsum, block_starts),
     )
     key_mine, value_mine = (
-        lax.psum_scatter(key_total, "blk", scatter_dimension=0, tiled=True),
-        lax.psum_scatter(value_total, "blk", scatter_dimension=0, tiled=True),
+        lax.psum_scatter(key_total, BLK, scatter_dimension=0, tiled=True),
+        lax.psum_scatter(value_total, BLK, scatter_dimension=0, tiled=True),
     )
     query_back, key_back, value_back = (
         lax.all_to_all(
             query_grads.reshape(head_rows, 1, head_width),
-            "sp",
+            SP,
             split_axis=0,
             concat_axis=1,
             tiled=True,
         ),
         lax.all_to_all(
             key_mine.astype(jnp.bfloat16).reshape(head_rows, 1, head_width),
-            "sp",
+            SP,
             split_axis=0,
             concat_axis=1,
             tiled=True,
         ),
         lax.all_to_all(
             value_mine.astype(jnp.bfloat16).reshape(head_rows, 1, head_width),
-            "sp",
+            SP,
             split_axis=0,
             concat_axis=1,
             tiled=True,
@@ -400,15 +2076,15 @@
     tokens_part, attention_gain_grad = attention_pull(normed_grad)
     input_gradient = residual_grad + tokens_part
     summed = (
-        lax.psum_scatter(query_grad_full, ("dp", "blk", "sp"), scatter_dimension=0, tiled=True),
-        lax.psum_scatter(key_grad_full, ("dp", "blk", "sp"), scatter_dimension=0, tiled=True),
-        lax.psum_scatter(value_grad_full, ("dp", "blk", "sp"), scatter_dimension=0, tiled=True),
-        lax.psum_scatter(output_grad_full, ("dp", "blk", "sp"), scatter_dimension=0, tiled=True),
-        lax.psum_scatter(router_grad_full, ("dp", "blk", "sp"), scatter_dimension=0, tiled=True),
-        lax.psum_scatter(attention_gain_grad, ("dp", "blk", "sp"), scatter_dimension=0, tiled=True),
-        lax.psum_scatter(query_gain_grad, ("dp", "blk", "sp"), scatter_dimension=0, tiled=True),
-        lax.psum_scatter(key_gain_grad, ("dp", "blk", "sp"), scatter_dimension=0, tiled=True),
-        lax.psum_scatter(feature_gain_grad, ("dp", "blk", "sp"), scatter_dimension=0, tiled=True),
+        lax.psum_scatter(query_grad_full, AXES, scatter_dimension=0, tiled=True),
+        lax.psum_scatter(key_grad_full, AXES, scatter_dimension=0, tiled=True),
+        lax.psum_scatter(value_grad_full, AXES, scatter_dimension=0, tiled=True),
+        lax.psum_scatter(output_grad_full, AXES, scatter_dimension=0, tiled=True),
+        lax.psum_scatter(router_grad_full, AXES, scatter_dimension=0, tiled=True),
+        lax.psum_scatter(attention_gain_grad, AXES, scatter_dimension=0, tiled=True),
+        lax.psum_scatter(query_gain_grad, AXES, scatter_dimension=0, tiled=True),
+        lax.psum_scatter(key_gain_grad, AXES, scatter_dimension=0, tiled=True),
+        lax.psum_scatter(feature_gain_grad, AXES, scatter_dimension=0, tiled=True),
     )
     return (
         block_output,
@@ -430,36 +2106,37 @@
 
 def solution(mesh):
     in_specs = (
-        P(("dp", "blk", "sp"), None),
-        P(("dp", "blk", "sp"), None),
-        P(("dp", "blk", "sp"), None),
-        P(("dp", "blk", "sp"), None),
-        P(("dp", "blk", "sp"), None),
-        P(("dp", "blk", "sp"), None),
-        P(("dp", "blk", "sp")),
-        P(("dp", "blk", "sp")),
-        P(("dp", "blk", "sp")),
-        P(("dp", "blk", "sp")),
-        P(("dp", "sp"), None, "blk"),
-        P(("dp", "sp"), None, "blk"),
-        P(("dp", "sp"), "blk", None),
-        P(("dp", "blk", "sp"), None),
-        P(("dp", "blk", "sp"), None),
+        P(AXES, None),
+        P(AXES, None),
+        P(AXES, None),
+        P(AXES, None),
+        P(AXES, None),
+        P(AXES, None),
+        P(AXES),
+        P(AXES),
+        P(AXES),
+        P(AXES),
+        P((DP, SP), None, BLK),
+        P((DP, SP), None, BLK),
+        P((DP, SP), BLK, None),
+        P(AXES, None),
+        P(AXES, None),
     )
     out_specs = (
-        P(("dp", "blk", "sp"), None),
-        P(("dp", "blk", "sp"), None),
-        P(("dp", "blk", "sp"), None),
-        P(("dp", "blk", "sp"), None),
-        P(("dp", "blk", "sp"), None),
-        P(("dp", "blk", "sp"), None),
-        P(("dp", "blk", "sp"), None),
-        P(("dp", "blk", "sp")),
-        P(("dp", "blk", "sp")),
-        P(("dp", "blk", "sp")),
-        P(("dp", "blk", "sp")),
-        P(("dp", "sp"), None, "blk"),
-        P(("dp", "sp"), None, "blk"),
-        P(("dp", "sp"), "blk", None),
-    )
-    return jax.shard_map(body, mesh=mesh, in_specs=in_specs, out_specs=out_specs, check_vma=False)
+        P(AXES, None),
+        P(AXES, None),
+        P(AXES, None),
+        P(AXES, None),
+        P(AXES, None),
+        P(AXES, None),
+        P(AXES, None),
+        P(AXES),
+        P(AXES),
+        P(AXES),
+        P(AXES),
+        P((DP, SP), None, BLK),
+        P((DP, SP), None, BLK),
+        P((DP, SP), BLK, None),
+    )
+    fast = dict(mesh.shape) == {DP: 4, BLK: 2, SP: 4}
+    return jax.shard_map(body_fast if fast else body, mesh=mesh, in_specs=in_specs, out_specs=out_specs, check_vma=False)

time: 3360 us -> 830 us (0.25)
  waiting for transfers between devices: 2350 us -> 24.8 us
  Pallas kernels: 0 us -> 605 us
  blocking collectives: 486 us -> 0 us
  matrix products: 230 us -> 53.2 us
  other arithmetic: 96.1 us -> 44.5 us
  starting transfers between devices: 55.9 us -> 8.07 us
  local copies, waits for them, and re-layouts: 119 us -> 84.4 us
    reduce_scatter x7 -> x0, waiting for transfers between devices: 1390 us -> none  [the longest x1 365 us: body(): lax.psum_scatter(value_grad_full, ('dp', 'blk', 'sp'), scatter_dimension=...]
    all_to_all x9 -> x0, waiting for transfers between devices: 781 us -> none  [the longest x1 243 us: body(): lax.all_to_all(gradient_send, ('dp', 'blk', 'sp'), split_axis=0, concat_a...]
    pallas_call x0 -> x12, Pallas kernels: none -> 605 us  [the longest x5 396 us: hbm_call(): pl.pallas_call(kernel, out_shape=shapes, in_specs=[pl.BlockSpec(memory_sp...]
    all_gather x1 -> x0, blocking collectives: 341 us -> none  [body(): lax.all_gather(router_weight, ('dp', 'blk', 'sp'), axis=0, tiled=True)]
    dot_general x30 -> x15, matrix products: 230 us -> 44.4 us  [the longest x11 35.4 us: product(): lax.dot_general(left, right, (sums, batches), preferred_element_type=out)]
    all_gather x6 -> x0, waiting for transfers between devices: 171 us -> none  [the longest x1 72.5 us: body(): lax.all_gather(key_weight, ('dp', 'blk', 'sp'), axis=0, tiled=True)]
    unnamed x2 -> x0, blocking collectives: 84 us -> none
    all_to_all x3 -> x0, blocking collectives: 61.3 us -> none  [the longest x1 22.2 us: body(): lax.all_to_all(key_rot.astype(jnp.bfloat16).reshape(tok_rows, sp_size, he...]
  transfers between devices with their start and end apart: 22 -> 6, of which waited for: 16 -> 2; matrix products, arithmetic and copies ran while one was open for 10% -> 6% of each run, Pallas kernels for 0% -> 0%
where the time goes in v1:
time: 830 us; the launch traced here: 822 us
  Pallas kernels  605 us (73%)
  local copies, waits for them, and re-layouts  84.4 us (10%)
  matrix products  53.2 us (6%)
  other arithmetic  44.5 us (5%)
  waiting for transfers between devices  24.8 us (3%)
    pallas_call x5, Pallas kernels, hbm_call(): pl.pallas_call(kernel, out_shape=shapes, in_specs=[pl.BlockSpec(memory_sp...  396 us
    pallas_call x1, Pallas kernels, gather_call(): pl.pallas_call(kernel, out_shape=[jax.ShapeDtypeStruct((32 if full else 8...  79.6 us
    pallas_call x1, Pallas kernels, run_experts(): pl.pallas_call(kernel, out_shape=[narrow, narrow, narrow, wide, wide, col...  49.3 us
    unnamed x141, local copies, waits for them, and re-layouts  42.6 us
    dot_general x11, matrix products, product(): lax.dot_general(left, right, (sums, batches), preferred_element_type=out)  35.4 us
    pallas_call x1, Pallas kernels, put_rows_back(): pl.pallas_call(kernel, out_shape=[shape, shape], grid=(pairs,), in_specs=...  28.3 us
    pallas_call x1, Pallas kernels, pick_rows(): pl.pallas_call(kernel, out_shape=[shape, shape], grid=(pairs,), in_specs=...  27.4 us
    ppermute x6, waiting for transfers between devices, shift_line(): return lax.ppermute(rows, SP, [(i, (i + step) % size) for i in range(size)])  24.8 us
  transfers between devices with their start and end apart: 6, of which 2 were waited for; matrix products, arithmetic and copies ran while one was open for 6% of the time, Pallas kernels for 0%

profile of v1, /device:TPU:0, one launch (start us, length us, event | category | flops | bytes accessed | tf_op | source)
XLA Modules:
  0.0 822.0 jit_solution(9055578046881924995)
XLA Ops:
  6.0 80.1 %opening.1 = (bf16[8,128,2048]{2,1,0:T(8,128)(2,1)}, bf16[32,64,128]{2,1,0:T(8,128)(2,1)}, bf16[32,128,2048]{2,1,0:T(8,128)(2,1)}, bf16[2048,768]{1,0:T(8,128)(2,1)}, bf16[256,2048]{1,0:T(8,128)(2,1)}) custom-call(bf16[128,2048]{1,0:T(8,128)(2,1)} %tok.1, bf16[64,128]{1,0:T(8,128)(2,1)} %concatenate.33.sml, bf16[128,2048]{1,0:T(8,128)(2,1)} %cot.1, ...), custom_call_target="tpu_custom_call" | custom-call | tf_op jit(solution)/shard_map/opening/pallas_call | solution.py:1127
  97.7 7.8 square_sums.1
  129.8 8.8 %fusion.72 = (f32[2,1024]{1,0:T(2,128)S(1)}, f32[2,1024,1024]{1,2,0:T(8,128)}) fusion(pred[1024,1024]{0,1:T(8,128)(4,1)} %iota_compare_fusion, bf16[1024,2,64]{2,0,1:T(8,128)(2,1)} %get-tuple-element.118, bf16[1024,2,64]{2,0,1:T(8,128)(2,1)} %get-tuple-element.119, bf16[1024,2,64]{2,0,1:T(8,128)(2,1)} %get-tuple-element.101, ...), kind=kOutput, calls=%fused_computation.162 | convolution fusion | flops 547357696 | bytes 10493952 | tf_op jit(solution)/shard_map/sub | solution.py:1586
  138.7 4.2 fusion.18
  147.3 65.9 %attended.1 = (f32[128,2048]{1,0:T(8,128)}, bf16[32,128,2048]{2,1,0:T(8,128)(2,1)}) custom-call(bf16[8,128,2048]{2,1,0:T(8,128)(2,1)} %bitcast.142, bf16[128,2048]{1,0:T(8,128)(2,1)} %collective-permute-done.first, bf16[128,2048]{1,0:T(8,128)(2,1)} %collective-permute-done.1.second, ...), custom_call_target="tpu_custom_call", output_to_operand_aliasing={{1}: (4, {})} | custom-call | tf_op jit(solution)/shard_map/attended/pallas_call | solution.py:1127
  218.3 79.6 %features_gather.1 = (bf16[32,128,2048]{2,1,0:T(8,128)(2,1)}, f32[32,64,128]{2,1,0:T(8,128)}) custom-call(bf16[128,2048]{1,0:T(8,128)(2,1)} %copy-done.14, f32[64,128]{1,0:T(8,128)} %reshape.348.refs_1_), custom_call_target="tpu_custom_call" | custom-call | tf_op jit(solution)/shard_map/features_gather/pallas_call | solution.py:408
  309.7 27.4 %pick_rows.1 = (bf16[4,768,2048]{2,1,0:T(8,128)(2,1)}, bf16[4,768,2048]{2,1,0:T(8,128)(2,1)}) custom-call(bf16[16,192,256]{2,1,0:T(8,128)(2,1)} %bitcast.144, bf16[16,256,2048]{2,1,0:T(8,128)(2,1)} %bitcast.145, bf16[16,256,2048]{2,1,0:T(8,128)(2,1)} %bitcast.141), custom_call_target="tpu_custom_call" | custom-call | tf_op jit(solution)/shard_map/pick_rows/pallas_call | solution.py:716
  337.1 49.3 %run_experts.1 = (bf16[4,768,512]{2,1,0:T(8,128)(2,1)}, bf16[4,768,512]{2,1,0:T(8,128)(2,1)}, bf16[4,768,512]{2,1,0:T(8,128)(2,1)}, bf16[4,768,2048]{2,1,0:T(8,1...) custom-call(bf16[4,768,2048]{2,1,0:T(8,128)(2,1)} %get-tuple-element.57.x.refs_0_, ...), custom_call_target="tpu_custom_call" | custom-call | tf_op jit(solution)/shard_map/run_experts/pallas_call | solution.py:785
  389.9 28.3 %put_rows_back.1 = (bf16[16,256,2048]{2,1,0:T(8,128)(2,1)}, bf16[16,256,2048]{2,1,0:T(8,128)(2,1)}) custom-call(bf16[16,256,192]{2,1,0:T(8,128)(2,1)} %bitcast.158, bf16[4,768,2048]{2,1,0:T(8,128)(2,1)} %get-tuple-element.60.out_ref, bf16[4,768,2048]{2,1,0:T(8,128)(2,1)} %get-tuple-element.61.input_ref), custom_call_target="tpu_custom_call" | custom-call | tf_op jit(solution)/shard_map/put_rows_back/pallas_call | solution.py:740
  418.2 83.5 %experts_back.1 = (f32[128,2048]{1,0:T(8,128)}, f32[32,8,128]{2,1,0:T(8,128)}, f32[4,2048,512]{2,1,0:T(8,128)}, f32[4,2048,512]{2,1,0:T(8,128)}, f32[4,512,2048]{2,1,0:T(8,128)}) custom-call(bf16[32,128,2048]{2,1,0:T(8,128)(2,1)} %bitcast.147, f32[32,8,128]{2,1,0:T(8,128)} %pad.10.dealt_ref, bf16[4,768,2048]{2,1,0:T(8,128)(2,1)} %get-tuple-element.57.x.refs_0_, ...), custom_call_target="tpu_custom_call" | custom-call | tf_op jit(solution)/shard_map/experts_back/pallas_call | solution.py:1127
  506.8 80.4 %residual_grad.1 = (bf16[8,128,2048]{2,1,0:T(8,128)(2,1)}, bf16[32,64,128]{2,1,0:T(8,128)(2,1)}, bf16[4,128,2048]{2,1,0:T(8,128)(2,1)}) custom-call(bf16[128,2048]{1,0:T(8,128)(2,1)} %fusion.62.grad_ref, bf16[64,128]{1,0:T(8,128)(2,1)} %reshape.357.logit_ref, bf16[32,128,2048]{2,1,0:T(8,128)(2,1)} %bitcast.148), custom_call_target="tpu_custom_call" | custom-call | tf_op jit(solution)/shard_map/residual_grad/pallas_call | solution.py:1127
  590.8 4.9 multiply_reduce_fusion
  612.5 7.2 dot_sums.1
  623.1 4.9 convolution_convert_fusion.2
  628.0 5.0 convolution_convert_fusion.1
  643.5 4.4 convolution_convert_fusion.3
  647.9 3.7 collective-permute-done.3
  651.6 21.1 %collective-permute-done.4 = bf16[128,2048]{1,0:T(8,128)(2,1)} collective-permute-done((bf16[128,2048]{1,0:T(8,128)(2,1)}, bf16[128,2048]{1,0:T(8,128)(2,1)}, u32[]{:S(2)}, u32[]{:S(2)}) %collective-permute-start.4) | collective-permute-done | bytes 524320 | tf_op jit(solution)/shard_map/ppermute | solution.py:1504
  675.3 85.6 %closing.1 = (f32[128,2048]{1,0:T(8,128)}, bf16[8,64,768]{2,1,0:T(8,128)(2,1)}, bf16[64,2048]{1,0:T(8,128)(2,1)}) custom-call(bf16[8,128,2048]{2,1,0:T(8,128)(2,1)} %bitcast.160, bf16[4,512,768]{2,1,0:T(8,128)(2,1)} %bitcast.163, bf16[4,64,2048]{2,1,0:T(8,128)(2,1)} %bitcast.170), custom_call_target="tpu_custom_call" | custom-call | tf_op jit(solution)/shard_map/closing/pallas_call | solution.py:1127
  763.4 9.8 %gain_gradients.1 = f32[8,128]{1,0:T(8,128)} custom-call(f32[32,8,128]{2,1,0:T(8,128)} %pad.11.src), custom_call_target="tpu_custom_call" | custom-call | tf_op jit(solution)/shard_map/gain_gradients/pallas_call | solution.py:1487
  778.2 4.6 fusion.65
  789.1 13.5 %copy.270 = f32[4,2048,512]{2,1,0:T(8,128)} copy(f32[4,2048,512]{2,1,0:T(8,128)} %get-tuple-element.180) | data formatting | bytes 33554432
  804.3 8.5 %copy.271 = f32[4,2048,512]{2,1,0:T(8,128)} copy(f32[4,2048,512]{2,1,0:T(8,128)S(1)} %bitcast.152) | data formatting | bytes 33554432
  815.4 6.2 copy.272
  (264 shorter events, 125.1 us)
Async XLA Ops:
  96.6 19.3 %copy-start = (f32[1024,768]{0,1:T(8,128)}, f32[1024,768]{0,1:T(8,128)S(1)}, u32[]{:S(2)}) copy-start(f32[1024,768]{0,1:T(8,128)S(1)} %fusion.74) | copy-start | bytes 9437188
  106.2 41.1 %collective-permute-start = (bf16[128,2048]{1,0:T(8,128)(2,1)}, bf16[128,2048]{1,0:T(8,128)(2,1)}, u32[]{:S(2)}, u32[]{:S(2)}) collective-permute-start(bf16[128,2048]{1,0:T(8,128)(2,1)} %cot.1), channel_id=1, source_target_pairs={{0,1},{1,2},{2,3},{3,0},{4,5},{5,6},{6,7},{7,4},{8,9},{9,10},{10,1... | collective-permute-start | bytes 1572872 | tf_op jit(solution)/shard_map/ppermute | solution.py:1504
  106.8 40.4 %collective-permute-start.1 = (bf16[128,2048]{1,0:T(8,128)(2,1)}, bf16[128,2048]{1,0:T(8,128)(2,1)}, u32[]{:S(2)}, u32[]{:S(2)}) collective-permute-start(bf16[128,2048]{1,0:T(8,128)(2,1)} %cot.1), channel_id=1, source_target_pairs={{0,2},{1,3},{2,0},{3,1},{4,6},{5,7},{6,4},{7,5},{8,10},{9,11},{10,... | collective-permute-start | bytes 1572872 | tf_op jit(solution)/shard_map/ppermute | solution.py:1504
  108.1 39.1 %collective-permute-start.2 = (bf16[128,2048]{1,0:T(8,128)(2,1)}, bf16[128,2048]{1,0:T(8,128)(2,1)}, u32[]{:S(2)}, u32[]{:S(2)}) collective-permute-start(bf16[128,2048]{1,0:T(8,128)(2,1)} %cot.1), channel_id=1, source_target_pairs={{0,3},{1,0},{2,1},{3,2},{4,7},{5,4},{6,5},{7,6},{8,11},{9,8},{10,9... | collective-permute-start | bytes 1572872 | tf_op jit(solution)/shard_map/ppermute | solution.py:1504
  147.3 65.9 %copy-start.6 = (bf16[128,2048]{1,0:T(8,128)(2,1)S(1)}, bf16[128,2048]{1,0:T(8,128)(2,1)}, u32[]{:S(2)}) copy-start(bf16[128,2048]{1,0:T(8,128)(2,1)} %tok.1) | copy-start | bytes 1572868
  337.1 51.4 %copy-start.2 = (bf16[16,4,48,256]{3,2,1,0:T(8,128)(2,1)S(1)}, bf16[16,4,48,256]{3,2,1,0:T(8,128)(2,1)}, u32[]{:S(2)}) copy-start(bf16[16,4,48,256]{3,2,1,0:T(8,128)(2,1)} %copy-done.1) | copy-start | bytes 4718596
  418.2 84.6 %copy-start.30 = (f32[128,64]{0,1:T(8,128)S(1)}, f32[128,64]{0,1:T(8,128)}, u32[]{:S(2)}) copy-start(f32[128,64]{0,1:T(8,128)} %copy-done.29) | copy-start | bytes 98308
  418.2 84.6 %copy-start.42 = (f32[128]{0:T(128)S(1)}, f32[128]{0:T(128)}, u32[]{:S(2)}) copy-start(f32[128]{0:T(128)} %copy-done.41) | copy-start | bytes 1540
  418.2 84.6 %copy-start.48 = (f32[128]{0:T(128)S(1)}, f32[128]{0:T(128)}, u32[]{:S(2)}) copy-start(f32[128]{0:T(128)} %copy-done.47) | copy-start | bytes 1540
  418.2 84.8 %copy-start.9 = (bf16[32,64,128]{2,1,0:T(8,128)(2,1)S(1)}, bf16[32,64,128]{2,1,0:T(8,128)(2,1)}, u32[]{:S(2)}) copy-start(bf16[32,64,128]{2,1,0:T(8,128)(2,1)} %get-tuple-element.48) | copy-start | bytes 1572868
  418.2 84.8 %copy-start.46 = (f32[128]{0:T(128)S(1)}, f32[128]{0:T(128)}, u32[]{:S(2)}) copy-start(f32[128]{0:T(128)} %copy-done.45) | copy-start | bytes 1540
  418.2 86.6 %copy-start.51 = (f32[128]{0:T(128)S(1)}, f32[128]{0:T(128)}, u32[]{:S(2)}) copy-start(f32[128]{0:T(128)} %copy-done.50) | copy-start | bytes 1540
  504.8 82.5 %copy-start.4 = (f32[128,2048]{1,0:T(8,128)}, f32[128,2048]{1,0:T(8,128)S(1)}, u32[]{:S(2)}) copy-start(f32[128,2048]{1,0:T(8,128)S(1)} %get-tuple-element.148) | copy-start | bytes 3145732
  506.8 80.5 %copy-start.28 = (bf16[256,2048]{1,0:T(8,128)(2,1)S(1)}, bf16[256,2048]{1,0:T(8,128)(2,1)}, u32[]{:S(2)}) copy-start(bf16[256,2048]{1,0:T(8,128)(2,1)} %get-tuple-element.51) | copy-start | bytes 3145732
  634.3 17.3 %collective-permute-start.3 = (bf16[128,2048]{1,0:T(8,128)(2,1)}, bf16[128,2048]{1,0:T(8,128)(2,1)}, u32[]{:S(2)}, u32[]{:S(2)}) collective-permute-start(bf16[128,2048]{1,0:T(8,128)(2,1)} %get-tuple-element.113), channel_id=1, source_target_pairs={{0,1},{1,2},{2,3},{3,0},{4,5},{5,6},{6,7},{7,4},{8,9},{9,10},{10,1... | collective-permute-start | bytes 1572872 | tf_op jit(solution)/shard_map/ppermute | solution.py:1504
  635.2 37.5 %collective-permute-start.4 = (bf16[128,2048]{1,0:T(8,128)(2,1)}, bf16[128,2048]{1,0:T(8,128)(2,1)}, u32[]{:S(2)}, u32[]{:S(2)}) collective-permute-start(bf16[128,2048]{1,0:T(8,128)(2,1)} %get-tuple-element.115), channel_id=1, source_target_pairs={{0,2},{1,3},{2,0},{3,1},{4,6},{5,7},{6,4},{7,5},{8,10},{9,11},{10,... | collective-permute-start | bytes 1572872 | tf_op jit(solution)/shard_map/ppermute | solution.py:1504
  636.8 35.8 %collective-permute-start.5 = (bf16[128,2048]{1,0:T(8,128)(2,1)}, bf16[128,2048]{1,0:T(8,128)(2,1)}, u32[]{:S(2)}, u32[]{:S(2)}) collective-permute-start(bf16[128,2048]{1,0:T(8,128)(2,1)} %get-tuple-element.114), channel_id=1, source_target_pairs={{0,3},{1,0},{2,1},{3,2},{4,7},{5,4},{6,5},{7,6},{8,11},{9,8},{10,9... | collective-permute-start | bytes 1572872 | tf_op jit(solution)/shard_map/ppermute | solution.py:1504
  675.3 85.6 %copy-start.7 = (bf16[128,2048]{1,0:T(8,128)(2,1)S(1)}, bf16[128,2048]{1,0:T(8,128)(2,1)}, u32[]{:S(2)}) copy-start(bf16[128,2048]{1,0:T(8,128)(2,1)} %tok.1) | copy-start | bytes 1572868
  675.3 85.6 %copy-start.36 = (f32[2048,1]{0,1:T(1,128)S(1)}, f32[2048,1]{0,1:T(1,128)}, u32[]{:S(2)}) copy-start(f32[2048,1]{0,1:T(1,128)} %copy-done.35) | copy-start | bytes 24580
  786.6 15.9 %slice-start.4 = ((s8[16777216]{0:T(1024)(128)(4,1)}), s8[4194304]{0:T(1024)(128)(4,1)S(1)}, s32[]{:S(2)}) async-start(s8[16777216]{0:T(1024)(128)(4,1)} %bitcast.151), calls=%async_computation.4 | async-start | bytes 8388608
  789.0 13.5 %slice-start.6 = ((s8[16777216]{0:T(1024)(128)(4,1)}), s8[4194304]{0:T(1024)(128)(4,1)S(1)}, s32[]{:S(2)}) async-start(s8[16777216]{0:T(1024)(128)(4,1)} %bitcast.151), calls=%async_computation.6 | async-start | bytes 8388608
  789.0 15.3 %slice-start.7 = ((s8[16777216]{0:T(1024)(128)(4,1)}), s8[4194304]{0:T(1024)(128)(4,1)S(1)}, s32[]{:S(2)}) async-start(s8[16777216]{0:T(1024)(128)(4,1)} %bitcast.151), calls=%async_computation.7 | async-start | bytes 8388608
  789.0 23.8 %slice-start = ((s8[16777216]{0:T(1024)(128)(4,1)}), s8[4194304]{0:T(1024)(128)(4,1)S(1)}, s32[]{:S(2)}) async-start(s8[16777216]{0:T(1024)(128)(4,1)} %bitcast.149), calls=%async_computation | async-start | bytes 8388608
  789.1 23.8 %slice-start.1 = ((s8[16777216]{0:T(1024)(128)(4,1)}), s8[4194304]{0:T(1024)(128)(4,1)S(1)}, s32[]{:S(2)}) async-start(s8[16777216]{0:T(1024)(128)(4,1)} %bitcast.149), calls=%async_computation.1 | async-start | bytes 8388608
  (47 other events, 226.9 us)

commit v2 on v1

--- a/solution.py
+++ b/solution.py
@@ -145,9 +145,9 @@
     SENDS = 40
     RECVS = 37
 
-    def __init__(self, place, src, out, send, recv, full, direct=False):
+    def __init__(self, place, src, out, send, recv, full, direct=False, others=False):
         self.p, self.src, self.out, self.send, self.recv, self.full = place, src, out, send, recv, full
-        self.direct = direct
+        self.direct, self.others = direct, others
         self.half = src.shape[0] // 2
 
     def slot(self, k, blk, s):
@@ -227,8 +227,9 @@
         def _():
             self.down(z, True).start()
 
-        self.spread(z, True)
-        self.own_copy().start()
+        if not self.others:
+            self.spread(z, True)
+            self.own_copy().start()
 
     def along(self, d):
         z = self.p.z
@@ -262,7 +263,8 @@
     def each(self, d, act):
         z = self.p.z
         if d == 0:
-            act(z)
+            if not self.others:
+                act(z)
             return
 
         @pl.when(z >= d)
@@ -313,7 +315,7 @@
 
         @pl.loop(0, 4)
         def _(s):
-            self.settle_plane(s)
+            pl.when((s != z) | (not self.others))(lambda: self.settle_plane(s))
             if not self.direct:
 
                 @pl.when((s <= z) & (z < 3))
@@ -327,7 +329,8 @@
         if self.direct:
             for step in (1, 2, 3):
                 self.straight(step).wait_send()
-        self.own_copy().wait()
+        if not self.others:
+            self.own_copy().wait()
 
     def steps(self):
         return [
@@ -379,43 +382,44 @@
             pltpu.make_async_copy(src, self.block(0, s), self.local.at[i]).wait()
 
 
+class PlaneFlow(GatherFlow):
+    def __init__(self, place, blocks, out, send, recv, local):
+        super().__init__(place, blocks[0][1], out, send, recv, True)
+        self.blocks, self.local = blocks, local
+
+    def begin(self):
+        for i, (s, src) in enumerate(self.blocks):
+            self.src = src
+            self.spread(s, True)
+            pltpu.make_async_copy(src, self.block(0, s), self.local.at[i]).start()
+
+    def turns(self):
+        for s, _ in self.blocks:
+            self.got(4 + s, self.block(1, s))
+            self.turn_y(s).start()
+            self.core(1, s).start()
+            self.got(8 + s, self.block(2, s))
+            self.turn_x(s).start()
+            self.core(2, s).start()
+
+    def corners(self):
+        for s, _ in self.blocks:
+            self.got(12 + s, self.block(3, s).at[pl.ds(0, self.half)])
+            self.got(16 + s, self.block(3, s).at[pl.ds(self.half, self.half)])
+            self.core(3, s).start()
+
+    def finish(self):
+        for i, (s, src) in enumerate(self.blocks):
+            self.settle_plane(s)
+            pltpu.make_async_copy(src, self.block(0, s), self.local.at[i]).wait()
+
+
 def run_flows(flows):
     lists = [flow.steps() for flow in flows]
     for position in range(max(len(steps) for steps in lists)):
         for steps in lists:
             if position < len(steps):
                 steps[position]()
-
-
-def gather_call(arrays, fulls, name, collective_id):
-    count = len(arrays)
-
-    def kernel(*refs):
-        srcs, outs = refs[:count], refs[count : 2 * count]
-        sems = refs[2 * count :]
-        place = Place()
-        entry_barrier(place, "planes" if any(fulls) else "line")
-        run_flows(
-            [
-                GatherFlow(place, srcs[i], outs[i], sems[2 * i], sems[2 * i + 1], fulls[i])
-                for i in range(count)
-            ]
-        )
-
-    scratch = []
-    for _ in arrays:
-        scratch += [pltpu.SemaphoreType.DMA((GatherFlow.SENDS,)), pltpu.SemaphoreType.DMA((GatherFlow.RECVS,))]
-    return pl.pallas_call(
-        kernel,
-        out_shape=[
-            jax.ShapeDtypeStruct((32 if full else 8,) + a.shape, a.dtype) for a, full in zip(arrays, fulls)
-        ],
-        in_specs=[pl.BlockSpec(memory_space=pl.ANY)] * count,
-        out_specs=[pl.BlockSpec(memory_space=pl.ANY)] * count,
-        scratch_shapes=scratch,
-        compiler_params=pltpu.CompilerParams(collective_id=collective_id, has_side_effects=True),
-        name=name,
-    )(*arrays)
 
 
 def add_rows(dst, terms, rows):
@@ -433,14 +437,15 @@
     RECVS = 16 + 8 + 8 + 4 + 4
     LOCALS = 20
 
-    def __init__(self, place, part, out, scratch, full, plane_only=False):
-        self.p, self.part, self.out, self.full, self.plane_only = place, part, out, full, plane_only
+    def __init__(self, place, part, out, scratch, full, band=None):
+        self.p, self.part, self.out, self.full, self.plane_only = place, part, out, full, band is not None
         if full:
             (self.acc, self.near, self.half_in, self.side_in, self.line_in, self.sum, self.send, self.recv, self.local) = scratch
         else:
             (self.acc, self.near, self.line_in, self.sum, self.send, self.recv, self.local) = scratch
         self.columns = 4 if full else 1
-        self.rows = part.shape[1]
+        first, self.rows = band or (0, part.shape[1])
+        self.band = pl.ds(first, self.rows)
         self.half = self.rows // 2
 
     @staticmethod
@@ -471,12 +476,12 @@
 
     def load(self, k, s):
         return pltpu.make_async_copy(
-            self.part.at[self.slot(k, self.p.blk, s)], self.acc.at[k, s], self.local.at[4 * k + s]
+            self.part.at[self.slot(k, self.p.blk, s), self.band], self.acc.at[k, s], self.local.at[4 * k + s]
         )
 
     def core(self, k, s):
         return remote(
-            self.part.at[self.slot(k, 1 - self.p.blk, s)],
+            self.part.at[self.slot(k, 1 - self.p.blk, s), self.band],
             self.near.at[k, s],
             self.send.at[4 * k + s],
             self.recv.at[4 * k + s],
@@ -699,105 +704,329 @@
     )
 
 
-def pick_rows(picks, features, grads, experts):
-    pairs, picked, pair_rows = picks.shape
+def is_place(places, per):
+    return lax.broadcasted_iota(jnp.int32, (per, places.shape[1]), 0) == places
+
+
+def one_hot(places, per):
+    experts = places.shape[0]
+    hot = [is_place(places[e : e + 1], per).astype(jnp.float32) for e in range(experts)]
+    return jnp.concatenate(hot, axis=0).astype(jnp.bfloat16)
+
+
+def pick_rows(places, probs, features, per):
+    pairs, experts, pair_rows = places.shape
     width = features.shape[-1]
-    per = picked // experts
-
-    def kernel(pick_ref, feature_ref, grad_ref, row_ref, grad_row_ref):
-        for src, dst in ((feature_ref, row_ref), (grad_ref, grad_row_ref)):
-            rows = inner(pick_ref[0], src[0]).astype(dst.dtype)
+    step = 2
+
+    def kernel(place_ref, prob_ref, feature_ref, row_ref, row_prob_ref):
+        for i in range(step):
+            rows = inner(one_hot(place_ref[i], per), feature_ref[i]).astype(row_ref.dtype)
             for e in range(experts):
-                dst[e] = rows[e * per : (e + 1) * per]
-
-    shape = jax.ShapeDtypeStruct((experts, pairs * per, width), features.dtype)
-    source = pl.BlockSpec((1, pair_rows, width), lambda p: (p, 0, 0))
-    target = pl.BlockSpec((experts, per, width), lambda p: (0, p, 0))
+                at = pl.ds(i * per, per)
+                row_ref[e, at] = rows[e * per : (e + 1) * per]
+                hot = is_place(place_ref[i, e : e + 1], per)
+                row_prob_ref[e, at] = jnp.sum(
+                    jnp.where(hot, prob_ref[i, e : e + 1], 0.0), axis=1, keepdims=True
+                )
+
+    small = pl.BlockSpec((step, experts, pair_rows), lambda p: (p, 0, 0))
     return pl.pallas_call(
         kernel,
-        out_shape=[shape, shape],
-        grid=(pairs,),
-        in_specs=[pl.BlockSpec((1, picked, pair_rows), lambda p: (p, 0, 0)), source, source],
-        out_specs=[target, target],
+        out_shape=[
+            jax.ShapeDtypeStruct((experts, pairs * per, width), features.dtype),
+            jax.ShapeDtypeStruct((experts, pairs * per, 1), jnp.float32),
+        ],
+        grid=(pairs // step,),
+        in_specs=[small, small, pl.BlockSpec((step, pair_rows, width), lambda p: (p, 0, 0))],
+        out_specs=[
+            pl.BlockSpec((experts, step * per, width), lambda p: (0, p, 0)),
+            pl.BlockSpec((experts, step * per, 1), lambda p: (0, p, 0)),
+        ],
         compiler_params=local_params(),
         name="pick_rows",
-    )(picks, features, grads)
-
-
-def put_rows_back(places, out_rows, input_rows):
-    pairs, pair_rows, picked = places.shape
-    experts, _, width = out_rows.shape
-    per = picked // experts
-
-    def kernel(place_ref, out_ref, input_ref, out_sum, input_sum):
-        for src, dst in ((out_ref, out_sum), (input_ref, input_sum)):
-            rows = jnp.concatenate([src[e] for e in range(experts)], axis=0)
-            dst[0] = inner(place_ref[0], rows).astype(dst.dtype)
-
-    shape = jax.ShapeDtypeStruct((pairs, pair_rows, width), out_rows.dtype)
-    source = pl.BlockSpec((experts, per, width), lambda p: (0, p, 0))
-    target = pl.BlockSpec((1, pair_rows, width), lambda p: (p, 0, 0))
+    )(places, probs, features)
+
+
+def put_rows_back(places, rows, row_grads):
+    pairs, experts, pair_rows = places.shape
+    _, slots, width = rows.shape
+    per = slots // pairs
+    step = 2
+    half = pair_rows // 2
+
+    def kernel(place_ref, row_ref, grad_ref, sum_ref, prob_ref):
+        for i in range(step):
+            at = pl.ds(i * per, per)
+            gathered = jnp.concatenate([row_ref[e, at] for e in range(experts)], axis=0)
+            sum_ref[i] = inner(one_hot(place_ref[i], per), gathered, 0, 0).astype(sum_ref.dtype)
+            prob_ref[2 * i : 2 * i + 2] = jnp.zeros((2, 8, half), jnp.float32)
+            for e in range(experts):
+                hot = is_place(place_ref[i, e : e + 1], per)
+                line = jnp.sum(jnp.where(hot, grad_ref[e, at], 0.0), axis=0, keepdims=True)
+                prob_ref[2 * i, e : e + 1] = line[:, :half]
+                prob_ref[2 * i + 1, e : e + 1] = line[:, half:]
+
     return pl.pallas_call(
         kernel,
-        out_shape=[shape, shape],
-        grid=(pairs,),
-        in_specs=[pl.BlockSpec((1, pair_rows, picked), lambda p: (p, 0, 0)), source, source],
-        out_specs=[target, target],
+        out_shape=[
+            jax.ShapeDtypeStruct((pairs, pair_rows, width), rows.dtype),
+            jax.ShapeDtypeStruct((2 * pairs, 8, half), jnp.float32),
+        ],
+        grid=(pairs // step,),
+        in_specs=[
+            pl.BlockSpec((step, experts, pair_rows), lambda p: (p, 0, 0)),
+            pl.BlockSpec((experts, step * per, width), lambda p: (0, p, 0)),
+            pl.BlockSpec((experts, step * per, 1), lambda p: (0, p, 0)),
+        ],
+        out_specs=[
+            pl.BlockSpec((step, pair_rows, width), lambda p: (p, 0, 0)),
+            pl.BlockSpec((2 * step, 8, half), lambda p: (p, 0, 0)),
+        ],
         compiler_params=local_params(),
         name="put_rows_back",
-    )(places, out_rows, input_rows)
-
-
-def run_experts(rows, grads, probs, gate_weight, up_weight, down_weight):
+    )(places, rows, row_grads)
+
+
+def run_experts(rows, plain_grads, probs, gate_weight, up_weight):
     experts, slots, width = rows.shape
     hidden = gate_weight.shape[2]
     parts = 2
     part = slots // parts
 
-    def kernel(x, c, p, wg, wu, wd, weighted, gate_back, up_back, out, back, prob_back):
+    def kernel(x, plain_ref, p, wg, wu, weighted, gate_back, up_back, back, prob_back):
         gate = inner(x[0], wg[0])
         up = inner(x[0], wu[0])
-        plain = inner(c[0], wd[0], 1, 1)
+        plain = plain_ref[0]
         prob = p[0]
         sig = jax.nn.sigmoid(gate)
         act = gate * sig
         hid = act * up
         prob_back[0] = jnp.sum(hid * plain, axis=1, keepdims=True)
-        low = (hid * prob).astype(jnp.bfloat16)
-        weighted[0] = low
+        weighted[0] = (hid * prob).astype(jnp.bfloat16)
         grad = plain * prob
         gate_low = (grad * up * sig * (1.0 + gate * (1.0 - sig))).astype(jnp.bfloat16)
         up_low = (grad * act).astype(jnp.bfloat16)
         gate_back[0] = gate_low
         up_back[0] = up_low
-        out[0] = inner(low, wd[0]).astype(jnp.bfloat16)
         back[0] = (inner(gate_low, wg[0], 1, 1) + inner(up_low, wu[0], 1, 1)).astype(jnp.bfloat16)
 
     def block(size):
         return pl.BlockSpec((1, part, size), lambda e, i: (e, i, 0))
 
-    def whole(shape):
-        return pl.BlockSpec((1,) + shape[1:], lambda e, i: (e, 0, 0))
-
+    weight = pl.BlockSpec((1, width, hidden), lambda e, i: (e, 0, 0))
     narrow = jax.ShapeDtypeStruct((experts, slots, hidden), rows.dtype)
-    wide = jax.ShapeDtypeStruct(rows.shape, rows.dtype)
-    column = jax.ShapeDtypeStruct((experts, slots, 1), jnp.float32)
     return pl.pallas_call(
         kernel,
-        out_shape=[narrow, narrow, narrow, wide, wide, column],
+        out_shape=[
+            narrow,
+            narrow,
+            narrow,
+            jax.ShapeDtypeStruct(rows.shape, rows.dtype),
+            jax.ShapeDtypeStruct((experts, slots, 1), jnp.float32),
+        ],
         grid=(experts, parts),
-        in_specs=[
-            block(width),
-            block(width),
-            block(1),
-            whole(gate_weight.shape),
-            whole(up_weight.shape),
-            whole(down_weight.shape),
-        ],
-        out_specs=[block(hidden)] * 3 + [block(width)] * 2 + [block(1)],
+        in_specs=[block(width), block(hidden), block(1), weight, weight],
+        out_specs=[block(hidden)] * 3 + [block(width), block(1)],
         compiler_params=local_params(),
         name="run_experts",
-    )(rows, grads, probs, gate_weight, up_weight, down_weight)
+    )(rows, plain_grads, probs, gate_weight, up_weight)
+
+
+class PickWork:
+    GROUP = 4
+
+    def __init__(self, places, source, weight, rows_out, plain_out, scratch):
+        self.places, self.source, self.weight = places, source, weight
+        self.rows_out, self.plain_out = rows_out, plain_out
+        self.block, self.rows, self.plain, self.held, self.in_sems, self.out_sems, self.held_sem = scratch
+        self.pairs = source.shape[0]
+        self.units = self.pairs + self.GROUP
+        self.experts = weight.shape[0]
+        self.per = self.rows.shape[2] // self.GROUP
+
+    @staticmethod
+    def scratch(source, weight, per):
+        experts, hidden, width = weight.shape
+        group = PickWork.GROUP * per
+        return [
+            pltpu.VMEM((2,) + source.shape[1:], source.dtype),
+            pltpu.VMEM((2, experts, group, width), source.dtype),
+            pltpu.VMEM((2, experts, group, hidden), jnp.float32),
+            pltpu.VMEM(weight.shape, weight.dtype),
+            pltpu.SemaphoreType.DMA((2,)),
+            pltpu.SemaphoreType.DMA((2, 2)),
+            pltpu.SemaphoreType.DMA((1,)),
+        ]
+
+    def load(self, unit, slot):
+        return pltpu.make_async_copy(self.source.at[unit], self.block.at[slot], self.in_sems.at[slot])
+
+    def hold(self):
+        return pltpu.make_async_copy(self.weight, self.held, self.held_sem.at[0])
+
+    def stores(self, group, slot):
+        height = self.GROUP * self.per
+        at = pl.ds(pl.multiple_of(group * height, height), height)
+        return [
+            pltpu.make_async_copy(self.rows.at[slot], self.rows_out.at[:, at], self.out_sems.at[slot, 0]),
+            pltpu.make_async_copy(self.plain.at[slot], self.plain_out.at[:, at], self.out_sems.at[slot, 1]),
+        ]
+
+    def begin(self):
+        self.hold().start()
+        self.load(0, 0).start()
+
+    def pick(self, unit):
+        slot, group, turn = unit % 2, unit // self.GROUP, unit % self.GROUP
+        side = group % 2
+
+        @pl.when(unit + 1 < self.pairs)
+        def _():
+            self.load(unit + 1, 1 - slot).start()
+
+        @pl.when((turn == 0) & (group >= 2))
+        def _():
+            for copy in self.stores(group - 2, side):
+                copy.wait()
+
+        self.load(unit, slot).wait()
+        rows = inner(one_hot(self.places[unit], self.per), self.block[slot]).astype(self.rows.dtype)
+        for e in range(self.experts):
+            at = pl.ds(pl.multiple_of(turn * self.per, self.per), self.per)
+            self.rows[side, e, at] = rows[e * self.per : (e + 1) * self.per]
+
+    def multiply(self, unit):
+        group, e = unit // self.GROUP, unit % self.GROUP
+        side = group % 2
+
+        @pl.when(unit == 0)
+        def _():
+            self.hold().wait()
+
+        self.plain[side, e] = inner(self.rows[side, e], self.held[e], 1, 1)
+
+        @pl.when(e == self.GROUP - 1)
+        def _():
+            for copy in self.stores(group, side):
+                copy.start()
+
+    def run(self, unit):
+        pl.when(unit < self.pairs)(lambda: self.pick(unit))
+        pl.when(unit >= self.GROUP)(lambda: self.multiply(unit - self.GROUP))
+
+    def finish(self):
+        groups = self.pairs // self.GROUP
+        for group in (groups - 2, groups - 1):
+            for copy in self.stores(group, group % 2):
+                copy.wait()
+
+
+class OutputWork:
+    def __init__(self, places, hidden, weight, out, scratch):
+        self.places, self.hidden, self.weight, self.out = places, hidden, weight, out
+        self.rows, self.held, self.narrow, self.block, self.in_sems, self.out_sems = scratch
+        self.experts, self.slots, _ = hidden.shape
+        self.pairs = out.shape[0]
+        self.per = self.slots // self.pairs
+        self.width = weight.shape[2]
+        self.units = 2 * self.experts + self.pairs
+
+    @staticmethod
+    def scratch(hidden, weight, out):
+        experts, slots, narrow = hidden.shape
+        return [
+            pltpu.VMEM((experts, slots, weight.shape[2]), weight.dtype),
+            pltpu.VMEM((2,) + weight.shape[1:], weight.dtype),
+            pltpu.VMEM((2, slots, narrow), hidden.dtype),
+            pltpu.VMEM((2,) + out.shape[1:], out.dtype),
+            pltpu.SemaphoreType.DMA((2, 2)),
+            pltpu.SemaphoreType.DMA((2,)),
+        ]
+
+    def loads(self, e):
+        slot = e % 2
+        return [
+            pltpu.make_async_copy(self.weight.at[e], self.held.at[slot], self.in_sems.at[slot, 0]),
+            pltpu.make_async_copy(self.hidden.at[e], self.narrow.at[slot], self.in_sems.at[slot, 1]),
+        ]
+
+    def store(self, pair):
+        return pltpu.make_async_copy(self.block.at[pair % 2], self.out.at[pair], self.out_sems.at[pair % 2])
+
+    def begin(self):
+        for copy in self.loads(0):
+            copy.start()
+
+    def run(self, unit):
+        half = self.width // 2
+
+        @pl.when(unit < 2 * self.experts)
+        def _():
+            e, side = unit // 2, unit % 2
+
+            @pl.when(side == 0)
+            def _():
+                @pl.when(e + 1 < self.experts)
+                def _():
+                    for copy in self.loads(e + 1):
+                        copy.start()
+
+                for copy in self.loads(e):
+                    copy.wait()
+
+            at = pl.ds(pl.multiple_of(side * half, half), half)
+            self.rows[e, :, at] = inner(self.narrow[e % 2], self.held[e % 2, :, at]).astype(self.rows.dtype)
+
+        @pl.when(unit >= 2 * self.experts)
+        def _():
+            pair = unit - 2 * self.experts
+
+            @pl.when(pair >= 2)
+            def _():
+                self.store(pair - 2).wait()
+
+            at = pl.ds(pl.multiple_of(pair * self.per, self.per), self.per)
+            rows = jnp.concatenate([self.rows[e, at] for e in range(self.experts)], axis=0)
+            self.block[pair % 2] = inner(one_hot(self.places[pair], self.per), rows, 0, 0).astype(self.block.dtype)
+            self.store(pair).start()
+
+    def finish(self):
+        for pair in (self.pairs - 2, self.pairs - 1):
+            self.store(pair).wait()
+
+
+def expert_weight_grads(rows, grads, weighted, gate_back, up_back):
+    experts, slots, width = rows.shape
+    hidden = weighted.shape[2]
+    parts = 4
+    part = width // parts
+
+    def kernel(x, c, low, gate, up, gate_out, up_out, down_out):
+        gate_out[0] = inner(x[0], gate[0], 0, 0)
+        up_out[0] = inner(x[0], up[0], 0, 0)
+        down_out[0] = inner(low[0], c[0], 0, 0)
+
+    source = pl.BlockSpec((1, slots, part), lambda e, i: (e, 0, i))
+    whole = pl.BlockSpec((1, slots, hidden), lambda e, i: (e, 0, 0))
+    tall = pl.BlockSpec((1, part, hidden), lambda e, i: (e, i, 0))
+    flat = pl.BlockSpec((1, hidden, part), lambda e, i: (e, 0, i))
+    return pl.pallas_call(
+        kernel,
+        out_shape=[
+            jax.ShapeDtypeStruct((experts, width, hidden), jnp.float32),
+            jax.ShapeDtypeStruct((experts, width, hidden), jnp.float32),
+            jax.ShapeDtypeStruct((experts, hidden, width), jnp.float32),
+        ],
+        grid=(experts, parts),
+        in_specs=[source, source, whole, whole, whole],
+        out_specs=[tall, tall, flat],
+        compiler_params=local_params(),
+        cost_estimate=pl.CostEstimate(
+            flops=6 * experts * slots * width * hidden, bytes_accessed=24 * experts * width * hidden, transcendentals=0
+        ),
+        name="expert_weight_grads",
+    )(rows, grads, weighted, gate_back, up_back)
 
 
 class ColumnsFlow:
@@ -939,9 +1168,9 @@
 
 
 class SumsFlow:
-    SENDS = 8 + 8 + 1
+    SENDS = 8 + 24 + 1
     RECVS = 8 + 8 + 1
-    LOCALS = 10
+    LOCALS = 12
 
     def __init__(self, place, wide, tall, wide_out, tall_out, scratch):
         self.p = place
@@ -983,24 +1212,30 @@
             self.acc[which].at[k], self.side_in[which].at[k - 1], self.send.at[slot], self.recv.at[slot], self.p.at(k)
         )
 
-    def deal(self, step):
+    def deal(self, step, i):
         to = (self.p.col + step) % 8
-        src = self.acc[0].at[0, pl.ds(pl.multiple_of(to * self.rows, self.rows), self.rows)]
+        src, dst = self.piece(to, i)
         return remote(
-            src, self.outs[0].at[self.p.col], self.send.at[8 + step], self.recv.at[8 + self.p.col], (self.p.dp, to // 4, to % 4)
-        )
-
-    def keep(self):
-        src = self.acc[0].at[0, pl.ds(pl.multiple_of(self.p.col * self.rows, self.rows), self.rows)]
-        return pltpu.make_async_copy(src, self.outs[0].at[self.p.col], self.local.at[8])
+            src, dst, self.send.at[8 + 3 * step + i], self.recv.at[8 + self.p.col], (self.p.dp, to // 4, to % 4)
+        )
+
+    def piece(self, to, i):
+        share = self.outs[0].shape[2] // 8
+        rows = pl.ds(pl.multiple_of(to * self.rows, self.rows), self.rows)
+        dst = self.outs[0].at[i, :, pl.ds(pl.multiple_of(self.p.col * share, share), share)]
+        return self.acc[0].at[0, rows, pl.ds(i * share, share)], dst
+
+    def keep(self, i):
+        src, dst = self.piece(self.p.col, i)
+        return pltpu.make_async_copy(src, dst, self.local.at[8 + i])
 
     def swap(self):
         return remote(
-            self.acc[1].at[0], self.outs[1], self.send.at[16], self.recv.at[16], (self.p.col // 2, self.p.col % 2, self.p.dp)
+            self.acc[1].at[0], self.outs[1], self.send.at[32], self.recv.at[16], (self.p.col // 2, self.p.col % 2, self.p.dp)
         )
 
     def stay(self):
-        return pltpu.make_async_copy(self.acc[1].at[0], self.outs[1], self.local.at[9])
+        return pltpu.make_async_copy(self.acc[1].at[0], self.outs[1], self.local.at[11])
 
     def at_home(self):
         return (self.p.col // 2 == self.p.dp) & (self.p.col % 2 == self.p.blk) & (self.p.z == self.p.dp)
@@ -1043,9 +1278,11 @@
 
         @pl.loop(1, 8)
         def _(step):
-            self.deal(step).start()
-
-        self.keep().start()
+            for i in range(3):
+                self.deal(step, i).start()
+
+        for i in range(3):
+            self.keep(i).start()
 
     def finish(self):
         home = self.at_home()
@@ -1058,16 +1295,18 @@
         def _():
             self.swap().wait()
 
-        self.keep().wait()
+        for i in range(3):
+            self.keep(i).wait()
 
         @pl.loop(1, 8)
         def _(step):
             col = (self.p.col + step) % 8
-            landed = self.outs[0].at[col]
+            landed = self.acc[0].at[0, pl.ds(0, self.rows)]
             remote(
                 landed, landed, self.send.at[0], self.recv.at[8 + col], self.p.at(0, 1 - self.p.blk)
             ).wait_recv()
-            self.deal(step).wait_send()
+            for i in range(3):
+                self.deal(step, i).wait_send()
 
         for which in (1, 0):
             for k in (1, 2):
@@ -1123,12 +1362,16 @@
         return [self.begin] + [lambda: None] * (length - 2) + [self.finish]
 
 
-def hbm_call(kernel, shapes, scratch, name, collective_id, args, aliases=None):
+def hbm_call(kernel, shapes, scratch, name, collective_id, args, aliases=None, in_vmem=(), out_vmem=()):
     return pl.pallas_call(
         kernel,
         out_shape=shapes,
-        in_specs=[pl.BlockSpec(memory_space=pl.ANY)] * len(args),
-        out_specs=[pl.BlockSpec(memory_space=pl.ANY)] * len(shapes),
+        in_specs=[
+            pl.BlockSpec(memory_space=pltpu.VMEM if i in in_vmem else pl.ANY) for i in range(len(args))
+        ],
+        out_specs=[
+            pl.BlockSpec(memory_space=pltpu.VMEM if i in out_vmem else pl.ANY) for i in range(len(shapes))
+        ],
         scratch_shapes=scratch,
         input_output_aliases=aliases or {},
         compiler_params=pltpu.CompilerParams(
@@ -1202,79 +1445,312 @@
     )
 
 
-def attended_call(part, others, gathered):
-    line = ScatterFlow.scratch(part.shape[1], part.shape[2], part.dtype, False)
-
-    def kernel(part_ref, first, second, third, _, out, gathered_out, *scratch):
+def attention_call(tokens_all, gains, wide, tall, head_gains, cosine, sine, cotangent, gathered):
+    count, tok_rows, width = tokens_all.shape
+    rows = count * tok_rows
+    share = tall.shape[0]
+    heads = share // HEAD_DIM
+    block = 2 * tok_rows
+    blocks = rows // block
+    scale = 1.0 / math.sqrt(HEAD_DIM)
+    bf16, f32 = jnp.bfloat16, jnp.float32
+    line = ScatterFlow.scratch(tok_rows, width, bf16, False)
+
+    def kernel(tok, gain, wide_in, tall_in, head_gain, cos, sin, cot, _, *refs):
+        outs, scratch = refs[:8], refs[8:]
+        normed_out, unit_out, row_out, context_out, scale_out, log_out, attended, gathered_out = outs
+        held, wide_ref, tall_ref, normed, unit, qkv, context, part, sums, landed = scratch[:10]
+        ins, stores, send, recv = scratch[10:14]
         place = Place()
-        entry_barrier(place, "planes")
-        flow = ScatterFlow(place, part_ref, out, scratch[: len(line)], False)
-        blocks = [((place.z + 4 - j) % 4, src) for j, src in ((1, first), (2, second), (3, third))]
-        plane = PlaneFlow(place, blocks, gathered_out, *scratch[len(line) :])
+        entry_barrier(place, "all")
+        flow = ScatterFlow(place, part, attended, scratch[14 : 14 + len(line)], False)
+        others = GatherFlow(
+            place, cot, gathered_out, scratch[-2], scratch[-1], True, others=True
+        )
+
+        def block_in(i):
+            return pltpu.make_async_copy(tok.at[pl.ds(2 * i, 2)], held.at[i], ins.at[i])
+
+        weights = [
+            pltpu.make_async_copy(wide_in, wide_ref, ins.at[blocks]),
+            pltpu.make_async_copy(tall_in, tall_ref, ins.at[blocks + 1]),
+        ]
+        for i in range(blocks):
+            block_in(i).start()
+        for copy in weights:
+            copy.start()
+        for copy in weights:
+            copy.wait()
+        sums[...] = jnp.zeros_like(sums)
+
+        @pl.loop(0, blocks)
+        def _(i):
+            block_in(i).wait()
+            at = pl.ds(pl.multiple_of(i * block, block), block)
+            values = held[i].reshape(block, width).astype(f32)
+            mean = jnp.mean(values * values, axis=1, keepdims=True)
+            low = (values * lax.rsqrt(mean + NORM_EPSILON) * gain[...]).astype(bf16)
+            normed[at] = low
+            linear = inner(low, wide_ref[...])
+            unit[at] = linear[:, : 2 * share]
+            qkv[at, 2 * share :] = linear[:, 2 * share :].astype(bf16)
+            for n in range(2):
+                part_lin = linear[:, n * share : (n + 1) * share]
+                sums[n : n + 1, at] = jnp.sum(jnp.transpose(part_lin * part_lin), axis=0, keepdims=True)
+
+        def exchange(step):
+            to = (place.col + step) % 8
+            return remote(
+                sums, landed.at[place.col], send.at[step], recv.at[place.col], (place.dp, to // 4, to % 4)
+            )
+
+        @pl.loop(1, 8)
+        def _(step):
+            exchange(step).start()
+
+        landed[place.col] = sums[...]
+
+        @pl.loop(1, 8)
+        def _(step):
+            col = (place.col + step) % 8
+            remote(sums, landed.at[col], send.at[0], recv.at[col], place.at(0, 1 - place.blk)).wait_recv()
+            exchange(step).wait_send()
+
+        others.begin()
+        total = landed[0]
+        for col in range(1, 8):
+            total = total + landed[col]
+        scales = jnp.transpose(lax.rsqrt(total / width + NORM_EPSILON))
+        scale_out[...] = scales
+
+        @pl.loop(0, blocks)
+        def _(i):
+            at = pl.ds(pl.multiple_of(i * block, block), block)
+            for n in range(2):
+                for h in range(heads):
+                    lanes = pl.ds(n * share + h * HEAD_DIM, HEAD_DIM)
+                    mine = unit[at, lanes] * scale_out[at, n : n + 1]
+                    unit[at, lanes] = mine
+                    scaled = mine * head_gain[n : n + 1, h * HEAD_DIM : (h + 1) * HEAD_DIM]
+                    turned = scaled * cos[at] + pltpu.roll(scaled, HEAD_DIM // 2, 1) * sin[at]
+                    qkv[at, lanes] = turned.astype(bf16)
+
+        out_copies = [
+            pltpu.make_async_copy(src, dst, stores.at[n])
+            for n, (src, dst) in enumerate(((normed, normed_out), (unit, unit_out), (qkv, row_out)))
+        ]
+        for copy in out_copies:
+            copy.start()
+        for h in range(heads):
+            for i in range(blocks):
+                seen = (i + 1) * block
+                queries = qkv[i * block : seen, h * HEAD_DIM : (h + 1) * HEAD_DIM]
+                keys = qkv[:seen, share + h * HEAD_DIM : share + (h + 1) * HEAD_DIM]
+                values = qkv[:seen, 2 * share + h * HEAD_DIM : 2 * share + (h + 1) * HEAD_DIM]
+                scores = inner(queries, keys, 1, 1) * scale
+                row = lax.broadcasted_iota(jnp.int32, scores.shape, 0) + i * block
+                column = lax.broadcasted_iota(jnp.int32, scores.shape, 1)
+                scores = jnp.where(column <= row, scores, MASKED)
+                peak = jnp.max(scores, axis=1, keepdims=True)
+                exponent = jnp.exp(scores - peak)
+                sum_row = jnp.sum(exponent, axis=1, keepdims=True)
+                low = (exponent / sum_row).astype(bf16)
+                context[i * block : seen, h * HEAD_DIM : (h + 1) * HEAD_DIM] = inner(low, values).astype(bf16)
+                log_out[i * block : seen, h : h + 1] = peak + jnp.log(sum_row)
+            if h == 0:
+                others.along(1)
+
+        @pl.loop(0, blocks)
+        def _(i):
+            at = pl.ds(pl.multiple_of(i * block, block), block)
+            rows_here = inner(context[at], tall_ref[...]).astype(bf16)
+            part[pl.ds(2 * i, 2)] = rows_here.reshape(2, tok_rows, width)
+
+        last = pltpu.make_async_copy(context, context_out, stores.at[3])
+        last.start()
+        flow.begin()
+        others.along(2)
+        flow.stage3(0)
+        flow.stage3(1)
+        flow.chain(0)
+        others.along(3)
+        others.turn(1)
+        flow.stage3(2)
+        flow.chain(1)
+        flow.chain(2)
+        others.turn(2)
+        others.corner(1)
+        flow.stage3(3)
+        flow.final()
+        others.turn(3)
+        others.corner(2)
+        others.corner(3)
+        others.finish()
+        for copy in out_copies + [last]:
+            copy.wait()
+
+    shapes = [
+        jax.ShapeDtypeStruct((rows, width), bf16),
+        jax.ShapeDtypeStruct((rows, 2 * share), f32),
+        jax.ShapeDtypeStruct((rows, 3 * share), bf16),
+        jax.ShapeDtypeStruct((rows, share), bf16),
+        jax.ShapeDtypeStruct((rows, 8), f32),
+        jax.ShapeDtypeStruct((rows, 8), f32),
+        jax.ShapeDtypeStruct((tok_rows, width), f32),
+        jax.ShapeDtypeStruct(gathered.shape, gathered.dtype),
+    ]
+    scratch = [
+        pltpu.VMEM((blocks, 2, tok_rows, width), bf16),
+        pltpu.VMEM(wide.shape, bf16),
+        pltpu.VMEM(tall.shape, bf16),
+        pltpu.VMEM((rows, width), bf16),
+        pltpu.VMEM((rows, 2 * share), f32),
+        pltpu.VMEM((rows, 3 * share), bf16),
+        pltpu.VMEM((rows, share), bf16),
+        pltpu.VMEM((8, tok_rows, width), bf16),
+        pltpu.VMEM((8, rows), f32),
+        pltpu.VMEM((8, 8, rows), f32),
+        pltpu.SemaphoreType.DMA((blocks + 2,)),
+        pltpu.SemaphoreType.DMA((4,)),
+        pltpu.SemaphoreType.DMA((8,)),
+        pltpu.SemaphoreType.DMA((8,)),
+    ]
+    args = (tokens_all, gains, wide, tall, head_gains, cosine, sine, cotangent, gathered)
+    return hbm_call(
+        kernel, shapes, scratch + line + gather_sems(), "attention", 5, args, {8: 7}, (1, 4, 5, 6), (4, 5)
+    )
+
+
+def closing_call(normed_part, wide, tall, out_part):
+    height = out_part.shape[1] // 2
+    line = ScatterFlow.scratch(normed_part.shape[1], normed_part.shape[2], normed_part.dtype, False)
+    half = ScatterFlow.scratch(height, out_part.shape[2], out_part.dtype, True)
+    sums = SumsFlow.scratch(wide, tall)
+    rows = tall.shape[1]
+
+    def kernel(part, wide_in, tall_in, mixed_in, out, wide_out, tall_out, mixed, *scratch):
+        place = Place()
+        entry_barrier(place, "all")
+        first, second = len(line), len(line) + len(half)
+        weights = SumsFlow(place, wide_in, tall_in, wide_out, tall_out, scratch[second:])
+        flow = ScatterFlow(place, part, out, scratch[:first], False)
+        plane = ScatterFlow(place, mixed_in, mixed, scratch[first:second], True, (height, height))
+        weights.begin()
         flow.begin()
         plane.begin()
         flow.stage3(0)
         flow.stage3(1)
+        weights.sides()
+        plane.stage1(0)
+        plane.stage1(1)
         flow.chain(0)
-        plane.turns()
         flow.stage3(2)
+        plane.stage1(2)
+        plane.stage1(3)
+        weights.total()
         flow.chain(1)
         flow.chain(2)
+        plane.stage2(0)
+        plane.stage2(1)
         flow.stage3(3)
+        plane.stage2(2)
+        plane.stage2(3)
         flow.final()
-        plane.corners()
-        plane.finish()
+        for i in range(4):
+            plane.stage3(i)
+        weights.finish()
+        plane.settle_plane()
+
+    shapes = [
+        jax.ShapeDtypeStruct(normed_part.shape[1:], jnp.float32),
+        jax.ShapeDtypeStruct((3, rows, 8 * wide.shape[2] // 3), wide.dtype),
+        jax.ShapeDtypeStruct((rows, tall.shape[2]), tall.dtype),
+        jax.ShapeDtypeStruct((4, height, out_part.shape[2]), out_part.dtype),
+    ]
+    return hbm_call(kernel, shapes, line + half + sums, "closing", 2, (normed_part, wide, tall, out_part))
+
+
+def run_beside(steps, work):
+    steps[0]()
+    work.begin()
+
+    @pl.loop(0, work.units)
+    def _(unit):
+        for i, step in enumerate(steps[1:-1]):
+            pl.when(unit == i)(step)
+        work.run(unit)
+
+    steps[-1]()
+    work.finish()
+
+
+def features_call(features, probs, places, cotangent_all, down_weight, per):
+    experts, hidden, width = down_weight.shape
+    slots = places.shape[0] * per
+
+    def kernel(feature_ref, prob_ref, place_ref, cot, weight, feature_out, prob_out, rows, plain, *scratch):
+        place = Place()
+        entry_barrier(place, "planes")
+        small = GatherFlow(place, prob_ref, prob_out, scratch[2], scratch[3], True)
+        flow = GatherFlow(place, feature_ref, feature_out, scratch[0], scratch[1], True)
+        work = PickWork(place_ref, cot, weight, rows, plain, scratch[4:])
+
+        def both(i):
+            def act():
+                small.steps()[i]()
+                flow.steps()[i]()
+
+            return act
+
+        run_beside([both(i) for i in range(len(flow.steps()))], work)
+
+    shapes = [
+        jax.ShapeDtypeStruct((32,) + features.shape, features.dtype),
+        jax.ShapeDtypeStruct((32,) + probs.shape, probs.dtype),
+        jax.ShapeDtypeStruct((experts, slots, width), features.dtype),
+        jax.ShapeDtypeStruct((experts, slots, hidden), jnp.float32),
+    ]
+    scratch = gather_sems() * 2 + PickWork.scratch(cotangent_all, down_weight, per)
+    return hbm_call(
+        kernel, shapes, scratch, "features", 6, (features, probs, places, cotangent_all, down_weight), None, (2,)
+    )
+
+
+def experts_back_call(part, dealt, places, hidden, weight):
+    sums = ScatterFlow.scratch(part.shape[1], part.shape[2], part.dtype, True)
+    out_shape = jax.ShapeDtypeStruct((places.shape[0], places.shape[2], part.shape[2]), part.dtype)
+
+    def kernel(part_ref, dealt_ref, place_ref, hidden_ref, weight_ref, out, dealt_out, mixed, *scratch):
+        place = Place()
+        entry_barrier(place, "all")
+        deal = DealFlow(place, dealt_ref, dealt_out, *scratch[:3])
+        flow = ScatterFlow(place, part_ref, out, scratch[3 : 3 + len(sums)], True)
+        work = OutputWork(place_ref, hidden_ref, weight_ref, mixed, scratch[3 + len(sums) :])
+        deal.begin()
+        run_beside(flow.steps(), work)
+        deal.finish()
 
     shapes = [
         jax.ShapeDtypeStruct(part.shape[1:], jnp.float32),
-        jax.ShapeDtypeStruct(gathered.shape, gathered.dtype),
+        jax.ShapeDtypeStruct(dealt.shape, dealt.dtype),
+        out_shape,
     ]
+    scratch = DealFlow.scratch() + sums + OutputWork.scratch(hidden, weight, out_shape)
     return hbm_call(
-        kernel, shapes, line + plane_sems(3), "attended", 5, (part,) + tuple(others) + (gathered,), {4: 1}
-    )
-
-
-def closing_call(normed_part, wide, tall):
-    line = ScatterFlow.scratch(normed_part.shape[1], normed_part.shape[2], normed_part.dtype, False)
-    sums = SumsFlow.scratch(wide, tall)
-    rows = tall.shape[1]
-
-    def kernel(part, wide_in, tall_in, out, wide_out, tall_out, *scratch):
-        place = Place()
-        entry_barrier(place, "all")
-        weights = SumsFlow(place, wide_in, tall_in, wide_out, tall_out, scratch[len(line) :])
-        flow = ScatterFlow(place, part, out, scratch[: len(line)], False)
-        weights.begin()
-        flow.begin()
-        flow.stage3(0)
-        flow.stage3(1)
-        weights.sides()
-        flow.chain(0)
-        flow.stage3(2)
-        flow.chain(1)
-        flow.chain(2)
-        flow.stage3(3)
-        weights.total()
-        flow.final()
-        weights.finish()
-
-    shapes = [
-        jax.ShapeDtypeStruct(normed_part.shape[1:], jnp.float32),
-        jax.ShapeDtypeStruct((8, rows, wide.shape[2]), wide.dtype),
-        jax.ShapeDtypeStruct((rows, tall.shape[2]), tall.dtype),
-    ]
-    return hbm_call(kernel, shapes, line + sums, "closing", 2, (normed_part, wide, tall))
+        kernel, shapes, scratch, "experts_back", 3, (part, dealt, places, hidden, weight), None, (2,)
+    )
 
 
 def residual_grad_call(grad, logit_grad, out_part):
-    sums = ScatterFlow.scratch(out_part.shape[1], out_part.shape[2], out_part.dtype, True)
+    height = out_part.shape[1] // 2
+    sums = ScatterFlow.scratch(height, out_part.shape[2], out_part.dtype, True)
 
     def kernel(grad_ref, logit_ref, part_ref, grad_out, logit_out, out, *scratch):
         place = Place()
         entry_barrier(place, "planes")
         line = GatherFlow(place, grad_ref, grad_out, scratch[0], scratch[1], False)
         logits = GatherFlow(place, logit_ref, logit_out, scratch[2], scratch[3], True)
-        flow = ScatterFlow(place, part_ref, out, scratch[4:], True, True)
+        flow = ScatterFlow(place, part_ref, out, scratch[4:], True, (0, height))
         line.begin()
         logits.begin()
         flow.begin()
@@ -1283,23 +1759,23 @@
         line.along(1)
         logits.along(1)
         logits.turn(0)
+        flow.stage1(2)
+        flow.stage1(3)
         flow.stage2(0)
-        flow.stage1(2)
         line.along(2)
         logits.along(2)
         logits.turn(1)
-        flow.stage1(3)
         flow.stage2(1)
-        flow.stage3(0)
+        flow.stage2(2)
         line.along(3)
         logits.along(3)
         logits.turn(2)
         logits.turn(3)
-        flow.stage2(2)
+        flow.stage3(0)
+        flow.stage2(3)
         flow.stage3(1)
         for d in range(4):
             logits.corner(d)
-        flow.stage2(3)
         flow.stage3(2)
         line.finish()
         logits.finish()
@@ -1309,124 +1785,9 @@
     shapes = [
         jax.ShapeDtypeStruct((8,) + grad.shape, grad.dtype),
         jax.ShapeDtypeStruct((32,) + logit_grad.shape, logit_grad.dtype),
-        jax.ShapeDtypeStruct((4,) + out_part.shape[1:], out_part.dtype),
+        jax.ShapeDtypeStruct((4, height, out_part.shape[2]), out_part.dtype),
     ]
     return hbm_call(kernel, shapes, gather_sems() * 2 + sums, "residual_grad", 7, (grad, logit_grad, out_part))
-
-
-class WeightGrads:
-    PARTS = 4
-
-    @staticmethod
-    def scratch(rows, hidden):
-        slots, part = rows.shape[1], rows.shape[2] // WeightGrads.PARTS
-        return [
-            pltpu.VMEM((2, 2, slots, part), rows.dtype),
-            pltpu.VMEM((2, 3, slots, hidden), rows.dtype),
-            pltpu.VMEM((2, 2, part, hidden), jnp.float32),
-            pltpu.VMEM((2, hidden, part), jnp.float32),
-            pltpu.SemaphoreType.DMA((2, 5)),
-            pltpu.SemaphoreType.DMA((2, 3)),
-        ]
-
-    def __init__(self, ins, outs, scratch):
-        self.ins, self.outs = ins, outs
-        self.wide, self.narrow, self.tall, self.flat, self.in_sems, self.out_sems = scratch
-        self.part = self.wide.shape[3]
-        self.units = ins[0].shape[0] * self.PARTS
-
-    def columns(self, unit):
-        return pl.ds(pl.multiple_of((unit % self.PARTS) * self.part, self.part), self.part)
-
-    def loads(self, unit, slot):
-        e = unit // self.PARTS
-        copies = []
-        for i in range(2):
-            copies.append((self.ins[i].at[e, :, self.columns(unit)], self.wide.at[slot, i]))
-        for i in range(3):
-            copies.append((self.ins[2 + i].at[e], self.narrow.at[slot, i]))
-        return [pltpu.make_async_copy(s, d, self.in_sems.at[slot, n]) for n, (s, d) in enumerate(copies)]
-
-    def stores(self, unit, slot):
-        e, columns = unit // self.PARTS, self.columns(unit)
-        copies = [
-            (self.tall.at[slot, 0], self.outs[0].at[e, columns]),
-            (self.tall.at[slot, 1], self.outs[1].at[e, columns]),
-            (self.flat.at[slot], self.outs[2].at[e, :, columns]),
-        ]
-        return [pltpu.make_async_copy(s, d, self.out_sems.at[slot, n]) for n, (s, d) in enumerate(copies)]
-
-    def begin(self):
-        for copy in self.loads(0, 0):
-            copy.start()
-
-    def run(self, unit):
-        slot = unit % 2
-
-        @pl.when(unit + 1 < self.units)
-        def _():
-            for copy in self.loads(unit + 1, 1 - slot):
-                copy.start()
-
-        for copy in self.loads(unit, slot):
-            copy.wait()
-
-        @pl.when(unit >= 2)
-        def _():
-            for copy in self.stores(unit - 2, slot):
-                copy.wait()
-
-        rows, grads = self.wide[slot, 0], self.wide[slot, 1]
-        self.tall[slot, 0] = inner(rows, self.narrow[slot, 1], 0, 0)
-        self.tall[slot, 1] = inner(rows, self.narrow[slot, 2], 0, 0)
-        self.flat[slot] = inner(self.narrow[slot, 0], grads, 0, 0)
-        for copy in self.stores(unit, slot):
-            copy.start()
-
-    def finish(self):
-        for unit in (self.units - 2, self.units - 1):
-            for copy in self.stores(unit, unit % 2):
-                copy.wait()
-
-
-def experts_back_call(part, dealt, rows, grads, weighted, gate_back, up_back):
-    sums = ScatterFlow.scratch(part.shape[1], part.shape[2], part.dtype, True)
-    experts, _, width = rows.shape
-    hidden = weighted.shape[2]
-
-    def kernel(part_ref, dealt_ref, *refs):
-        ins, (out, dealt_out), outs, scratch = refs[:5], refs[5:7], refs[7:10], refs[10:]
-        place = Place()
-        entry_barrier(place, "all")
-        deal = DealFlow(place, dealt_ref, dealt_out, *scratch[:3])
-        flow = ScatterFlow(place, part_ref, out, scratch[3 : 3 + len(sums)], True)
-        grads_here = WeightGrads(ins, outs, scratch[3 + len(sums) :])
-        deal.begin()
-        steps = flow.steps()
-        steps[0]()
-        grads_here.begin()
-
-        @pl.loop(0, grads_here.units)
-        def _(unit):
-            for i, step in enumerate(steps[1:-1]):
-                pl.when(unit == i)(step)
-            grads_here.run(unit)
-
-        steps[-1]()
-        grads_here.finish()
-        deal.finish()
-
-    shapes = [
-        jax.ShapeDtypeStruct(part.shape[1:], jnp.float32),
-        jax.ShapeDtypeStruct(dealt.shape, dealt.dtype),
-        jax.ShapeDtypeStruct((experts, width, hidden), jnp.float32),
-        jax.ShapeDtypeStruct((experts, width, hidden), jnp.float32),
-        jax.ShapeDtypeStruct((experts, hidden, width), jnp.float32),
-    ]
-    scratch = DealFlow.scratch() + sums + WeightGrads.scratch(rows, hidden)
-    return hbm_call(
-        kernel, shapes, scratch, "experts_back", 3, (part, dealt, rows, grads, weighted, gate_back, up_back)
-    )
 
 
 def column_sum(values, name, collective_id):
@@ -1560,37 +1921,30 @@
     gain_share = lax.dynamic_slice_in_dim(gain_all, column * share, share, axis=0)
     gain_query, gain_key = gain_share[:, 1], gain_share[:, 2]
 
-    sequence = tokens_all.reshape(seq_rows, model_width).astype(f32)
-    normed_all = norm_apply(sequence, gain_attention).astype(bf16)
-    linear = jnp.dot(normed_all, wide_weight, preferred_element_type=f32)
-    query_lin, key_lin = linear[:, :share], linear[:, share : 2 * share]
-    values = linear[:, 2 * share :].astype(bf16)
-    squares = jnp.stack([jnp.sum(query_lin * query_lin, axis=1), jnp.sum(key_lin * key_lin, axis=1)])
-    squares = column_sum(squares.reshape(16, seq_rows // 8), "square_sums", 4).reshape(2, seq_rows)
-    own_cotangent, squares = lax.optimization_barrier((cotangent, squares))
-    cotangent_others = [shift_line(own_cotangent, j) for j in (1, 2, 3)]
-    scales = lax.rsqrt(squares / model_width + NORM_EPSILON)
-    query_r, key_r = scales[0][:, None], scales[1][:, None]
-    cosine, sine = rope_tables(jnp.arange(seq_rows, dtype=jnp.int32), HEAD_DIM)
-    query_u, key_u = query_lin * query_r, key_lin * key_r
-    queries = rotate_heads(query_u * gain_query, cosine, sine).astype(bf16)
-    keys = rotate_heads(key_u * gain_key, cosine, sine).astype(bf16)
+    half_cos, half_sin = rope_tables(jnp.arange(seq_rows, dtype=jnp.int32), HEAD_DIM)
+    cosine = jnp.concatenate([half_cos, half_cos], axis=1)
+    sine = jnp.concatenate([-half_sin, half_sin], axis=1)
+    head_gains = gain_share[:, 1:3].T
+    normed_all, unit_rows, head_rows, context, scales, logs, attended, cotangent_all = attention_call(
+        tokens_all,
+        gain_attention[None],
+        wide_weight,
+        tall_weight,
+        head_gains,
+        cosine,
+        sine,
+        cotangent,
+        cotangent_all,
+    )
+    query_u, key_u = unit_rows[:, :share], unit_rows[:, share:]
+    queries, keys, values = head_rows[:, :share], head_rows[:, share : 2 * share], head_rows[:, 2 * share :]
+    query_r, key_r = scales[:, :1], scales[:, 1:2]
 
     def split(rows):
         return rows.reshape(seq_rows, heads_here, HEAD_DIM)
 
-    scores = product(split(queries), split(keys), ((2,), (2,)), HEAD_BATCH)
-    places = jnp.arange(seq_rows, dtype=jnp.int32)
-    causal = places[None, :] <= places[:, None]
-    scores = jnp.where(causal[None], scores * score_scale, MASKED)
-    attn_weights = jax.nn.softmax(scores, axis=-1)
-    attn_low = attn_weights.astype(bf16)
-    context = product(attn_low, split(values), ((2,), (0,)), ((0,), (1,))).transpose(1, 0, 2)
-    context = context.astype(bf16).reshape(seq_rows, share)
-    attended_part = jnp.dot(context, tall_weight, preferred_element_type=f32).astype(bf16)
-    attended, cotangent_all = attended_call(
-        attended_part.reshape(column_size, tok_rows, model_width), cotangent_others, cotangent_all
-    )
+    places_row = jnp.arange(seq_rows, dtype=jnp.int32)
+    causal = places_row[None, :] <= places_row[:, None]
 
     tokens_f = tokens.astype(f32)
     residual = tokens_f + attended
@@ -1598,50 +1952,33 @@
     features = features_f.astype(bf16)
     logits = jnp.dot(features, router_full, preferred_element_type=f32)
     router_probs = jax.nn.softmax(logits, axis=-1)
-    features_all, probs_all = gather_call(
-        [features, router_probs.reshape(tok_rows // 2, 2 * EXPERTS)], [True, True], "features_gather", 6
-    )
 
     first_expert = (lax.axis_index(DP) * 4 + lax.axis_index(SP)) * experts_here
     expert_ids = first_expert + jnp.arange(experts_here, dtype=jnp.int32)
     named = jnp.any(routes_all[:, None] == expert_ids[None, :, None, None], axis=3)
-    named_low = named.astype(bf16)
     earlier = (jnp.arange(tok_rows)[:, None] < jnp.arange(tok_rows)[None, :]).astype(bf16)
-    rank = product(named_low, earlier, ((2,), (0,))).astype(jnp.int32)
-    slot = jnp.arange(CAP, dtype=jnp.int32)
-    hot = (named[:, :, None, :] & (rank[:, :, None, :] == slot[None, None, :, None])).astype(bf16)
-    pairs = devices // 2
-    hot = hot.reshape(pairs, 2, experts_here, CAP, tok_rows)
-    zero = jnp.zeros_like(hot[:, 0])
-    picks = jnp.concatenate(
-        [jnp.concatenate([hot[:, 0], zero], axis=3), jnp.concatenate([zero, hot[:, 1]], axis=3)], axis=2
-    )
-    pair_rows = 2 * tok_rows
-    slots = devices * CAP
-    pick_matrix = picks.reshape(pairs, experts_here * 2 * CAP, pair_rows)
+    rank = product(named.astype(bf16), earlier, ((2,), (0,))).astype(jnp.int32)
+    pairs, pair_rows, per = devices // 2, 2 * tok_rows, 2 * CAP
+    places = jnp.where(named, rank, -per).reshape(pairs, 2, experts_here, tok_rows)
+    places = places + CAP * jnp.arange(2, dtype=jnp.int32)[None, :, None, None]
+    places = places.transpose(0, 2, 1, 3).reshape(pairs, experts_here, pair_rows)
+    cotangent_all = cotangent_all.reshape(pairs, pair_rows, model_width)
+    features_all, probs_all, grad_rows, plain_grads = features_call(
+        features, router_probs.reshape(tok_rows // 2, 2 * EXPERTS), places, cotangent_all, down_weight, per
+    )
+    probs_all = probs_all.reshape(pairs, pair_rows, EXPERTS)
+    probs_here = lax.dynamic_slice_in_dim(probs_all, first_expert, experts_here, axis=2).transpose(0, 2, 1)
     features_all = features_all.reshape(pairs, pair_rows, model_width)
-    cotangent_all = cotangent_all.reshape(pairs, pair_rows, model_width)
-    expert_rows, grad_rows = pick_rows(pick_matrix, features_all, cotangent_all, experts_here)
-    probs_all = probs_all.reshape(pairs, pair_rows, EXPERTS)
-    probs_here = lax.dynamic_slice_in_dim(probs_all, first_expert, experts_here, axis=2)
-    slot_probs = jnp.sum(picks.astype(f32) * probs_here.transpose(0, 2, 1)[:, :, None, :], axis=3)
-    slot_probs = slot_probs.transpose(1, 0, 2).reshape(experts_here, slots)[:, :, None]
-    weighted_hidden, gate_grad, up_grad, out_rows, input_rows, slot_grad = run_experts(
-        expert_rows, grad_rows, slot_probs, gate_weight, up_weight, down_weight
-    )
-    token_grad = jnp.sum(
-        picks.astype(f32) * slot_grad.reshape(experts_here, pairs, 2 * CAP).transpose(1, 0, 2)[:, :, :, None],
-        axis=2,
-    )
-    token_grad = token_grad.reshape(pairs, experts_here, 2, tok_rows).transpose(0, 2, 1, 3)
-    token_grad = token_grad.reshape(devices, experts_here, tok_rows)
-    token_grad = jnp.pad(token_grad, ((0, 0), (0, 8 - experts_here), (0, 0)))
-    out_part, input_part = put_rows_back(pick_matrix.transpose(0, 2, 1), out_rows, input_rows)
+    expert_rows, row_probs = pick_rows(places, probs_here, features_all, per)
+    weighted_hidden, gate_grad, up_grad, input_rows, row_grads = run_experts(
+        expert_rows, plain_grads, row_probs, gate_weight, up_weight
+    )
+    input_part, token_grad = put_rows_back(places, input_rows, row_grads)
+    input_part = input_part.reshape(devices, tok_rows, model_width)
+    input_grad, prob_parts, out_part = experts_back_call(
+        input_part, token_grad, places, weighted_hidden, down_weight
+    )
     out_part = out_part.reshape(devices, tok_rows, model_width)
-    input_part = input_part.reshape(devices, tok_rows, model_width)
-    input_grad, prob_parts, gate_grad_local, up_grad_local, down_grad_local = experts_back_call(
-        input_part, token_grad, expert_rows, grad_rows, weighted_hidden, gate_grad, up_grad
-    )
 
     prob_parts = prob_parts.reshape(4, 2, 4, 8, tok_rows)[:, :, :, :experts_here]
     prob_grad = jnp.sum(prob_parts, axis=1).reshape(EXPERTS, tok_rows).T
@@ -1652,15 +1989,18 @@
     residual_part, feature_gain_grad = feature_pull(feature_grad)
     residual_grad = cotangent.astype(f32) + residual_part
     attended_grad = residual_grad.astype(bf16)
-    grads_all, logit_all, out_sums = residual_grad_call(
+    grads_all, logit_all, first_sums = residual_grad_call(
         attended_grad, logit_grad.reshape(tok_rows // 2, 2 * EXPERTS), out_part
     )
-    mixture = jnp.zeros((tok_rows, model_width), f32)
-    for j in range(4):
-        there = (lax.axis_index(SP) + j) % 4
-        block = lax.dynamic_index_in_dim(out_sums, there, axis=0, keepdims=False)
-        mixture = mixture + (block if j == 0 else shift_line(block, j)).astype(f32)
-    block_output = (residual + mixture).astype(bf16)
+
+    def along_line(sums):
+        total = lax.dynamic_index_in_dim(sums, lax.axis_index(SP), axis=0, keepdims=False).astype(f32)
+        for j in (1, 2, 3):
+            block = lax.dynamic_index_in_dim(sums, (lax.axis_index(SP) + j) % 4, axis=0, keepdims=False)
+            total = total + shift_line(block, j).astype(f32)
+        return total
+
+    first_half = along_line(first_sums)
     own_index = (lax.axis_index(DP) * 2 + lax.axis_index(BLK)) * 4 + lax.axis_index(SP)
     own_features = lax.dynamic_slice_in_dim(
         features_all.reshape(devices * tok_rows, model_width), own_index * own_rows, own_rows, axis=1
@@ -1670,6 +2010,9 @@
     grads_all = grads_all.reshape(seq_rows, model_width)
     tall_grad = product(context, grads_all, ((0,), (0,))).astype(bf16)
     context_grad = product(grads_all, tall_weight, ((1,), (1,))).astype(bf16)
+    scores = product(split(queries), split(keys), ((2,), (2,)), HEAD_BATCH) * score_scale
+    attn_weights = jnp.where(causal[None], jnp.exp(scores - logs[:, :heads_here].T[:, :, None]), 0.0)
+    attn_low = attn_weights.astype(bf16)
     prob_dots = product(split(context_grad), split(values), ((2,), (2,)), HEAD_BATCH)
     row_delta = jnp.sum(attn_weights * prob_dots, axis=-1, keepdims=True)
     score_grad = (attn_weights * (prob_dots - row_delta)).astype(bf16)
@@ -1680,31 +2023,29 @@
 
     def unrotate(grad):
         grad = grad.astype(bf16).astype(f32).reshape(seq_rows, share)
-        return rotate_heads(grad, cosine, -sine)
+        return rotate_heads(grad, half_cos, -half_sin)
 
     query_back, key_back = unrotate(query_back), unrotate(key_back)
     query_gain_grad = jnp.sum(query_back * query_u, axis=0)
     key_gain_grad = jnp.sum(key_back * key_u, axis=0)
     query_w, key_w = query_back * gain_query, key_back * gain_key
     dots = jnp.stack([jnp.sum(query_w * query_u, axis=1), jnp.sum(key_w * key_u, axis=1)])
+    dots, first_half = lax.optimization_barrier((dots, first_half))
     dots = column_sum(dots.reshape(16, seq_rows // 8), "dot_sums", 8).reshape(2, seq_rows) / model_width
     query_low = (query_r * (query_w - query_u * dots[0][:, None])).astype(bf16)
     key_low = (key_r * (key_w - key_u * dots[1][:, None])).astype(bf16)
     linear_grad = jnp.concatenate([query_low, key_low, value_low], axis=1)
     wide_grad = product(normed_all, linear_grad, ((0,), (0,))).astype(bf16)
     normed_part = product(linear_grad, wide_weight, ((1,), (1,))).astype(bf16)
-    normed_part, mixture = lax.optimization_barrier((normed_part, mixture))
-    normed_grad, wide_back, tall_back = closing_call(
+    normed_grad, wide_back, tall_back, second_sums = closing_call(
         normed_part.reshape(column_size, tok_rows, model_width),
         wide_grad.reshape(4, model_width // 4, 3 * share),
         tall_grad.reshape(4, share // 4, model_width),
+        out_part,
     )
     _, attention_pull = jax.vjp(norm_apply, tokens_f, gain_attention)
     tokens_part, attention_gain_grad = attention_pull(normed_grad)
     input_gradient = residual_grad + tokens_part
-    wide_back = wide_back.reshape(column_size, own_rows, 3, share).transpose(2, 1, 0, 3)
-    wide_back = wide_back.reshape(3, own_rows, model_width).astype(f32)
-
     def spread(share_grad):
         placed = jnp.zeros((model_width,), f32)
         return lax.dynamic_update_slice(placed, share_grad, (column * share,))
@@ -1715,12 +2056,18 @@
     gain_grads = gain_grads.reshape(4, devices, own_rows).transpose(1, 0, 2)
     gain_grads = jnp.pad(gain_grads, ((0, 0), (0, 4), (0, 128 - own_rows)))
     gain_sums = deal_sum(gain_grads, 9)
+    second_sums, gain_sums, weighted_hidden = lax.optimization_barrier((second_sums, gain_sums, weighted_hidden))
+    mixture = jnp.concatenate([first_half, along_line(second_sums)], axis=0)
+    block_output = (residual + mixture).astype(bf16)
+    gate_grad_local, up_grad_local, down_grad_local = expert_weight_grads(
+        expert_rows, grad_rows, weighted_hidden, gate_grad, up_grad
+    )
     return (
         block_output,
         input_gradient,
-        wide_back[0],
-        wide_back[1],
-        wide_back[2],
+        wide_back[0].astype(f32),
+        wide_back[1].astype(f32),
+        wide_back[2].astype(f32),
         tall_back.astype(f32),
         router_grad,
         gain_sums[0, :own_rows],

time: 830 us -> 739 us (0.89)
  local copies, waits for them, and re-layouts: 84.4 us -> 40.7 us
  waiting for transfers between devices: 24.8 us -> 0.02 us
  matrix products: 53.2 us -> 35.9 us
  other arithmetic: 44.5 us -> 31.4 us
    pallas_call x5 -> x6, Pallas kernels: 396 us -> 491 us  [hbm_call(): pl.pallas_call(kernel, out_shape=shapes, in_specs=[pl.BlockSpec(memory_sp...]
    pallas_call x4, Pallas kernels: 185 us -> 99.4 us  [the longest x1 35.6 us: expert_weight_grads(): pl.pallas_call(kernel, out_shape=[jax.ShapeDtypeStruct((experts, width, h...]
    unnamed x141 -> x63, local copies, waits for them, and re-layouts: 42.6 us -> 4.82 us
    ppermute x6, waiting for transfers between devices: 24.8 us -> 0.02 us  [shift_line(): return lax.ppermute(rows, SP, [(i, (i + step) % size) for i in range(size)])]
    sub x1 -> x0, matrix products: 8.81 us -> none  [body_fast(): attn_weights = jax.nn.softmax(scores, axis=-1)]
  transfers between devices with their start and end apart: 6 -> 6, of which waited for: 2 -> 0; matrix products, arithmetic and copies ran while one was open for 6% -> 7% of each run, Pallas kernels for 0% -> 5%
where the time goes in v2:
time: 739 us; the launch traced here: 729 us
  Pallas kernels  611 us (83%)
  local copies, waits for them, and re-layouts  40.7 us (6%)
  matrix products  35.9 us (5%)
  other arithmetic  31.4 us (4%)
  starting transfers between devices  8.56 us (1%)
    pallas_call x6, Pallas kernels, hbm_call(): pl.pallas_call(kernel, out_shape=shapes, in_specs=[pl.BlockSpec(memory_sp...  491 us
    pallas_call x1, Pallas kernels, expert_weight_grads(): pl.pallas_call(kernel, out_shape=[jax.ShapeDtypeStruct((experts, width, h...  35.6 us
    pallas_call x1, Pallas kernels, run_experts(): pl.pallas_call(kernel, out_shape=[narrow, narrow, narrow, jax.ShapeDtypeS...  34.4 us
    dot_general x11, matrix products, product(): lax.dot_general(left, right, (sums, batches), preferred_element_type=out)  33.8 us
    pallas_call x1, Pallas kernels, put_rows_back(): pl.pallas_call(kernel, out_shape=[jax.ShapeDtypeStruct((pairs, pair_rows,...  14.8 us
  transfers between devices with their start and end apart: 6, of which 0 were waited for; matrix products, arithmetic and copies ran while one was open for 7% of the time, Pallas kernels for 5%

profile of v2, /device:TPU:0, one launch (start us, length us, event | category | flops | bytes accessed | tf_op | source)
XLA Modules:
  0.0 729.2 jit_solution(6835630219856016460)
XLA Ops:
  6.1 80.1 %opening.1 = (bf16[8,128,2048]{2,1,0:T(8,128)(2,1)}, bf16[32,64,128]{2,1,0:T(8,128)(2,1)}, bf16[32,128,2048]{2,1,0:T(8,128)(2,1)}, bf16[2048,768]{1,0:T(8,128)(2,1)}, bf16[256,2048]{1,0:T(8,128)(2,1)}) custom-call(bf16[128,2048]{1,0:T(8,128)(2,1)} %tok.1, bf16[64,128]{1,0:T(8,128)(2,1)} %concatenate.22.sml, bf16[128,2048]{1,0:T(8,128)(2,1)} %cot.3, ...), custom_call_target="tpu_custom_call" | custom-call | tf_op jit(solution)/shard_map/opening/pallas_call | solution.py:1366
  93.5 95.5 %attention.1 = (bf16[1024,2048]{1,0:T(8,128)(2,1)}, f32[1024,512]{1,0:T(8,128)}, bf16[1024,768]{1,0:T(8,128)(2,1)}, bf16[1024,256]{1,0:T(8,128)(2,1)}, f32[1024,...) custom-call(bf16[8,128,2048]{2,1,0:T(8,128)(2,1)} %get-tuple-element, ...), custom_call_target="tpu_custom_call", output_to_operand_aliasing={{7}: (8, {})} | custom-call | tf_op jit(solution)/shard_map/attention/pallas_call | solution.py:1366
  194.1 92.8 %features.1 = (bf16[32,128,2048]{2,1,0:T(8,128)(2,1)}, f32[32,64,128]{2,1,0:T(8,128)}, bf16[4,768,2048]{2,1,0:T(8,128)(2,1)}, f32[4,768,512]{2,1,0:T(8,128)}) custom-call(bf16[128,2048]{1,0:T(8,128)(2,1)} %copy-done.13, f32[64,128]{1,0:T(8,128)} %reshape.271.prob_ref, s32[16,4,256]{2,1,0:T(4,128)} %reshape.270.place_ref, bf16[16,256,2048]{2,1,0:T(8,128)(2,1)} %bitcast.117, ...), custom_call_target="tpu_custom_call" | custom-call | tf_op jit(solution)/shard_map/features/pallas_call | solution.py:1366
  290.4 2.8 copy.179
  293.3 14.6 %pick_rows.1 = (bf16[4,768,2048]{2,1,0:T(8,128)(2,1)}, f32[4,768,1]{2,1,0:T(8,128)}) custom-call(s32[16,4,256]{2,1,0:T(4,128)} %reshape.270.place_ref, f32[16,4,256]{2,1,0:T(4,128)} %bitcast.141, bf16[16,256,2048]{2,1,0:T(8,128)(2,1)} %bitcast.120), custom_call_target="tpu_custom_call" | custom-call | tf_op jit(solution)/shard_map/pick_rows/pallas_call | solution.py:734
  307.9 34.4 %run_experts.1 = (bf16[4,768,512]{2,1,0:T(8,128)(2,1)}, bf16[4,768,512]{2,1,0:T(8,128)(2,1)}, bf16[4,768,512]{2,1,0:T(8,128)(2,1)}, bf16[4,768,2048]{2,1,0:T(8,128)(2,1)}, f32[4,768,1]{2,1,0:T(8,128)}) custom-call(bf16[4,768,2048]{2,1,0:T(8,128)(2,1)} %get-tuple-element.69.x, f32[4,768,512]{2,1,0:T(8,128)} %get-tuple-element.70.plain_ref, ...), custom_call_target="tpu_custom_call" | custom-call | tf_op jit(solution)/shard_map/run_experts/pallas_call | solution.py:819
  342.3 14.8 %put_rows_back.1 = (bf16[16,256,2048]{2,1,0:T(8,128)(2,1)}, f32[32,8,128]{2,1,0:T(8,128)}) custom-call(s32[16,4,256]{2,1,0:T(4,128)} %reshape.270.place_ref, bf16[4,768,2048]{2,1,0:T(8,128)(2,1)} %get-tuple-element.72.row_ref, f32[4,768,1]{2,1,0:T(8,128)} %get-tuple-element.73.grad_ref), custom_call_target="tpu_custom_call" | custom-call | tf_op jit(solution)/shard_map/put_rows_back/pallas_call | solution.py:770
  357.1 86.9 %experts_back.1 = (f32[128,2048]{1,0:T(8,128)}, f32[32,8,128]{2,1,0:T(8,128)}, bf16[16,256,2048]{2,1,0:T(8,128)(2,1)}) custom-call(bf16[32,128,2048]{2,1,0:T(8,128)(2,1)} %bitcast.122, f32[32,8,128]{2,1,0:T(8,128)} %get-tuple-element.75.dealt_ref, s32[16,4,256]{2,1,0:T(4,128)} %reshape.270.place_ref, bf16[4,768,512]{2,1,0:T(8,128)(2,1)} %get-tuple-element.96.hidden_ref.low, ...), custom_call_target="tpu_custom_call" | custom-call | tf_op jit(solution)/shard_map/experts_back/pallas_call | solution.py:1366
  448.9 50.7 %residual_grad.1 = (bf16[8,128,2048]{2,1,0:T(8,128)(2,1)}, bf16[32,64,128]{2,1,0:T(8,128)(2,1)}, bf16[4,64,2048]{2,1,0:T(8,128)(2,1)}) custom-call(bf16[128,2048]{1,0:T(8,128)(2,1)} %fusion.47.grad_ref, bf16[64,128]{1,0:T(8,128)(2,1)} %reshape.278.logit_ref, bf16[32,128,2048]{2,1,0:T(8,128)(2,1)} %bitcast.118), custom_call_target="tpu_custom_call" | custom-call | tf_op jit(solution)/shard_map/residual_grad/pallas_call | solution.py:1366
  505.8 4.3 convolution_convert_fusion.3
  517.3 2.8 multiply_reduce_fusion
  520.7 2.9 multiply_convert_fusion
  523.6 2.5 fusion.9
  530.0 6.7 fusion.4
  552.5 2.4 reshape.290
  554.8 2.9 fusion.21
  560.5 7.2 dot_sums.1
  568.5 2.3 multiply_convert_fusion.2
  570.9 5.0 convolution_convert_fusion
  575.9 5.2 convolution_convert_fusion.1
  581.1 85.4 %closing.1 = (f32[128,2048]{1,0:T(8,128)}, bf16[3,64,2048]{2,1,0:T(8,128)(2,1)}, bf16[64,2048]{1,0:T(8,128)(2,1)}, bf16[4,64,2048]{2,1,0:T(8,128)(2,1)}) custom-call(bf16[8,128,2048]{2,1,0:T(8,128)(2,1)} %bitcast.132, bf16[4,512,768]{2,1,0:T(8,128)(2,1)} %bitcast.133, bf16[4,64,2048]{2,1,0:T(8,128)(2,1)} %bitcast.135, bf16[32,128,2048]{2,1,0:T(8,128)(2,1)} %bitcast.119), custom_call_target="tpu_custom_call" | custom-call | tf_op jit(solution)/shard_map/closing/pallas_call | solution.py:1366
  669.0 12.8 %gain_gradients.1 = f32[8,128]{1,0:T(8,128)} custom-call(f32[32,8,128]{2,1,0:T(8,128)} %pad.4.src), custom_call_target="tpu_custom_call" | custom-call | tf_op jit(solution)/shard_map/gain_gradients/pallas_call | solution.py:1848
  684.0 2.4 collective-permute-start.4
  689.0 35.6 %expert_weight_grads.1 = (f32[4,2048,512]{2,1,0:T(8,128)}, f32[4,2048,512]{2,1,0:T(8,128)}, f32[4,512,2048]{2,1,0:T(8,128)}) custom-call(bf16[4,768,2048]{2,1,0:T(8,128)(2,1)} %get-tuple-element.69.x, bf16[4,768,2048]{2,1,0:T(8,128)(2,1)} %get-tuple-element.95.c, bf16[4,768,512]{2,1,0:T(8,128)(2,1)} %get-tuple-element.96.hidden_ref.low, ...), custom_call_target="tpu_custom_call" | custom-call | flops 19327352832 | bytes 100663296 | tf_op jit(solution)/shard_map/expert_weight_grads/pallas_call | solution.py:1014
  (166 shorter events, 74.4 us)
Async XLA Ops:
  92.2 96.8 %copy-start.11 = (f32[1024,64]{1,0:T(8,128)}, f32[1024,64]{1,0:T(8,128)S(1)}, u32[]{:S(2)}) copy-start(f32[1024,64]{1,0:T(8,128)S(1)} %get-tuple-element.145) | copy-start | bytes 786436
  92.2 96.8 %copy-start.12 = (f32[1024,64]{1,0:T(8,128)}, f32[1024,64]{1,0:T(8,128)S(1)}, u32[]{:S(2)}) copy-start(f32[1024,64]{1,0:T(8,128)S(1)} %get-tuple-element.147) | copy-start | bytes 786436
  93.5 95.5 %copy-start.5 = (bf16[128,2048]{1,0:T(8,128)(2,1)S(1)}, bf16[128,2048]{1,0:T(8,128)(2,1)}, u32[]{:S(2)}) copy-start(bf16[128,2048]{1,0:T(8,128)(2,1)} %tok.1) | copy-start | bytes 1572868
  357.1 88.0 %copy-start.10 = (bf16[32,64,128]{2,1,0:T(8,128)(2,1)S(1)}, bf16[32,64,128]{2,1,0:T(8,128)(2,1)}, u32[]{:S(2)}) copy-start(bf16[32,64,128]{2,1,0:T(8,128)(2,1)} %get-tuple-element.59) | copy-start | bytes 1572868
  446.9 52.8 %copy-start.1 = (f32[128,2048]{1,0:T(8,128)}, f32[128,2048]{1,0:T(8,128)S(1)}, u32[]{:S(2)}) copy-start(f32[128,2048]{1,0:T(8,128)S(1)} %get-tuple-element.154) | copy-start | bytes 3145732
  448.9 56.9 %copy-start.20 = (bf16[256,2048]{1,0:T(8,128)(2,1)S(1)}, bf16[256,2048]{1,0:T(8,128)(2,1)}, u32[]{:S(2)}) copy-start(bf16[256,2048]{1,0:T(8,128)(2,1)} %get-tuple-element.61.tall_in) | copy-start | bytes 3145732
  501.7 56.1 %collective-permute-start = (bf16[64,2048]{1,0:T(8,128)(2,1)}, bf16[64,2048]{1,0:T(8,128)(2,1)}, u32[]{:S(2)}, u32[]{:S(2)}) collective-permute-start(bf16[64,2048]{1,0:T(8,128)(2,1)} %get-tuple-element.130), channel_id=1, source_target_pairs={{0,1},{1,2},{2,3},{3,0},{4,5},{5,6},{6,7},{7,4},{8,9},{9,10},{10,1... | collective-permute-start | bytes 786440 | tf_op jit(solution)/shard_map/ppermute | solution.py:1865
  501.7 56.1 %collective-permute-start.1 = (bf16[64,2048]{1,0:T(8,128)(2,1)}, bf16[64,2048]{1,0:T(8,128)(2,1)}, u32[]{:S(2)}, u32[]{:S(2)}) collective-permute-start(bf16[64,2048]{1,0:T(8,128)(2,1)} %get-tuple-element.132), channel_id=1, source_target_pairs={{0,2},{1,3},{2,0},{3,1},{4,6},{5,7},{6,4},{7,5},{8,10},{9,11},{10,... | collective-permute-start | bytes 786440 | tf_op jit(solution)/shard_map/ppermute | solution.py:1865
  503.7 6.3 copy-start.19
  503.8 54.0 %collective-permute-start.2 = (bf16[64,2048]{1,0:T(8,128)(2,1)}, bf16[64,2048]{1,0:T(8,128)(2,1)}, u32[]{:S(2)}, u32[]{:S(2)}) collective-permute-start(bf16[64,2048]{1,0:T(8,128)(2,1)} %get-tuple-element.131), channel_id=1, source_target_pairs={{0,3},{1,0},{2,1},{3,2},{4,7},{5,4},{6,5},{7,6},{8,11},{9,8},{10,9... | collective-permute-start | bytes 786440 | tf_op jit(solution)/shard_map/ppermute | solution.py:1865
  511.4 5.9 copy-start.3
  530.0 6.7 copy-start.28
  530.0 6.7 copy-start.29
  581.1 85.4 %copy-start.6 = (bf16[128,2048]{1,0:T(8,128)(2,1)S(1)}, bf16[128,2048]{1,0:T(8,128)(2,1)}, u32[]{:S(2)}) copy-start(bf16[128,2048]{1,0:T(8,128)(2,1)} %tok.1) | copy-start | bytes 1572868
  666.5 21.3 %copy-start.22 = (bf16[3,64,2048]{2,1,0:T(8,128)(2,1)S(1)}, bf16[3,64,2048]{2,1,0:T(8,128)(2,1)}, u32[]{:S(2)}) copy-start(bf16[3,64,2048]{2,1,0:T(8,128)(2,1)} %get-tuple-element.91) | copy-start | bytes 2359300
  683.1 42.9 %collective-permute-start.3 = (bf16[64,2048]{1,0:T(8,128)(2,1)S(1)}, bf16[64,2048]{1,0:T(8,128)(2,1)S(1)}, u32[]{:S(2)}, u32[]{:S(2)}) collective-permute-start(bf16[64,2048]{1,0:T(8,128)(2,1)S(1)} %get-tuple-element.127), channel_id=1, source_target_pairs={{0,1},{1,2},{2,3},{3,0},{4,5},{5,6},{6,7},{7,4},{8,9},{9,10},{10,1... | collective-permute-start | bytes 786440 | tf_op jit(solution)/shard_map/ppermute | solution.py:1865
  684.0 42.0 %collective-permute-start.4 = (bf16[64,2048]{1,0:T(8,128)(2,1)S(1)}, bf16[64,2048]{1,0:T(8,128)(2,1)S(1)}, u32[]{:S(2)}, u32[]{:S(2)}) collective-permute-start(bf16[64,2048]{1,0:T(8,128)(2,1)S(1)} %get-tuple-element.129), channel_id=1, source_target_pairs={{0,2},{1,3},{2,0},{3,1},{4,6},{5,7},{6,4},{7,5},{8,10},{9,11},{10,... | collective-permute-start | bytes 786440 | tf_op jit(solution)/shard_map/ppermute | solution.py:1865
  686.4 39.6 %collective-permute-start.5 = (bf16[64,2048]{1,0:T(8,128)(2,1)S(1)}, bf16[64,2048]{1,0:T(8,128)(2,1)S(1)}, u32[]{:S(2)}, u32[]{:S(2)}) collective-permute-start(bf16[64,2048]{1,0:T(8,128)(2,1)S(1)} %get-tuple-element.128), channel_id=1, source_target_pairs={{0,3},{1,0},{2,1},{3,2},{4,7},{5,4},{6,5},{7,6},{8,11},{9,8},{10,9... | collective-permute-start | bytes 786440 | tf_op jit(solution)/shard_map/ppermute | solution.py:1865
  689.0 35.6 %copy-start.25 = (bf16[64,2048]{1,0:T(8,128)(2,1)S(1)}, bf16[64,2048]{1,0:T(8,128)(2,1)}, u32[]{:S(2)}) copy-start(bf16[64,2048]{1,0:T(8,128)(2,1)} %get-tuple-element.92) | copy-start | bytes 786436
  689.0 36.5 %copy-start.26 = (f32[8,128]{1,0:T(8,128)S(1)}, f32[8,128]{1,0:T(8,128)}, u32[]{:S(2)}) copy-start(f32[8,128]{1,0:T(8,128)} %gain_gradients.1) | copy-start | bytes 12292
  689.0 38.1 %copy-start.2 = (f32[128,2048]{1,0:T(8,128)S(1)}, f32[128,2048]{1,0:T(8,128)}, u32[]{:S(2)}) copy-start(f32[128,2048]{1,0:T(8,128)} %copy-done.1) | copy-start | bytes 3145732
  689.0 38.1 %copy-start.8 = (bf16[128,2048]{1,0:T(8,128)(2,1)S(1)}, bf16[128,2048]{1,0:T(8,128)(2,1)}, u32[]{:S(2)}) copy-start(bf16[128,2048]{1,0:T(8,128)(2,1)} %cot.3) | copy-start | bytes 1572868
  689.0 38.1 %copy-start.14 = (f32[128,2048]{1,0:T(8,128)S(1)}, f32[128,2048]{1,0:T(8,128)}, u32[]{:S(2)}) copy-start(f32[128,2048]{1,0:T(8,128)} %get-tuple-element.89) | copy-start | bytes 3145732
  689.0 38.1 %copy-start.17 = (f32[64,2048]{1,0:T(8,128)S(1)}, f32[64,2048]{1,0:T(8,128)}, u32[]{:S(2)}) copy-start(f32[64,2048]{1,0:T(8,128)} %fusion.29) | copy-start | bytes 1572868
  (12 other events, 33.3 us)

commit v3 on v2

--- a/solution.py
+++ b/solution.py
@@ -63,7 +63,7 @@
 
 
 MESH_ID = pl.DeviceIdType.MESH
-VMEM_BYTES = 56 * 1024 * 1024
+VMEM_BYTES = 60 * 1024 * 1024
 
 
 class Place:
@@ -112,22 +112,30 @@
 
         pl.semaphore_wait(barrier, 7)
     else:
-        planes = reach == "planes"
-        tell(place.at(0, 1 - place.blk))
-        if planes:
-            tell(place.at(1))
-            tell(place.at(2))
-
-        @pl.when(place.z > 0)
-        def _():
-            tell(place.at(z=place.z - 1))
-
-        @pl.when(place.z < 3)
-        def _():
-            tell(place.at(z=place.z + 1))
-
-        ends = (3 - place.z) // 3 + place.z // 3
-        pl.semaphore_wait(barrier, 3 + (2 if planes else 0) - ends)
+        tell_partners(place, barrier)
+        wait_partners(place, barrier)
+
+
+def tell_partners(place, semaphore):
+    def tell(target):
+        pl.semaphore_signal(semaphore, inc=1, device_id=target, device_id_type=MESH_ID)
+
+    tell(place.at(0, 1 - place.blk))
+    tell(place.at(1))
+    tell(place.at(2))
+
+    @pl.when(place.z > 0)
+    def _():
+        tell(place.at(z=place.z - 1))
+
+    @pl.when(place.z < 3)
+    def _():
+        tell(place.at(z=place.z + 1))
+
+
+def wait_partners(place, semaphore):
+    ends = (3 - place.z) // 3 + place.z // 3
+    pl.semaphore_wait(semaphore, 5 - ends)
 
 
 def remote(src, dst, send_sem, recv_sem, target):
@@ -438,7 +446,7 @@
     LOCALS = 20
 
     def __init__(self, place, part, out, scratch, full, band=None):
-        self.p, self.part, self.out, self.full, self.plane_only = place, part, out, full, band is not None
+        self.p, self.part, self.out, self.full = place, part, out, full
         if full:
             (self.acc, self.near, self.half_in, self.side_in, self.line_in, self.sum, self.send, self.recv, self.local) = scratch
         else:
@@ -583,9 +591,7 @@
             self.side_y(s).wait_recv()
             terms = terms + [self.side_in.at[0, s], self.side_in.at[1, s]]
         add_rows(self.acc.at[0, s], terms, self.rows)
-        if self.plane_only:
-            self.keep_plane(i).start()
-        elif i < 3:
+        if i < 3:
 
             @pl.when(z == 0)
             def _():
@@ -657,21 +663,6 @@
                 self.line_down(s).wait_send()
 
         done.wait()
-
-    def keep_plane(self, i):
-        s = self.order(i)
-        return pltpu.make_async_copy(self.acc.at[0, s], self.out.at[s], self.local.at[16 + i])
-
-    def settle_plane(self):
-        for i in range(4):
-            s = self.order(i)
-            self.keep_plane(i).wait()
-            for k in range(4):
-                self.core(k, s).wait_send()
-            self.half_x(s).wait_send()
-            self.half_y(s).wait_send()
-            self.side_x(s).wait_send()
-            self.side_y(s).wait_send()
 
     def steps(self):
         plan = [
@@ -726,11 +717,9 @@
                 at = pl.ds(i * per, per)
                 row_ref[e, at] = rows[e * per : (e + 1) * per]
                 hot = is_place(place_ref[i, e : e + 1], per)
-                row_prob_ref[e, at] = jnp.sum(
-                    jnp.where(hot, prob_ref[i, e : e + 1], 0.0), axis=1, keepdims=True
-                )
-
-    small = pl.BlockSpec((step, experts, pair_rows), lambda p: (p, 0, 0))
+                prob = jnp.concatenate([prob_ref[2 * i, e : e + 1], prob_ref[2 * i + 1, e : e + 1]], axis=1)
+                row_prob_ref[e, at] = jnp.sum(jnp.where(hot, prob, 0.0), axis=1, keepdims=True)
+
     return pl.pallas_call(
         kernel,
         out_shape=[
@@ -738,7 +727,11 @@
             jax.ShapeDtypeStruct((experts, pairs * per, 1), jnp.float32),
         ],
         grid=(pairs // step,),
-        in_specs=[small, small, pl.BlockSpec((step, pair_rows, width), lambda p: (p, 0, 0))],
+        in_specs=[
+            pl.BlockSpec((step, experts, pair_rows), lambda p: (p, 0, 0)),
+            pl.BlockSpec((2 * step, experts, pair_rows // 2), lambda p: (p, 0, 0)),
+            pl.BlockSpec((step, pair_rows, width), lambda p: (p, 0, 0)),
+        ],
         out_specs=[
             pl.BlockSpec((experts, step * per, width), lambda p: (0, p, 0)),
             pl.BlockSpec((experts, step * per, 1), lambda p: (0, p, 0)),
@@ -1030,8 +1023,8 @@
 
 
 class ColumnsFlow:
-    SENDS = 24 + 1 + 8
-    RECVS = 8 + 1 + 8
+    SENDS = 24 + 1 + 16
+    RECVS = 24 + 1 + 16
     LOCALS = 4
 
     def __init__(self, place, sources, rows_in, wide, tall, send, recv, local):
@@ -1040,25 +1033,25 @@
         self.rows = rows_in.shape[0]
         self.share = wide.shape[1] // len(sources)
 
-    def wide_rows(self, col):
-        return pl.ds(pl.multiple_of((self.p.dp * 8 + col) * self.rows, self.rows), self.rows)
-
-    def piece(self, i, to, start):
-        share = self.share
-        src = self.sources[i].at[:, pl.ds(pl.multiple_of(to * share, share), share)]
-        dst = self.wide.at[self.wide_rows(self.p.col), pl.ds(i * share, share)]
-        return src, dst
+    def spot(self, i, col):
+        rows = pl.ds(pl.multiple_of((self.p.dp * 8 + col) * self.rows, self.rows), self.rows)
+        return self.wide.at[rows, pl.ds(i * self.share, self.share)]
+
+    def piece(self, i, to):
+        return self.sources[i].at[:, pl.ds(pl.multiple_of(to * self.share, self.share), self.share)]
 
     def scatter(self, step, i):
         to = (self.p.col + step) % 8
-        src, dst = self.piece(i, to, step)
         return remote(
-            src, dst, self.send.at[3 * step + i], self.recv.at[self.p.col], (self.p.dp, to // 4, to % 4)
+            self.piece(i, to),
+            self.spot(i, self.p.col),
+            self.send.at[3 * step + i],
+            self.recv.at[3 * self.p.col + i],
+            (self.p.dp, to // 4, to % 4),
         )
 
     def keep(self, i):
-        src, dst = self.piece(i, self.p.col, 0)
-        return pltpu.make_async_copy(src, dst, self.local.at[i])
+        return pltpu.make_async_copy(self.piece(i, self.p.col), self.spot(i, self.p.col), self.local.at[i])
 
     def tall_rows(self, k):
         return self.tall.at[pl.ds(pl.multiple_of(self.p.column(k) * self.rows, self.rows), self.rows)]
@@ -1067,7 +1060,7 @@
         group = self.p.dp * 2 + self.p.blk
         dst = self.tall.at[pl.ds(pl.multiple_of(self.p.z * self.rows, self.rows), self.rows)]
         return remote(
-            self.rows_in, dst, self.send.at[24], self.recv.at[8], (self.p.z, group // 4, group % 4)
+            self.rows_in, dst, self.send.at[24], self.recv.at[24], (self.p.z, group // 4, group % 4)
         )
 
     def stay(self):
@@ -1077,26 +1070,24 @@
         group = self.p.dp * 2 + self.p.blk
         return (self.p.z == self.p.dp) & (group == self.p.col)
 
-    def band(self, which, k):
-        if which == 0:
-            height = 8 * self.rows
-            return self.wide.at[pl.ds(pl.multiple_of(self.p.column(k) * height, height), height)]
-        return self.tall_rows(k)
-
-    def across(self, which, k):
-        ref = self.band(which, 0)
-        slot = 4 * which + k - 1
-        return remote(ref, ref, self.send.at[25 + slot], self.recv.at[9 + slot], self.p.at(k))
-
-    def part(self, which, k, first):
-        ref = self.band(which, k)
-        half = ref.shape[0] // 2
-        return ref.at[pl.ds(0 if first else half, half)]
-
-    def turn(self, which, k):
-        ref = self.part(which, k, k == 1)
-        slot = 4 * which + 1 + k
-        return remote(ref, ref, self.send.at[25 + slot], self.recv.at[9 + slot], self.p.at(3 - k))
+    def band(self, i, k, first=0, parts=1):
+        if i == 3:
+            height, ref = self.rows, self.tall
+        else:
+            height, ref = 8 * self.rows, self.wide
+        part = height // parts
+        rows = pl.ds(pl.multiple_of(self.p.column(k) * height + first * part, part), part)
+        return ref.at[rows] if i == 3 else ref.at[rows, pl.ds(i * self.share, self.share)]
+
+    def across(self, i, k):
+        ref = self.band(i, 0)
+        slot = 25 + 4 * i + k - 1
+        return remote(ref, ref, self.send.at[slot], self.recv.at[slot], self.p.at(k))
+
+    def turn(self, i, k):
+        ref = self.band(i, k, k - 1, 2)
+        slot = 25 + 4 * i + 1 + k
+        return remote(ref, ref, self.send.at[slot], self.recv.at[slot], self.p.at(3 - k))
 
     def got(self, sem, ref):
         remote(ref, ref, self.send.at[0], self.recv.at[sem], self.p.at(0, 1 - self.p.blk)).wait_recv()
@@ -1112,50 +1103,48 @@
         def _():
             self.swap().start()
 
-        @pl.loop(1, 8)
-        def _(step):
-            for i in range(3):
+        for i in range(3):
+
+            @pl.loop(1, 8)
+            def _(step):
                 self.scatter(step, i).start()
 
-        for i in range(3):
             self.keep(i).start()
 
-    def settle(self):
-        home = self.at_home()
-
-        @pl.when(home)
-        def _():
-            self.stay().wait()
-
-        @pl.when(jnp.logical_not(home))
-        def _():
-            self.got(8, self.tall_rows(0))
-
-        self.across(1, 1).start()
-        self.across(1, 2).start()
-        for i in range(3):
+    def settle(self, i):
+        if i == 3:
+            home = self.at_home()
+
+            @pl.when(home)
+            def _():
+                self.stay().wait()
+
+            @pl.when(jnp.logical_not(home))
+            def _():
+                self.got(24, self.tall_rows(0))
+
+        else:
             self.keep(i).wait()
 
-        @pl.loop(1, 8)
-        def _(step):
-            col = (self.p.col + step) % 8
-            self.got(col, self.wide.at[self.wide_rows(col)])
-
-        self.across(0, 1).start()
-        self.across(0, 2).start()
-
-    def turns(self):
-        for which in (1, 0):
+            @pl.loop(1, 8)
+            def _(step):
+                col = (self.p.col + step) % 8
+                self.got(3 * col + i, self.spot(i, col))
+
+        self.across(i, 1).start()
+        self.across(i, 2).start()
+
+    def turns(self, i):
+        for k in (1, 2):
+            self.got(25 + 4 * i + k - 1, self.band(i, k))
+            self.turn(i, k).start()
+
+    def finish(self):
+        for i in (3, 0, 1, 2):
             for k in (1, 2):
-                self.got(9 + 4 * which + k - 1, self.band(which, k))
-                self.turn(which, k).start()
-
-    def finish(self):
-        for which in (1, 0):
-            for k in (1, 2):
-                self.got(9 + 4 * which + 1 + k, self.part(which, 3, k == 1))
-                self.turn(which, k).wait_send()
-                self.across(which, k).wait_send()
+                self.got(25 + 4 * i + 1 + k, self.band(i, 3, k - 1, 2))
+                self.turn(i, k).wait_send()
+                self.across(i, k).wait_send()
 
         @pl.when(jnp.logical_not(self.at_home()))
         def _():
@@ -1172,9 +1161,8 @@
     RECVS = 8 + 8 + 1
     LOCALS = 12
 
-    def __init__(self, place, wide, tall, wide_out, tall_out, scratch):
+    def __init__(self, place, wide_out, tall_out, scratch):
         self.p = place
-        self.parts = (wide, tall)
         self.outs = (wide_out, tall_out)
         self.acc, self.half_in, self.side_in = scratch[0:2], scratch[2:4], scratch[4:6]
         self.send, self.recv, self.local = scratch[6:9]
@@ -1184,18 +1172,13 @@
     def scratch(wide, tall):
         shapes = []
         for kind in ((4, 1), (2, 2), (2, 1)):
-            for part in (wide, tall):
-                shapes.append(pltpu.VMEM((kind[0], part.shape[1] // kind[1], part.shape[2]), part.dtype))
+            for rows, width in (wide, tall):
+                shapes.append(pltpu.VMEM((kind[0], rows // kind[1], width), jnp.bfloat16))
         return shapes + [
             pltpu.SemaphoreType.DMA((SumsFlow.SENDS,)),
             pltpu.SemaphoreType.DMA((SumsFlow.RECVS,)),
             pltpu.SemaphoreType.DMA((SumsFlow.LOCALS,)),
         ]
-
-    def load(self, which, k):
-        return pltpu.make_async_copy(
-            self.parts[which].at[self.p.column(k)], self.acc[which].at[k], self.local.at[4 * which + k]
-        )
 
     def halves(self, ref):
         half = ref.shape[0] // 2
@@ -1240,42 +1223,35 @@
     def at_home(self):
         return (self.p.col // 2 == self.p.dp) & (self.p.col % 2 == self.p.blk) & (self.p.z == self.p.dp)
 
-    def begin(self):
-        for which in (1, 0):
-            for k in (3, 2, 1, 0):
-                self.load(which, k).start()
-        for which in (1, 0):
-            self.load(which, 3).wait()
-            self.corner(which, 1).start()
-            self.corner(which, 2).start()
-
-    def sides(self):
-        for which in (1, 0):
-            for k, other in ((2, 1), (1, 2)):
-                self.load(which, k).wait()
-                self.corner(which, other).wait_recv()
-                target = self.halves(self.acc[which].at[k])[other - 1]
-                add_rows(target, [target, self.half_in[which].at[other - 1]], target.shape[0])
-                self.side(which, k).start()
-
-    def total(self):
-        for which in (1, 0):
-            self.load(which, 0).wait()
-            self.side(which, 1).wait_recv()
-            self.side(which, 2).wait_recv()
-            mine = self.acc[which].at[0]
-            add_rows(mine, [mine, self.side_in[which].at[0], self.side_in[which].at[1]], mine.shape[0])
-            if which == 1:
-                home = self.at_home()
-
-                @pl.when(home)
-                def _():
-                    self.stay().start()
-
-                @pl.when(jnp.logical_not(home))
-                def _():
-                    self.swap().start()
-
+    def corners(self, which):
+        self.corner(which, 1).start()
+        self.corner(which, 2).start()
+
+    def sides(self, which):
+        for k, other in ((2, 1), (1, 2)):
+            self.corner(which, other).wait_recv()
+            target = self.halves(self.acc[which].at[k])[other - 1]
+            add_rows(target, [target, self.half_in[which].at[other - 1]], target.shape[0])
+            self.side(which, k).start()
+
+    def total(self, which):
+        self.side(which, 1).wait_recv()
+        self.side(which, 2).wait_recv()
+        mine = self.acc[which].at[0]
+        add_rows(mine, [mine, self.side_in[which].at[0], self.side_in[which].at[1]], mine.shape[0])
+
+    def hand_out_tall(self):
+        home = self.at_home()
+
+        @pl.when(home)
+        def _():
+            self.stay().start()
+
+        @pl.when(jnp.logical_not(home))
+        def _():
+            self.swap().start()
+
+    def hand_out_wide(self):
         @pl.loop(1, 8)
         def _(step):
             for i in range(3):
@@ -1407,16 +1383,22 @@
         plane.begin()
         for d in range(4):
             params.turn(d)
+        weights.settle(3)
+        weights.settle(0)
         plane.turns()
-        weights.settle()
+        weights.settle(1)
         line.begin()
+        weights.turns(3)
         for d in range(4):
             params.corner(d)
         plane.corners()
+        weights.settle(2)
+        weights.turns(0)
         line.along(1)
+        weights.turns(1)
         params.finish()
         line.along(2)
-        weights.turns()
+        weights.turns(2)
         line.along(3)
         plane.finish()
         line.finish()
@@ -1621,67 +1603,10 @@
     )
 
 
-def closing_call(normed_part, wide, tall, out_part):
-    height = out_part.shape[1] // 2
-    line = ScatterFlow.scratch(normed_part.shape[1], normed_part.shape[2], normed_part.dtype, False)
-    half = ScatterFlow.scratch(height, out_part.shape[2], out_part.dtype, True)
-    sums = SumsFlow.scratch(wide, tall)
-    rows = tall.shape[1]
-
-    def kernel(part, wide_in, tall_in, mixed_in, out, wide_out, tall_out, mixed, *scratch):
-        place = Place()
-        entry_barrier(place, "all")
-        first, second = len(line), len(line) + len(half)
-        weights = SumsFlow(place, wide_in, tall_in, wide_out, tall_out, scratch[second:])
-        flow = ScatterFlow(place, part, out, scratch[:first], False)
-        plane = ScatterFlow(place, mixed_in, mixed, scratch[first:second], True, (height, height))
-        weights.begin()
-        flow.begin()
-        plane.begin()
-        flow.stage3(0)
-        flow.stage3(1)
-        weights.sides()
-        plane.stage1(0)
-        plane.stage1(1)
-        flow.chain(0)
-        flow.stage3(2)
-        plane.stage1(2)
-        plane.stage1(3)
-        weights.total()
-        flow.chain(1)
-        flow.chain(2)
-        plane.stage2(0)
-        plane.stage2(1)
-        flow.stage3(3)
-        plane.stage2(2)
-        plane.stage2(3)
-        flow.final()
-        for i in range(4):
-            plane.stage3(i)
-        weights.finish()
-        plane.settle_plane()
-
-    shapes = [
-        jax.ShapeDtypeStruct(normed_part.shape[1:], jnp.float32),
-        jax.ShapeDtypeStruct((3, rows, 8 * wide.shape[2] // 3), wide.dtype),
-        jax.ShapeDtypeStruct((rows, tall.shape[2]), tall.dtype),
-        jax.ShapeDtypeStruct((4, height, out_part.shape[2]), out_part.dtype),
-    ]
-    return hbm_call(kernel, shapes, line + half + sums, "closing", 2, (normed_part, wide, tall, out_part))
-
-
-def run_beside(steps, work):
-    steps[0]()
-    work.begin()
-
-    @pl.loop(0, work.units)
+def run_units(work, first, last):
+    @pl.loop(first, last)
     def _(unit):
-        for i, step in enumerate(steps[1:-1]):
-            pl.when(unit == i)(step)
         work.run(unit)
-
-    steps[-1]()
-    work.finish()
 
 
 def features_call(features, probs, places, cotangent_all, down_weight, per):
@@ -1695,14 +1620,41 @@
         flow = GatherFlow(place, feature_ref, feature_out, scratch[0], scratch[1], True)
         work = PickWork(place_ref, cot, weight, rows, plain, scratch[4:])
 
-        def both(i):
-            def act():
-                small.steps()[i]()
-                flow.steps()[i]()
-
-            return act
-
-        run_beside([both(i) for i in range(len(flow.steps()))], work)
+        flows = (small, flow)
+
+        def along(d):
+            for each in flows:
+                each.along(d)
+
+        def turn(d):
+            for each in flows:
+                each.turn(d)
+
+        def corner(d):
+            for each in flows:
+                each.corner(d)
+
+        for each in flows:
+            each.begin()
+        work.begin()
+        run_units(work, 0, 4)
+        along(1)
+        turn(0)
+        run_units(work, 4, 9)
+        along(2)
+        corner(0)
+        run_units(work, 9, 13)
+        along(3)
+        turn(1)
+        run_units(work, 13, work.units)
+        corner(1)
+        turn(2)
+        corner(2)
+        turn(3)
+        corner(3)
+        for each in flows:
+            each.finish()
+        work.finish()
 
     shapes = [
         jax.ShapeDtypeStruct((32,) + features.shape, features.dtype),
@@ -1727,7 +1679,28 @@
         flow = ScatterFlow(place, part_ref, out, scratch[3 : 3 + len(sums)], True)
         work = OutputWork(place_ref, hidden_ref, weight_ref, mixed, scratch[3 + len(sums) :])
         deal.begin()
-        run_beside(flow.steps(), work)
+        flow.begin()
+        work.begin()
+        for i in range(4):
+            flow.stage1(i)
+        run_units(work, 0, 8)
+        flow.stage2(0)
+        flow.stage2(1)
+        run_units(work, 8, 12)
+        flow.stage2(2)
+        flow.stage2(3)
+        run_units(work, 12, 16)
+        flow.stage3(0)
+        flow.stage3(1)
+        flow.chain(0)
+        run_units(work, 16, 20)
+        flow.stage3(2)
+        flow.chain(1)
+        flow.chain(2)
+        run_units(work, 20, work.units)
+        flow.stage3(3)
+        flow.final()
+        work.finish()
         deal.finish()
 
     shapes = [
@@ -1741,138 +1714,309 @@
     )
 
 
-def residual_grad_call(grad, logit_grad, out_part):
-    height = out_part.shape[1] // 2
-    sums = ScatterFlow.scratch(height, out_part.shape[2], out_part.dtype, True)
-
-    def kernel(grad_ref, logit_ref, part_ref, grad_out, logit_out, out, *scratch):
+def attention_back_call(
+    grad, logit_grad, out_part, tokens, gain, feature_row, wide, tall, head_gains, cosine, sine, kept
+):
+    tok_rows, width = grad.shape
+    rows = kept[0].shape[0]
+    share = tall.shape[0]
+    heads = share // HEAD_DIM
+    own_rows = width // 32
+    block = 2 * tok_rows
+    blocks = rows // block
+    band_rows = width // 4
+    height = tok_rows // 2
+    scale = 1.0 / math.sqrt(HEAD_DIM)
+    bf16, f32 = jnp.bfloat16, jnp.float32
+    line = ScatterFlow.scratch(tok_rows, width, bf16, False)
+    mixed = ScatterFlow.scratch(height, width, bf16, True)
+    sums = SumsFlow.scratch((band_rows, 3 * share), (share // 4, width))
+    flow_scratch = line + mixed + mixed[-3:] + sums + DealFlow.scratch() + gather_sems() * 2
+    flow_scratch += [pltpu.SemaphoreType.REGULAR]
+
+    def kernel(*refs):
+        grad_ref, logit_ref, part_ref, tok_in, gain_ref, feature_ref, wide_in, tall_in = refs[:8]
+        head_gain, cos, sin, normed_in, unit_in, qkv_in, context_in, scale_ref, log_ref = refs[8:17]
+        logit_out, first_out, second_out, normed_grad, wide_out, tall_out, gain_out = refs[17:24]
+        scratch = refs[24:]
+        grads, tok, wide_ref, tall_ref, normed, unit, qkv, context, context_grad = scratch[:9]
+        grad_q, grad_k, grad_v, low_grads, dots, landed, deals, dealt, tall_grad = scratch[9:18]
+        ins, send, recv = scratch[18:21]
+        rest = list(scratch[21:])
+
+        def take(count):
+            taken = rest[:count]
+            del rest[:count]
+            return taken
+
         place = Place()
-        entry_barrier(place, "planes")
-        line = GatherFlow(place, grad_ref, grad_out, scratch[0], scratch[1], False)
-        logits = GatherFlow(place, logit_ref, logit_out, scratch[2], scratch[3], True)
-        flow = ScatterFlow(place, part_ref, out, scratch[4:], True, (0, height))
-        line.begin()
+        entry_barrier(place, "all")
+        line_scratch, mixed_scratch, more = take(len(line)), take(len(mixed)), take(3)
+        weights = SumsFlow(place, wide_out, tall_out, take(len(sums)))
+        deal = DealFlow(place, deals, dealt, *take(3))
+        gather = GatherFlow(place, grad_ref, grads, *take(2), False)
+        logits = GatherFlow(place, logit_ref, logit_out, *take(2), True)
+        freed = take(1)[0]
+        flow = ScatterFlow(place, grads, normed_grad, line_scratch, False)
+        first = ScatterFlow(place, part_ref, first_out, mixed_scratch, True, (0, height))
+        second = ScatterFlow(
+            place, part_ref, second_out, mixed_scratch[:-3] + more, True, (height, height)
+        )
+        gather.begin()
         logits.begin()
-        flow.begin()
-        flow.stage1(0)
-        flow.stage1(1)
-        line.along(1)
+        first.begin()
+        sources = (tok_in, wide_in, tall_in, normed_in, unit_in, qkv_in, context_in)
+        held = (tok, wide_ref, tall_ref, normed, unit, qkv, context)
+        loads = [pltpu.make_async_copy(s, d, ins.at[n]) for n, (s, d) in enumerate(zip(sources, held))]
+        for copy in loads:
+            copy.start()
+        deals[...] = jnp.zeros_like(deals)
+        dots[...] = jnp.zeros_like(dots)
+        first.stage1(0)
+        first.stage1(1)
+        gather.along(1)
         logits.along(1)
         logits.turn(0)
-        flow.stage1(2)
-        flow.stage1(3)
-        flow.stage2(0)
-        line.along(2)
+        first.stage1(2)
+        first.stage1(3)
+        first.stage2(0)
+        gather.along(2)
         logits.along(2)
         logits.turn(1)
-        flow.stage2(1)
-        flow.stage2(2)
-        line.along(3)
+        first.stage2(1)
+        first.stage2(2)
+        gather.along(3)
         logits.along(3)
         logits.turn(2)
         logits.turn(3)
-        flow.stage3(0)
-        flow.stage2(3)
-        flow.stage3(1)
+        first.stage3(0)
+        first.stage2(3)
+        first.stage3(1)
+        first.chain(0)
         for d in range(4):
             logits.corner(d)
-        flow.stage3(2)
-        line.finish()
-        logits.finish()
-        flow.stage3(3)
-        flow.settle_plane()
-
-    shapes = [
-        jax.ShapeDtypeStruct((8,) + grad.shape, grad.dtype),
-        jax.ShapeDtypeStruct((32,) + logit_grad.shape, logit_grad.dtype),
-        jax.ShapeDtypeStruct((4, height, out_part.shape[2]), out_part.dtype),
-    ]
-    return hbm_call(kernel, shapes, gather_sems() * 2 + sums, "residual_grad", 7, (grad, logit_grad, out_part))
-
-
-def column_sum(values, name, collective_id):
-    def kernel(src, out, landed, send, recv):
-        place = Place()
-        entry_barrier(place, "column")
-
-        def copy(step):
+        gather.finish()
+        for copy in loads:
+            copy.wait()
+
+        @pl.loop(0, blocks)
+        def _(i):
+            at = pl.ds(pl.multiple_of(i * block, block), block)
+            values = grads[pl.ds(2 * i, 2)].reshape(block, width)
+            context_grad[at] = inner(values, tall_ref[...], 1, 1).astype(bf16)
+
+        first.stage3(2)
+        first.chain(1)
+        first.chain(2)
+        first.stage3(3)
+
+        @pl.loop(0, 4)
+        def _(i):
+            lanes = pl.ds(pl.multiple_of(i * band_rows, band_rows), band_rows)
+            values = grads[:, :, lanes].reshape(rows, band_rows)
+            tall_grad[:, lanes] = inner(context[...], values, 0, 0).astype(bf16)
+
+        for k in range(4):
+            at = pl.ds(pl.multiple_of(place.column(k) * own_rows, own_rows), own_rows)
+            weights.acc[1][k] = tall_grad[at]
+        first.final()
+        tell_partners(place, freed)
+
+        def back_block(h, i):
+            seen = (i + 1) * block
+            here, lanes = slice(i * block, seen), slice(h * HEAD_DIM, (h + 1) * HEAD_DIM)
+            queries = qkv[here, lanes]
+            keys = qkv[:seen, share + h * HEAD_DIM : share + (h + 1) * HEAD_DIM]
+            values = qkv[:seen, 2 * share + h * HEAD_DIM : 2 * share + (h + 1) * HEAD_DIM]
+            outer = context_grad[here, lanes]
+            scores = inner(queries, keys, 1, 1) * scale
+            row = lax.broadcasted_iota(jnp.int32, scores.shape, 0) + i * block
+            column = lax.broadcasted_iota(jnp.int32, scores.shape, 1)
+            probs = jnp.where(column <= row, jnp.exp(scores - log_ref[here, h : h + 1]), 0.0)
+            prob_dots = inner(outer, values, 1, 1)
+            delta = jnp.sum(probs * prob_dots, axis=1, keepdims=True)
+            score_grad = (probs * (prob_dots - delta)).astype(bf16)
+            grad_q[here, lanes] = inner(score_grad, keys) * scale
+            key_part = inner(score_grad, queries, 0, 0) * scale
+            value_part = inner(probs.astype(bf16), outer, 0, 0)
+            if i == blocks - 1:
+                grad_k[:, lanes] = key_part
+                grad_v[:, lanes] = value_part
+            else:
+                grad_k[:seen, lanes] += key_part
+                grad_v[:seen, lanes] += value_part
+
+        back_block(0, 3)
+        wait_partners(place, freed)
+        second.begin()
+        weights.corners(1)
+        back_block(0, 2)
+        for i in range(4):
+            second.stage1(i)
+        back_block(0, 1)
+        back_block(0, 0)
+        back_block(1, 3)
+        second.stage2(0)
+        weights.sides(1)
+        back_block(1, 2)
+        second.stage2(1)
+        back_block(1, 1)
+        second.stage2(2)
+        back_block(1, 0)
+        second.stage2(3)
+
+        @pl.loop(0, blocks)
+        def _(i):
+            at = pl.ds(pl.multiple_of(i * block, block), block)
+            low_grads[at, 2 * share :] = grad_v[at].astype(bf16)
+            for n, grad_n in enumerate((grad_q, grad_k)):
+                total = jnp.zeros((block, 1), f32)
+                for h in range(heads):
+                    lanes = slice(h * HEAD_DIM, (h + 1) * HEAD_DIM)
+                    turned = grad_n[at, lanes].astype(bf16).astype(f32)
+                    back = turned * cos[at] - pltpu.roll(turned, HEAD_DIM // 2, 1) * sin[at]
+                    mine = unit[at, n * share + h * HEAD_DIM : n * share + (h + 1) * HEAD_DIM]
+                    for j in range(HEAD_DIM // own_rows):
+                        to = place.col * 4 + h * (HEAD_DIM // own_rows) + j
+                        columns = slice(j * own_rows, (j + 1) * own_rows)
+                        deals[to, 1 + n : 2 + n, :own_rows] += jnp.sum(
+                            (back * mine)[:, columns], axis=0, keepdims=True
+                        )
+                    weighted = back * head_gain[n : n + 1, lanes]
+                    grad_n[at, lanes] = weighted
+                    total += jnp.sum(weighted * mine, axis=1, keepdims=True)
+                dots[n : n + 1, at] = jnp.transpose(jnp.broadcast_to(total, (block, 128)))[:1]
+
+        def exchange(step):
             to = (place.col + step) % 8
             return remote(
-                src, landed.at[place.col], send.at[step], recv.at[place.col], (place.dp, to // 4, to % 4)
+                dots, landed.at[place.col], send.at[step], recv.at[place.col], (place.dp, to // 4, to % 4)
             )
 
         @pl.loop(1, 8)
         def _(step):
-            copy(step).start()
-
-        landed[place.col] = src[...]
+            exchange(step).start()
+
+        landed[place.col] = dots[...]
+        second.stage3(0)
 
         @pl.loop(1, 8)
         def _(step):
             col = (place.col + step) % 8
-            remote(src, landed.at[col], send.at[0], recv.at[col], place.at(0, 1 - place.blk)).wait_recv()
-            copy(step).wait_send()
-
-        total = landed[0]
+            remote(dots, landed.at[col], send.at[0], recv.at[col], place.at(0, 1 - place.blk)).wait_recv()
+            exchange(step).wait_send()
+
+        total_dots = landed[0]
         for col in range(1, 8):
-            total = total + landed[col]
-        out[...] = total
-
-    return pl.pallas_call(
+            total_dots = total_dots + landed[col]
+        columns = jnp.transpose(total_dots / width)
+        for n, grad_n in enumerate((grad_q, grad_k)):
+            mine = unit[:, n * share : (n + 1) * share]
+            low = scale_ref[:, n : n + 1] * (grad_n[...] - mine * columns[:, n : n + 1])
+            low_grads[:, n * share : (n + 1) * share] = low.astype(bf16)
+
+        def wide_grad(k):
+            lanes = pl.ds(pl.multiple_of(place.column(k) * band_rows, band_rows), band_rows)
+            weights.acc[0][k] = inner(normed[:, lanes], low_grads[...], 0, 0).astype(bf16)
+
+        wide_grad(3)
+        weights.corners(0)
+
+        @pl.loop(0, blocks)
+        def _(i):
+            at = pl.ds(pl.multiple_of(i * block, block), block)
+            values = inner(low_grads[at], wide_ref[...], 1, 1).astype(bf16)
+            grads[pl.ds(2 * i, 2)] = values.reshape(2, tok_rows, width)
+
+        flow.begin()
+        wide_grad(2)
+        wide_grad(1)
+        second.stage3(1)
+        second.chain(0)
+        flow.stage3(0)
+        weights.sides(0)
+        flow.stage3(1)
+        wide_grad(0)
+        flow.chain(0)
+        second.stage3(2)
+        second.chain(1)
+        second.chain(2)
+        flow.stage3(2)
+        flow.chain(1)
+        weights.total(0)
+        weights.hand_out_wide()
+        flow.chain(2)
+        flow.stage3(3)
+        second.stage3(3)
+        weights.total(1)
+        weights.hand_out_tall()
+        flow.final()
+
+        values = tok[...].astype(f32)
+        scaled = values * lax.rsqrt(jnp.mean(values * values, axis=1, keepdims=True) + NORM_EPSILON)
+        attention_row = jnp.sum(scaled * flow.sum[...], axis=0, keepdims=True)
+        for to in range(32):
+            lanes = slice(to * own_rows, (to + 1) * own_rows)
+            deals[to, 0:1, :own_rows] = attention_row[:, lanes]
+            deals[to, 3:4, :own_rows] = feature_ref[:, lanes]
+        deal.begin()
+        second.final()
+        logits.finish()
+        weights.finish()
+        deal.finish()
+        total = dealt[0]
+        for index in range(1, 32):
+            total = total + dealt[index]
+        gain_out[...] = total
+
+    shapes = [
+        jax.ShapeDtypeStruct((32,) + logit_grad.shape, logit_grad.dtype),
+        jax.ShapeDtypeStruct((height, width), f32),
+        jax.ShapeDtypeStruct((height, width), f32),
+        jax.ShapeDtypeStruct((tok_rows, width), f32),
+        jax.ShapeDtypeStruct((3, own_rows, width), bf16),
+        jax.ShapeDtypeStruct((own_rows, width), bf16),
+        jax.ShapeDtypeStruct((8, 128), f32),
+    ]
+    scratch = [
+        pltpu.VMEM((8, tok_rows, width), bf16),
+        pltpu.VMEM((tok_rows, width), bf16),
+        pltpu.VMEM(wide.shape, bf16),
+        pltpu.VMEM(tall.shape, bf16),
+        pltpu.VMEM((rows, width), bf16),
+        pltpu.VMEM((rows, 2 * share), f32),
+        pltpu.VMEM((rows, 3 * share), bf16),
+        pltpu.VMEM((rows, share), bf16),
+        pltpu.VMEM((rows, share), bf16),
+        pltpu.VMEM((rows, share), f32),
+        pltpu.VMEM((rows, share), f32),
+        pltpu.VMEM((rows, share), f32),
+        pltpu.VMEM((rows, 3 * share), bf16),
+        pltpu.VMEM((8, rows), f32),
+        pltpu.VMEM((8, 8, rows), f32),
+        pltpu.VMEM((32, 8, 128), f32),
+        pltpu.VMEM((32, 8, 128), f32),
+        pltpu.VMEM(tall.shape, bf16),
+        pltpu.SemaphoreType.DMA((7,)),
+        pltpu.SemaphoreType.DMA((8,)),
+        pltpu.SemaphoreType.DMA((8,)),
+    ]
+    args = (grad, logit_grad, out_part, tokens, gain, feature_row, wide, tall, head_gains, cosine, sine)
+    return hbm_call(
         kernel,
-        out_shape=jax.ShapeDtypeStruct(values.shape, values.dtype),
-        in_specs=[pl.BlockSpec(memory_space=pltpu.VMEM)],
-        out_specs=pl.BlockSpec(memory_space=pltpu.VMEM),
-        scratch_shapes=[
-            pltpu.VMEM((8,) + values.shape, values.dtype),
-            pltpu.SemaphoreType.DMA((8,)),
-            pltpu.SemaphoreType.DMA((8,)),
-        ],
-        compiler_params=pltpu.CompilerParams(collective_id=collective_id, has_side_effects=True),
-        name=name,
-    )(values)
-
-
-def deal_sum(values, collective_id):
-    def kernel(src, out, landed, send, recv, local):
-        place = Place()
-        entry_barrier(place, "all")
-        flow = DealFlow(place, src, landed, send, recv, local)
-        flow.begin()
-        flow.finish()
-        total = landed[0]
-        for index in range(1, 32):
-            total = total + landed[index]
-        out[...] = total
-
-    return pl.pallas_call(
-        kernel,
-        out_shape=jax.ShapeDtypeStruct(values.shape[1:], values.dtype),
-        in_specs=[pl.BlockSpec(memory_space=pltpu.VMEM)],
-        out_specs=pl.BlockSpec(memory_space=pltpu.VMEM),
-        scratch_shapes=[pltpu.VMEM(values.shape, values.dtype)] + DealFlow.scratch(),
-        compiler_params=pltpu.CompilerParams(collective_id=collective_id, has_side_effects=True),
-        name="gain_gradients",
-    )(values)
+        shapes,
+        scratch + flow_scratch,
+        "attention_back",
+        2,
+        args + tuple(kept),
+        None,
+        (4, 5, 8, 9, 10, 15, 16),
+        (6,),
+    )
 
 
 def product(left, right, sums, batches=((), ()), out=jnp.float32):
     return lax.dot_general(left, right, (sums, batches), preferred_element_type=out)
-
-
-def shift_line(rows, step):
-    size = lax.axis_size(SP)
-    return lax.ppermute(rows, SP, [(i, (i + step) % size) for i in range(size)])
-
-
-HEAD_BATCH = ((1,), (1,))
-BATCH = ((0,), (0,))
-
-
-def rotate_heads(values, cosine, sine):
-    rows, width = values.shape
-    heads = values.reshape(rows, width // HEAD_DIM, HEAD_DIM)
-    return rotate(heads, cosine, sine).reshape(rows, width)
 
 
 def body_fast(
@@ -1904,28 +2048,26 @@
     column = lax.axis_index(BLK) * 4 + lax.axis_index(SP)
     f32, bf16 = jnp.float32, jnp.bfloat16
 
-    gains = jnp.stack([attention_gain, query_gain, key_gain, feature_gain], axis=1)
+    gains = jnp.stack([attention_gain, query_gain, key_gain, feature_gain])
     named_here = routes.astype(bf16).reshape(own_rows, tok_rows * TOPK // own_rows)
-    filled = EXPERTS + 4 + named_here.shape[1]
-    small = jnp.concatenate(
-        [router_weight, gains, named_here, jnp.zeros((own_rows, 128 - filled), bf16)], axis=1
-    )
+    filled = EXPERTS + named_here.shape[1]
+    small = jnp.concatenate([router_weight, named_here], axis=1)
+    small = jnp.concatenate([small, jnp.pad(gains, ((0, 28), (0, filled - own_rows)))], axis=0)
+    small = jnp.pad(small, ((0, 0), (0, 128 - filled)))
     tokens_all, small_all, cotangent_all, wide_weight, tall_weight = opening_call(
         tokens, small, cotangent, query_weight, key_weight, value_weight, output_weight
     )
-    routes_all = small_all[:, :, EXPERTS + 4 : filled].astype(jnp.int32).reshape(devices, tok_rows, TOPK)
-    small_all = small_all.reshape(model_width, 128)
-    router_full = small_all[:, :EXPERTS]
-    gain_all = small_all[:, EXPERTS : EXPERTS + 4].astype(f32)
-    gain_attention, gain_feature = gain_all[:, 0], gain_all[:, 3]
-    gain_share = lax.dynamic_slice_in_dim(gain_all, column * share, share, axis=0)
-    gain_query, gain_key = gain_share[:, 1], gain_share[:, 2]
+    routes_all = small_all[:, :own_rows, EXPERTS:filled].astype(jnp.int32).reshape(devices, tok_rows, TOPK)
+    router_full = small_all[:, :own_rows, :EXPERTS].reshape(model_width, EXPERTS)
+    gain_all = small_all[:, own_rows : own_rows + 4, :own_rows].astype(f32)
+    gain_all = gain_all.transpose(1, 0, 2).reshape(4, model_width)
+    gain_attention, gain_feature = gain_all[0], gain_all[3]
+    head_gains = lax.dynamic_slice_in_dim(gain_all[1:3], column * share, share, axis=1)
 
     half_cos, half_sin = rope_tables(jnp.arange(seq_rows, dtype=jnp.int32), HEAD_DIM)
     cosine = jnp.concatenate([half_cos, half_cos], axis=1)
     sine = jnp.concatenate([-half_sin, half_sin], axis=1)
-    head_gains = gain_share[:, 1:3].T
-    normed_all, unit_rows, head_rows, context, scales, logs, attended, cotangent_all = attention_call(
+    *kept, attended, cotangent_all = attention_call(
         tokens_all,
         gain_attention[None],
         wide_weight,
@@ -1936,16 +2078,6 @@
         cotangent,
         cotangent_all,
     )
-    query_u, key_u = unit_rows[:, :share], unit_rows[:, share:]
-    queries, keys, values = head_rows[:, :share], head_rows[:, share : 2 * share], head_rows[:, 2 * share :]
-    query_r, key_r = scales[:, :1], scales[:, 1:2]
-
-    def split(rows):
-        return rows.reshape(seq_rows, heads_here, HEAD_DIM)
-
-    places_row = jnp.arange(seq_rows, dtype=jnp.int32)
-    causal = places_row[None, :] <= places_row[:, None]
-
     tokens_f = tokens.astype(f32)
     residual = tokens_f + attended
     features_f, feature_pull = jax.vjp(norm_apply, residual, gain_feature)
@@ -1964,10 +2096,9 @@
     places = places.transpose(0, 2, 1, 3).reshape(pairs, experts_here, pair_rows)
     cotangent_all = cotangent_all.reshape(pairs, pair_rows, model_width)
     features_all, probs_all, grad_rows, plain_grads = features_call(
-        features, router_probs.reshape(tok_rows // 2, 2 * EXPERTS), places, cotangent_all, down_weight, per
-    )
-    probs_all = probs_all.reshape(pairs, pair_rows, EXPERTS)
-    probs_here = lax.dynamic_slice_in_dim(probs_all, first_expert, experts_here, axis=2).transpose(0, 2, 1)
+        features, router_probs.T, places, cotangent_all, down_weight, per
+    )
+    probs_here = lax.dynamic_slice_in_dim(probs_all, first_expert, experts_here, axis=1)
     features_all = features_all.reshape(pairs, pair_rows, model_width)
     expert_rows, row_probs = pick_rows(places, probs_here, features_all, per)
     weighted_hidden, gate_grad, up_grad, input_rows, row_grads = run_experts(
@@ -1989,76 +2120,29 @@
     residual_part, feature_gain_grad = feature_pull(feature_grad)
     residual_grad = cotangent.astype(f32) + residual_part
     attended_grad = residual_grad.astype(bf16)
-    grads_all, logit_all, first_sums = residual_grad_call(
-        attended_grad, logit_grad.reshape(tok_rows // 2, 2 * EXPERTS), out_part
-    )
-
-    def along_line(sums):
-        total = lax.dynamic_index_in_dim(sums, lax.axis_index(SP), axis=0, keepdims=False).astype(f32)
-        for j in (1, 2, 3):
-            block = lax.dynamic_index_in_dim(sums, (lax.axis_index(SP) + j) % 4, axis=0, keepdims=False)
-            total = total + shift_line(block, j).astype(f32)
-        return total
-
-    first_half = along_line(first_sums)
+    logit_all, first_half, second_half, normed_grad, wide_back, tall_back, gain_sums = attention_back_call(
+        attended_grad,
+        logit_grad.reshape(tok_rows // 2, 2 * EXPERTS),
+        out_part,
+        tokens,
+        gain_attention[None],
+        feature_gain_grad[None],
+        wide_weight,
+        tall_weight,
+        head_gains,
+        cosine,
+        sine,
+        kept,
+    )
     own_index = (lax.axis_index(DP) * 2 + lax.axis_index(BLK)) * 4 + lax.axis_index(SP)
     own_features = lax.dynamic_slice_in_dim(
         features_all.reshape(devices * tok_rows, model_width), own_index * own_rows, own_rows, axis=1
     )
     router_grad = product(own_features, logit_all.reshape(devices * tok_rows, EXPERTS), ((0,), (0,)))
 
-    grads_all = grads_all.reshape(seq_rows, model_width)
-    tall_grad = product(context, grads_all, ((0,), (0,))).astype(bf16)
-    context_grad = product(grads_all, tall_weight, ((1,), (1,))).astype(bf16)
-    scores = product(split(queries), split(keys), ((2,), (2,)), HEAD_BATCH) * score_scale
-    attn_weights = jnp.where(causal[None], jnp.exp(scores - logs[:, :heads_here].T[:, :, None]), 0.0)
-    attn_low = attn_weights.astype(bf16)
-    prob_dots = product(split(context_grad), split(values), ((2,), (2,)), HEAD_BATCH)
-    row_delta = jnp.sum(attn_weights * prob_dots, axis=-1, keepdims=True)
-    score_grad = (attn_weights * (prob_dots - row_delta)).astype(bf16)
-    query_back = product(score_grad, split(keys), ((2,), (0,)), ((0,), (1,))).transpose(1, 0, 2) * score_scale
-    key_back = product(score_grad, split(queries), ((1,), (0,)), ((0,), (1,))).transpose(1, 0, 2) * score_scale
-    value_low = product(attn_low, split(context_grad), ((1,), (0,)), ((0,), (1,))).transpose(1, 0, 2)
-    value_low = value_low.astype(bf16).reshape(seq_rows, share)
-
-    def unrotate(grad):
-        grad = grad.astype(bf16).astype(f32).reshape(seq_rows, share)
-        return rotate_heads(grad, half_cos, -half_sin)
-
-    query_back, key_back = unrotate(query_back), unrotate(key_back)
-    query_gain_grad = jnp.sum(query_back * query_u, axis=0)
-    key_gain_grad = jnp.sum(key_back * key_u, axis=0)
-    query_w, key_w = query_back * gain_query, key_back * gain_key
-    dots = jnp.stack([jnp.sum(query_w * query_u, axis=1), jnp.sum(key_w * key_u, axis=1)])
-    dots, first_half = lax.optimization_barrier((dots, first_half))
-    dots = column_sum(dots.reshape(16, seq_rows // 8), "dot_sums", 8).reshape(2, seq_rows) / model_width
-    query_low = (query_r * (query_w - query_u * dots[0][:, None])).astype(bf16)
-    key_low = (key_r * (key_w - key_u * dots[1][:, None])).astype(bf16)
-    linear_grad = jnp.concatenate([query_low, key_low, value_low], axis=1)
-    wide_grad = product(normed_all, linear_grad, ((0,), (0,))).astype(bf16)
-    normed_part = product(linear_grad, wide_weight, ((1,), (1,))).astype(bf16)
-    normed_grad, wide_back, tall_back, second_sums = closing_call(
-        normed_part.reshape(column_size, tok_rows, model_width),
-        wide_grad.reshape(4, model_width // 4, 3 * share),
-        tall_grad.reshape(4, share // 4, model_width),
-        out_part,
-    )
-    _, attention_pull = jax.vjp(norm_apply, tokens_f, gain_attention)
-    tokens_part, attention_gain_grad = attention_pull(normed_grad)
-    input_gradient = residual_grad + tokens_part
-    def spread(share_grad):
-        placed = jnp.zeros((model_width,), f32)
-        return lax.dynamic_update_slice(placed, share_grad, (column * share,))
-
-    gain_grads = jnp.stack(
-        [attention_gain_grad, spread(query_gain_grad), spread(key_gain_grad), feature_gain_grad]
-    )
-    gain_grads = gain_grads.reshape(4, devices, own_rows).transpose(1, 0, 2)
-    gain_grads = jnp.pad(gain_grads, ((0, 0), (0, 4), (0, 128 - own_rows)))
-    gain_sums = deal_sum(gain_grads, 9)
-    second_sums, gain_sums, weighted_hidden = lax.optimization_barrier((second_sums, gain_sums, weighted_hidden))
-    mixture = jnp.concatenate([first_half, along_line(second_sums)], axis=0)
-    block_output = (residual + mixture).astype(bf16)
+    _, attention_pull = jax.vjp(lambda values: norm_apply(values, gain_attention), tokens_f)
+    input_gradient = residual_grad + attention_pull(normed_grad)[0]
+    block_output = (residual + jnp.concatenate([first_half, second_half], axis=0)).astype(bf16)
     gate_grad_local, up_grad_local, down_grad_local = expert_weight_grads(
         expert_rows, grad_rows, weighted_hidden, gate_grad, up_grad
     )

time: 739 us -> 677 us (0.916)
  local copies, waits for them, and re-layouts: 40.7 us -> 9.01 us
  matrix products: 35.9 us -> 5.43 us
  Pallas kernels: 611 us -> 631 us
  other arithmetic: 31.4 us -> 20.8 us
  starting transfers between devices: 8.56 us -> 0 us
    pallas_call x6 -> x5, Pallas kernels: 491 us -> 531 us  [hbm_call(): pl.pallas_call(kernel, out_shape=shapes, in_specs=[pl.BlockSpec(memory_sp...]
    dot_general x11 -> x2, matrix products: 33.8 us -> 2.73 us  [product(): lax.dot_general(left, right, (sums, batches), preferred_element_type=out)]
    pallas_call x2 -> x0, Pallas kernels: 20 us -> none  [the longest x1 12.8 us: deal_sum(): pl.pallas_call(kernel, out_shape=jax.ShapeDtypeStruct(values.shape[1:], v...]
    ppermute x6 -> x0, starting transfers between devices: 8.56 us -> none  [shift_line(): return lax.ppermute(rows, SP, [(i, (i + step) % size) for i in range(size)])]
    reshape x8 -> x0, local copies, waits for them, and re-layouts: 8.46 us -> none  [the longest x1 2.04 us: body_fast(): value_low = value_low.astype(bf16).reshape(seq_rows, share)]
  transfers between devices with their start and end apart: 6 -> 0, of which waited for: 0 -> 0; matrix products, arithmetic and copies ran while one was open for 7% -> 0% of each run, Pallas kernels for 5% -> 0%
where the time goes in v3:
time: 677 us; the launch traced here: 667 us
  Pallas kernels  631 us (93%)
  other arithmetic  20.8 us (3%)
  local copies, waits for them, and re-layouts  9.01 us (1%)
    pallas_call x5, Pallas kernels, hbm_call(): pl.pallas_call(kernel, out_shape=shapes, in_specs=[pl.BlockSpec(memory_sp...  531 us
    pallas_call x1, Pallas kernels, expert_weight_grads(): pl.pallas_call(kernel, out_shape=[jax.ShapeDtypeStruct((experts, width, h...  35.4 us
    pallas_call x1, Pallas kernels, run_experts(): pl.pallas_call(kernel, out_shape=[narrow, narrow, narrow, jax.ShapeDtypeS...  34.4 us
    pallas_call x1, Pallas kernels, put_rows_back(): pl.pallas_call(kernel, out_shape=[jax.ShapeDtypeStruct((pairs, pair_rows,...  14.8 us
    pallas_call x1, Pallas kernels, pick_rows(): pl.pallas_call(kernel, out_shape=[jax.ShapeDtypeStruct((experts, pairs *...  14.6 us

profile of v3, /device:TPU:0, one launch (start us, length us, event | category | flops | bytes accessed | tf_op | source)
XLA Modules:
  0.0 667.1 jit_solution(16013471628021439661)
XLA Ops:
  2.3 1.4 fusion.19.sml
  3.7 1.9 fusion.8
  5.6 1.3 pad_maximum_fusion
  6.9 79.8 %opening.1 = (bf16[8,128,2048]{2,1,0:T(8,128)(2,1)}, bf16[32,96,128]{2,1,0:T(8,128)(2,1)}, bf16[32,128,2048]{2,1,0:T(8,128)(2,1)}, bf16[2048,768]{1,0:T(8,128)(2,1)}, bf16[256,2048]{1,0:T(8,128)(2,1)}) custom-call(bf16[128,2048]{1,0:T(8,128)(2,1)} %refs_3_.1, bf16[96,128]{1,0:T(8,128)(2,1)} %fusion.19.sml, bf16[128,2048]{1,0:T(8,128)(2,1)} %cot.3, ...), custom_call_target="tpu_custom_call" | custom-call | tf_op jit(solution)/shard_map/opening/pallas_call | solution.py:1342
  89.3 1.1 slice.55
  90.3 1.3 slice_convert_fusion
  93.7 96.0 %attention.1 = (bf16[1024,2048]{1,0:T(8,128)(2,1)}, f32[1024,512]{1,0:T(8,128)}, bf16[1024,768]{1,0:T(8,128)(2,1)}, bf16[1024,256]{1,0:T(8,128)(2,1)}, f32[1024,...) custom-call(bf16[8,128,2048]{2,1,0:T(8,128)(2,1)} %get-tuple-element, ...), custom_call_target="tpu_custom_call", output_to_operand_aliasing={{7}: (8, {})} | custom-call | tf_op jit(solution)/shard_map/attention/pallas_call | solution.py:1342
  189.7 1.4 multiply_reduce_fusion.2
  192.3 80.9 %features.1 = (bf16[32,128,2048]{2,1,0:T(8,128)(2,1)}, f32[32,64,128]{2,1,0:T(8,128)}, bf16[4,768,2048]{2,1,0:T(8,128)(2,1)}, f32[4,768,512]{2,1,0:T(8,128)}) custom-call(bf16[128,2048]{1,0:T(8,128)(2,1)} %copy-done.3, f32[64,128]{1,0:T(8,128)} %fusion.35.prob_ref, s32[16,4,256]{2,1,0:T(4,128)} %reshape.138.place_ref, bf16[16,256,2048]{2,1,0:T(8,128)(2,1)} %bitcast.49, ...), custom_call_target="tpu_custom_call" | custom-call | tf_op jit(solution)/shard_map/features/pallas_call | solution.py:1342
  273.3 1.6 constant_dynamic-slice_fusion.prob_ref
  274.8 14.6 %pick_rows.1 = (bf16[4,768,2048]{2,1,0:T(8,128)(2,1)}, f32[4,768,1]{2,1,0:T(8,128)}) custom-call(s32[16,4,256]{2,1,0:T(4,128)} %reshape.138.place_ref, f32[32,4,128]{2,1,0:T(4,128)} %constant_dynamic-slice_fusion.prob_ref, bf16[16,256,2048]{2,1,0:T(8,128)(2,1)} %bitcast.50), custom_call_target="tpu_custom_call" | custom-call | tf_op jit(solution)/shard_map/pick_rows/pallas_call | solution.py:723
  289.4 34.4 %run_experts.1 = (bf16[4,768,512]{2,1,0:T(8,128)(2,1)}, bf16[4,768,512]{2,1,0:T(8,128)(2,1)}, bf16[4,768,512]{2,1,0:T(8,128)(2,1)}, bf16[4,768,2048]{2,1,0:T(8,128)(2,1)}, f32[4,768,1]{2,1,0:T(8,128)}) custom-call(bf16[4,768,2048]{2,1,0:T(8,128)(2,1)} %get-tuple-element.62.x, f32[4,768,512]{2,1,0:T(8,128)} %get-tuple-element.63.plain_ref, ...), custom_call_target="tpu_custom_call" | custom-call | tf_op jit(solution)/shard_map/run_experts/pallas_call | solution.py:812
  323.8 14.8 %put_rows_back.1 = (bf16[16,256,2048]{2,1,0:T(8,128)(2,1)}, f32[32,8,128]{2,1,0:T(8,128)}) custom-call(s32[16,4,256]{2,1,0:T(4,128)} %reshape.138.place_ref, bf16[4,768,2048]{2,1,0:T(8,128)(2,1)} %get-tuple-element.65.row_ref, f32[4,768,1]{2,1,0:T(8,128)} %get-tuple-element.66.grad_ref), custom_call_target="tpu_custom_call" | custom-call | tf_op jit(solution)/shard_map/put_rows_back/pallas_call | solution.py:763
  338.6 83.0 %experts_back.1 = (f32[128,2048]{1,0:T(8,128)}, f32[32,8,128]{2,1,0:T(8,128)}, bf16[16,256,2048]{2,1,0:T(8,128)(2,1)}) custom-call(bf16[32,128,2048]{2,1,0:T(8,128)(2,1)} %bitcast.53, f32[32,8,128]{2,1,0:T(8,128)} %get-tuple-element.68.dealt_ref, s32[16,4,256]{2,1,0:T(4,128)} %reshape.138.place_ref, bf16[4,768,512]{2,1,0:T(8,128)(2,1)} %get-tuple-element.69.hidden_ref.low, ...), custom_call_target="tpu_custom_call" | custom-call | tf_op jit(solution)/shard_map/experts_back/pallas_call | solution.py:1342
  421.6 0.9 slice_reduce_fusion
  422.6 2.4 multiply_reduce_fusion
  425.8 1.2 fusion.36.refs_0_
  426.9 191.7 %attention_back.1 = (bf16[32,64,128]{2,1,0:T(8,128)(2,1)}, f32[64,2048]{1,0:T(8,128)}, f32[64,2048]{1,0:T(8,128)}, f32[128,2048]{1,0:T(8,128)}, bf16[3,64,2048]{...) custom-call(bf16[128,2048]{1,0:T(8,128)(2,1)} %fusion.36.refs_0_, bf16[64,128]{1,0:T(8,128)(2,1)} %reshape.144.refs_1_, ...), custom_call_target="tpu_custom_call" | custom-call | tf_op jit(solution)/shard_map/attention_back/pallas_call | solution.py:1342
  618.6 1.6 fusion.3
  620.2 3.1 fusion.2
  624.7 1.6 reshape.147
  626.4 2.6 fusion.6
  628.9 2.3 bitcast_convert_fusion
  631.2 35.4 %expert_weight_grads.1 = (f32[4,2048,512]{2,1,0:T(8,128)}, f32[4,2048,512]{2,1,0:T(8,128)}, f32[4,512,2048]{2,1,0:T(8,128)}) custom-call(bf16[4,768,2048]{2,1,0:T(8,128)(2,1)} %get-tuple-element.62.x, bf16[4,768,2048]{2,1,0:T(8,128)(2,1)} %get-tuple-element.86.c, bf16[4,768,512]{2,1,0:T(8,128)(2,1)} %get-tuple-element.69.hidden_ref.low, ...), custom_call_target="tpu_custom_call" | custom-call | flops 19327352832 | bytes 100663296 | tf_op jit(solution)/shard_map/expert_weight_grads/pallas_call | solution.py:1007
  (49 shorter events, 9.6 us)
Async XLA Ops:
  93.7 96.0 %copy-start = (bf16[128,2048]{1,0:T(8,128)(2,1)S(1)}, bf16[128,2048]{1,0:T(8,128)(2,1)}, u32[]{:S(2)}) copy-start(bf16[128,2048]{1,0:T(8,128)(2,1)} %refs_3_.1) | copy-start | bytes 1572868
  191.3 1.0 copy-start.3
  338.6 87.2 %copy-start.2 = (bf16[128,2048]{1,0:T(8,128)(2,1)S(1)}, bf16[128,2048]{1,0:T(8,128)(2,1)}, u32[]{:S(2)}) copy-start(bf16[128,2048]{1,0:T(8,128)(2,1)} %cot.3) | copy-start | bytes 1572868
  426.9 191.7 %copy-start.1 = (bf16[128,2048]{1,0:T(8,128)(2,1)S(1)}, bf16[128,2048]{1,0:T(8,128)(2,1)}, u32[]{:S(2)}) copy-start(bf16[128,2048]{1,0:T(8,128)(2,1)} %refs_3_.1) | copy-start | bytes 1572868
  618.6 4.7 copy-start.5
  618.6 5.3 copy-start.4

commit v4 on v3

--- a/solution.py
+++ b/solution.py
@@ -3,6 +3,7 @@
 
 import jax
 import jax.numpy as jnp
+import numpy as np
 from jax import lax
 from jax.experimental import pallas as pl
 from jax.experimental.pallas import tpu as pltpu
@@ -340,23 +341,6 @@
         if not self.others:
             self.own_copy().wait()
 
-    def steps(self):
-        return [
-            self.begin,
-            lambda: self.along(1),
-            lambda: self.turn(0),
-            lambda: self.along(2),
-            lambda: self.turn(1),
-            lambda: self.along(3),
-            lambda: self.corner(0),
-            lambda: self.turn(2),
-            lambda: self.corner(1),
-            lambda: self.turn(3),
-            lambda: self.corner(2),
-            lambda: self.corner(3),
-            self.finish,
-        ]
-
 
 class PlaneFlow(GatherFlow):
     def __init__(self, place, blocks, out, send, recv, local):
@@ -443,7 +427,7 @@
 class ScatterFlow:
     SENDS = 16 + 8 + 8 + 4 + 4
     RECVS = 16 + 8 + 8 + 4 + 4
-    LOCALS = 20
+    LOCALS = 16
 
     def __init__(self, place, part, out, scratch, full, band=None):
         self.p, self.part, self.out, self.full = place, part, out, full
@@ -452,6 +436,7 @@
         else:
             (self.acc, self.near, self.line_in, self.sum, self.send, self.recv, self.local) = scratch
         self.columns = 4 if full else 1
+        self.left = False
         first, self.rows = band or (0, part.shape[1])
         self.band = pl.ds(first, self.rows)
         self.half = self.rows // 2
@@ -542,12 +527,28 @@
             self.p.at(z=jnp.maximum(self.p.z - 1, 0)),
         )
 
-    def begin(self):
+    def begin(self, columns=None):
         for i in range(4):
             s = self.order(i)
-            for k in reversed(range(self.columns)):
+            for k in columns or reversed(range(self.columns)):
                 self.core(k, s).start()
                 self.load(k, s).start()
+
+    def unsent(self):
+        return range(self.columns)
+
+    def leave(self, s):
+        self.half_x(s).wait_send()
+        self.half_y(s).wait_send()
+        self.side_x(s).wait_send()
+        self.side_y(s).wait_send()
+
+    def leave_all(self):
+        self.left = True
+
+        @pl.loop(0, 4)
+        def _(s):
+            self.leave(s)
 
     def arrive(self, k, s):
         self.load(k, s).wait()
@@ -646,13 +647,10 @@
 
         @pl.loop(0, 4)
         def _(s):
-            for k in range(self.columns):
+            for k in self.unsent():
                 self.core(k, s).wait_send()
-            if self.full:
-                self.half_x(s).wait_send()
-                self.half_y(s).wait_send()
-                self.side_x(s).wait_send()
-                self.side_y(s).wait_send()
+            if self.full and not self.left:
+                self.leave(s)
 
             @pl.when(s > z)
             def _():
@@ -664,25 +662,27 @@
 
         done.wait()
 
-    def steps(self):
-        plan = [
-            (self.stage1, 0),
-            (self.stage1, 1),
-            (self.stage2, 0),
-            (self.stage1, 2),
-            (self.stage2, 1),
-            (self.stage3, 0),
-            (self.stage1, 3),
-            (self.stage2, 2),
-            (self.stage3, 1),
-            (self.chain, 0),
-            (self.stage2, 3),
-            (self.stage3, 2),
-            (self.chain, 1),
-            (self.chain, 2),
-            (self.stage3, 3),
-        ]
-        return [self.begin] + [functools.partial(act, i) for act, i in plan] + [self.final]
+
+class MadeFlow(ScatterFlow):
+    def __init__(self, place, out, scratch, stage):
+        self.stage = stage
+        super().__init__(place, stage.at[0], out, scratch, True)
+
+    def core(self, k, s):
+        return remote(
+            self.stage.at[k % 2, s],
+            self.near.at[k, s],
+            self.send.at[4 * k + s],
+            self.recv.at[4 * k + s],
+            self.p.at(0, 1 - self.p.blk),
+        )
+
+    def unsent(self):
+        return (0, 1)
+
+    def arrive(self, k, s):
+        self.core(k, s).wait_recv()
+        return [self.acc.at[k, s], self.near.at[k, s]]
 
 
 def local_params():
@@ -741,46 +741,6 @@
     )(places, probs, features)
 
 
-def put_rows_back(places, rows, row_grads):
-    pairs, experts, pair_rows = places.shape
-    _, slots, width = rows.shape
-    per = slots // pairs
-    step = 2
-    half = pair_rows // 2
-
-    def kernel(place_ref, row_ref, grad_ref, sum_ref, prob_ref):
-        for i in range(step):
-            at = pl.ds(i * per, per)
-            gathered = jnp.concatenate([row_ref[e, at] for e in range(experts)], axis=0)
-            sum_ref[i] = inner(one_hot(place_ref[i], per), gathered, 0, 0).astype(sum_ref.dtype)
-            prob_ref[2 * i : 2 * i + 2] = jnp.zeros((2, 8, half), jnp.float32)
-            for e in range(experts):
-                hot = is_place(place_ref[i, e : e + 1], per)
-                line = jnp.sum(jnp.where(hot, grad_ref[e, at], 0.0), axis=0, keepdims=True)
-                prob_ref[2 * i, e : e + 1] = line[:, :half]
-                prob_ref[2 * i + 1, e : e + 1] = line[:, half:]
-
-    return pl.pallas_call(
-        kernel,
-        out_shape=[
-            jax.ShapeDtypeStruct((pairs, pair_rows, width), rows.dtype),
-            jax.ShapeDtypeStruct((2 * pairs, 8, half), jnp.float32),
-        ],
-        grid=(pairs // step,),
-        in_specs=[
-            pl.BlockSpec((step, experts, pair_rows), lambda p: (p, 0, 0)),
-            pl.BlockSpec((experts, step * per, width), lambda p: (0, p, 0)),
-            pl.BlockSpec((experts, step * per, 1), lambda p: (0, p, 0)),
-        ],
-        out_specs=[
-            pl.BlockSpec((step, pair_rows, width), lambda p: (p, 0, 0)),
-            pl.BlockSpec((2 * step, 8, half), lambda p: (p, 0, 0)),
-        ],
-        compiler_params=local_params(),
-        name="put_rows_back",
-    )(places, rows, row_grads)
-
-
 def run_experts(rows, plain_grads, probs, gate_weight, up_weight):
     experts, slots, width = rows.shape
     hidden = gate_weight.shape[2]
@@ -913,6 +873,79 @@
         for group in (groups - 2, groups - 1):
             for copy in self.stores(group, group % 2):
                 copy.wait()
+
+
+class PutWork:
+    def __init__(self, place, places, source, row_grads, flow, deals, scratch):
+        self.p, self.places, self.source, self.row_grads = place, places, source, row_grads
+        self.flow, self.deals = flow, deals
+        self.rows, self.sems = scratch
+        self.experts, self.per = self.rows.shape[1:3]
+
+    @staticmethod
+    def scratch(source, per):
+        experts, _, width = source.shape
+        return [pltpu.VMEM((2, experts, per, width), source.dtype), pltpu.SemaphoreType.DMA((2,))]
+
+    def pair(self, k, unit):
+        side = unit // 2
+        blk = side * self.p.blk + (1 - side) * (1 - self.p.blk)
+        return self.p.column(k) * 4 + blk * 2 + unit % 2
+
+    def load(self, k, unit, slot):
+        at = pl.ds(pl.multiple_of(self.pair(k, unit) * self.per, self.per), self.per)
+        return pltpu.make_async_copy(self.source.at[:, at], self.rows.at[slot], self.sems.at[slot])
+
+    def column(self, k):
+        flow = self.flow
+        if k < 2:
+
+            @pl.loop(0, 4)
+            def _(s):
+                flow.core(k + 2, s).wait_send()
+
+        @pl.loop(0, 4)
+        def _(unit):
+            slot = unit % 2
+
+            @pl.when(unit < 3)
+            def _():
+                self.load(k, unit + 1, 1 - slot).start()
+
+            if k:
+
+                @pl.when(unit == 3)
+                def _():
+                    self.load(k - 1, 0, 1 - slot).start()
+
+            self.load(k, unit, slot).wait()
+            pair = self.pair(k, unit)
+            places = self.places[pair]
+            rows = jnp.concatenate([self.rows[slot, e] for e in range(self.experts)], axis=0)
+            summed = inner(one_hot(places, self.per), rows, 0, 0).astype(self.rows.dtype)
+            summed = summed.reshape(2, summed.shape[0] // 2, summed.shape[1])
+            blocks = pl.ds(2 * (unit % 2), 2)
+
+            @pl.when(unit < 2)
+            def _():
+                flow.stage[k % 2, blocks] = summed
+
+            @pl.when(unit >= 2)
+            def _():
+                flow.acc[k, blocks] = summed
+
+            at = pl.ds(pl.multiple_of(pair * self.per, self.per), self.per)
+            half = places.shape[1] // 2
+            for e in range(self.experts):
+                hot = is_place(places[e : e + 1], self.per)
+                line = jnp.sum(jnp.where(hot, self.row_grads[e, at], 0.0), axis=0, keepdims=True)
+                self.deals[2 * pair, e : e + 1] = line[:, :half]
+                self.deals[2 * pair + 1, e : e + 1] = line[:, half:]
+
+            @pl.when(unit == 1)
+            def _():
+                for s in range(4):
+                    flow.core(k, s).start()
 
 
 class OutputWork:
@@ -1157,22 +1190,23 @@
 
 
 class SumsFlow:
-    SENDS = 8 + 24 + 1
-    RECVS = 8 + 8 + 1
-    LOCALS = 12
+    SENDS = 12 + 24 + 1
+    RECVS = 12 + 16 + 1
+    LOCALS = 4
 
     def __init__(self, place, wide_out, tall_out, scratch):
         self.p = place
-        self.outs = (wide_out, tall_out)
-        self.acc, self.half_in, self.side_in = scratch[0:2], scratch[2:4], scratch[4:6]
-        self.send, self.recv, self.local = scratch[6:9]
+        self.wide_out, self.tall_out = wide_out, tall_out
+        self.acc, self.half_in, self.side_in = scratch[0:3], scratch[3:6], scratch[6:9]
+        self.send, self.recv, self.local = scratch[9:12]
         self.rows = tall_out.shape[0]
+        self.share = wide_out.shape[2] // 8
 
     @staticmethod
-    def scratch(wide, tall):
+    def scratch(arrays):
         shapes = []
         for kind in ((4, 1), (2, 2), (2, 1)):
-            for rows, width in (wide, tall):
+            for rows, width in arrays:
                 shapes.append(pltpu.VMEM((kind[0], rows // kind[1], width), jnp.bfloat16))
         return shapes + [
             pltpu.SemaphoreType.DMA((SumsFlow.SENDS,)),
@@ -1195,30 +1229,39 @@
             self.acc[which].at[k], self.side_in[which].at[k - 1], self.send.at[slot], self.recv.at[slot], self.p.at(k)
         )
 
+    def piece(self, to, i):
+        rows = pl.ds(pl.multiple_of(to * self.rows, self.rows), self.rows)
+        dst = self.wide_out.at[i, :, pl.ds(pl.multiple_of(self.p.col * self.share, self.share), self.share)]
+        if i == 2:
+            return self.acc[2].at[0, rows], dst
+        return self.acc[0].at[0, rows, pl.ds(i * self.share, self.share)], dst
+
     def deal(self, step, i):
         to = (self.p.col + step) % 8
         src, dst = self.piece(to, i)
         return remote(
-            src, dst, self.send.at[8 + 3 * step + i], self.recv.at[8 + self.p.col], (self.p.dp, to // 4, to % 4)
+            src,
+            dst,
+            self.send.at[12 + 3 * step + i],
+            self.recv.at[12 + 8 * (i // 2) + self.p.col],
+            (self.p.dp, to // 4, to % 4),
         )
-
-    def piece(self, to, i):
-        share = self.outs[0].shape[2] // 8
-        rows = pl.ds(pl.multiple_of(to * self.rows, self.rows), self.rows)
-        dst = self.outs[0].at[i, :, pl.ds(pl.multiple_of(self.p.col * share, share), share)]
-        return self.acc[0].at[0, rows, pl.ds(i * share, share)], dst
 
     def keep(self, i):
         src, dst = self.piece(self.p.col, i)
-        return pltpu.make_async_copy(src, dst, self.local.at[8 + i])
+        return pltpu.make_async_copy(src, dst, self.local.at[i])
 
     def swap(self):
         return remote(
-            self.acc[1].at[0], self.outs[1], self.send.at[32], self.recv.at[16], (self.p.col // 2, self.p.col % 2, self.p.dp)
+            self.acc[1].at[0],
+            self.tall_out,
+            self.send.at[36],
+            self.recv.at[28],
+            (self.p.col // 2, self.p.col % 2, self.p.dp),
         )
 
     def stay(self):
-        return pltpu.make_async_copy(self.acc[1].at[0], self.outs[1], self.local.at[11])
+        return pltpu.make_async_copy(self.acc[1].at[0], self.tall_out, self.local.at[3])
 
     def at_home(self):
         return (self.p.col // 2 == self.p.dp) & (self.p.col % 2 == self.p.blk) & (self.p.z == self.p.dp)
@@ -1251,13 +1294,13 @@
         def _():
             self.swap().start()
 
-    def hand_out_wide(self):
+    def hand_out(self, weights):
         @pl.loop(1, 8)
         def _(step):
-            for i in range(3):
+            for i in weights:
                 self.deal(step, i).start()
 
-        for i in range(3):
+        for i in weights:
             self.keep(i).start()
 
     def finish(self):
@@ -1277,21 +1320,24 @@
         @pl.loop(1, 8)
         def _(step):
             col = (self.p.col + step) % 8
-            landed = self.acc[0].at[0, pl.ds(0, self.rows)]
-            remote(
-                landed, landed, self.send.at[0], self.recv.at[8 + col], self.p.at(0, 1 - self.p.blk)
-            ).wait_recv()
+            for which, landed in (
+                (0, self.acc[0].at[0, pl.ds(0, self.rows)]),
+                (1, self.acc[2].at[0, pl.ds(0, self.rows)]),
+            ):
+                remote(
+                    landed,
+                    landed,
+                    self.send.at[0],
+                    self.recv.at[12 + 8 * which + col],
+                    self.p.at(0, 1 - self.p.blk),
+                ).wait_recv()
             for i in range(3):
                 self.deal(step, i).wait_send()
 
-        for which in (1, 0):
+        for which in (1, 2, 0):
             for k in (1, 2):
                 self.corner(which, k).wait_send()
                 self.side(which, k).wait_send()
-
-    def steps(self):
-        idle = lambda: None
-        return [self.begin, self.sides, idle, idle, self.total, idle, idle, idle, idle, idle, idle, idle, idle, idle, idle, idle, self.finish]
 
 
 class DealFlow:
@@ -1338,7 +1384,7 @@
         return [self.begin] + [lambda: None] * (length - 2) + [self.finish]
 
 
-def hbm_call(kernel, shapes, scratch, name, collective_id, args, aliases=None, in_vmem=(), out_vmem=()):
+def hbm_call(kernel, shapes, scratch, name, collective_id, args, in_vmem=(), out_vmem=()):
     return pl.pallas_call(
         kernel,
         out_shape=shapes,
@@ -1349,7 +1395,6 @@
             pl.BlockSpec(memory_space=pltpu.VMEM if i in out_vmem else pl.ANY) for i in range(len(shapes))
         ],
         scratch_shapes=scratch,
-        input_output_aliases=aliases or {},
         compiler_params=pltpu.CompilerParams(
             collective_id=collective_id, has_side_effects=True, vmem_limit_bytes=VMEM_BYTES
         ),
@@ -1365,19 +1410,44 @@
     return gather_sems() + [pltpu.SemaphoreType.DMA((count,))]
 
 
-def opening_call(tokens, small, cotangent, query_weight, key_weight, value_weight, output_weight):
-    width = tokens.shape[1]
-    rows = query_weight.shape[0]
-
-    def kernel(tok, sml, cot, wq, wk, wv, wo, tok_out, sml_out, cot_out, wide, tall, *sems):
+def attention_call(
+    tokens, small, cotangent, query_weight, key_weight, value_weight, output_weight, cosine, sine, experts
+):
+    tok_rows, width = tokens.shape
+    own_rows = query_weight.shape[0]
+    rows = 8 * tok_rows
+    share = width // 8
+    heads = share // HEAD_DIM
+    block = 2 * tok_rows
+    blocks = rows // block
+    scale = 1.0 / math.sqrt(HEAD_DIM)
+    bf16, f32 = jnp.bfloat16, jnp.float32
+    line = ScatterFlow.scratch(tok_rows, width, bf16, False)
+
+    def kernel(tok, sml, cot, wq, wk, wv, wo, cos, sin, *refs):
+        outs, scratch = refs[:13], refs[13:]
+        normed_out, unit_out, row_out, context_out, scale_out, log_out = outs[:6]
+        attended, small_out, gathered_out, wide_out, tall_out, gains, place_out = outs[6:]
+        held, wide_ref, tall_ref, normed, unit, qkv, context, part, sums, landed = scratch[:10]
+        small_held, hits, normed_t, context_t, stores, send, recv = scratch[10:17]
+        rest = list(scratch[17:])
+
+        def take(count):
+            taken = rest[:count]
+            del rest[:count]
+            return taken
+
         place = Place()
         entry_barrier(place, "all")
-        weights = ColumnsFlow(place, (wq, wk, wv), wo, wide, tall, *sems[7:10])
-        line = GatherFlow(place, tok, tok_out, sems[0], sems[1], False)
-        params = GatherFlow(place, sml, sml_out, sems[2], sems[3], True, True)
-        plane = PlaneFlow(place, [(place.z, cot)], cot_out, *sems[4:7])
+        flow = ScatterFlow(place, part, attended, take(len(line)), False)
+        params = GatherFlow(place, sml, small_held, *take(2), True, True)
+        tokens_in = GatherFlow(place, tok, held, *take(2), False)
+        others = GatherFlow(place, cot, gathered_out, *take(2), True, others=True)
+        plane = PlaneFlow(place, [(place.z, cot)], gathered_out, *take(3))
+        weights = ColumnsFlow(place, (wq, wk, wv), wo, wide_ref, tall_ref, *take(3))
         params.begin()
         weights.begin()
+        sums[...] = jnp.zeros_like(sums)
         for d in range(1, 4):
             params.along(d)
         plane.begin()
@@ -1387,91 +1457,51 @@
         weights.settle(0)
         plane.turns()
         weights.settle(1)
-        line.begin()
+        tokens_in.begin()
         weights.turns(3)
         for d in range(4):
             params.corner(d)
         plane.corners()
         weights.settle(2)
         weights.turns(0)
-        line.along(1)
+        tokens_in.along(1)
         weights.turns(1)
         params.finish()
-        line.along(2)
+        for to in range(32):
+            rows_here = small_held[to, own_rows : own_rows + 16, :own_rows].astype(f32)
+            gains[:, to * own_rows : (to + 1) * own_rows] = rows_here[:4]
+        tokens_in.along(2)
         weights.turns(2)
-        line.along(3)
+        first_expert = (place.dp * 4 + place.z) * experts
+
+        @pl.loop(0, 32)
+        def _(d):
+            named = small_held[d, own_rows + 16 : own_rows + 32].astype(f32)[:TOPK]
+            for e in range(experts):
+                matches = jnp.where(named == (first_expert + e).astype(f32), 1.0, 0.0)
+                hits[e, pl.ds(d, 1)] = jnp.sum(matches, axis=0, keepdims=True)
+
+        earlier = lax.broadcasted_iota(jnp.int32, (tok_rows, tok_rows), 0)
+        earlier = earlier < lax.broadcasted_iota(jnp.int32, (tok_rows, tok_rows), 1)
+        earlier = earlier.astype(f32).astype(bf16)
+        for e in range(experts):
+            hit = hits[e]
+            rank = inner(hit.astype(bf16), earlier)
+            place_out[e] = jnp.where(hit > 0.5, rank, -1.0).astype(jnp.int32)
+
+        tokens_in.along(3)
         plane.finish()
-        line.finish()
         weights.finish()
-
-    shapes = [
-        jax.ShapeDtypeStruct((8,) + tokens.shape, tokens.dtype),
-        jax.ShapeDtypeStruct((32,) + small.shape, small.dtype),
-        jax.ShapeDtypeStruct((32,) + cotangent.shape, cotangent.dtype),
-        jax.ShapeDtypeStruct((32 * rows, 3 * width // 8), tokens.dtype),
-        jax.ShapeDtypeStruct((4 * rows, width), tokens.dtype),
-    ]
-    scratch = gather_sems() * 2 + plane_sems(1)
-    scratch += [
-        pltpu.SemaphoreType.DMA((ColumnsFlow.SENDS,)),
-        pltpu.SemaphoreType.DMA((ColumnsFlow.RECVS,)),
-        pltpu.SemaphoreType.DMA((ColumnsFlow.LOCALS,)),
-    ]
-    return hbm_call(
-        kernel,
-        shapes,
-        scratch,
-        "opening",
-        1,
-        (tokens, small, cotangent, query_weight, key_weight, value_weight, output_weight),
-    )
-
-
-def attention_call(tokens_all, gains, wide, tall, head_gains, cosine, sine, cotangent, gathered):
-    count, tok_rows, width = tokens_all.shape
-    rows = count * tok_rows
-    share = tall.shape[0]
-    heads = share // HEAD_DIM
-    block = 2 * tok_rows
-    blocks = rows // block
-    scale = 1.0 / math.sqrt(HEAD_DIM)
-    bf16, f32 = jnp.bfloat16, jnp.float32
-    line = ScatterFlow.scratch(tok_rows, width, bf16, False)
-
-    def kernel(tok, gain, wide_in, tall_in, head_gain, cos, sin, cot, _, *refs):
-        outs, scratch = refs[:8], refs[8:]
-        normed_out, unit_out, row_out, context_out, scale_out, log_out, attended, gathered_out = outs
-        held, wide_ref, tall_ref, normed, unit, qkv, context, part, sums, landed = scratch[:10]
-        ins, stores, send, recv = scratch[10:14]
-        place = Place()
-        entry_barrier(place, "all")
-        flow = ScatterFlow(place, part, attended, scratch[14 : 14 + len(line)], False)
-        others = GatherFlow(
-            place, cot, gathered_out, scratch[-2], scratch[-1], True, others=True
-        )
-
-        def block_in(i):
-            return pltpu.make_async_copy(tok.at[pl.ds(2 * i, 2)], held.at[i], ins.at[i])
-
-        weights = [
-            pltpu.make_async_copy(wide_in, wide_ref, ins.at[blocks]),
-            pltpu.make_async_copy(tall_in, tall_ref, ins.at[blocks + 1]),
-        ]
-        for i in range(blocks):
-            block_in(i).start()
-        for copy in weights:
-            copy.start()
-        for copy in weights:
-            copy.wait()
-        sums[...] = jnp.zeros_like(sums)
+        tokens_in.finish()
+        others.begin()
+        head_gain = gains[1:3, pl.ds(pl.multiple_of(place.col * share, share), share)]
 
         @pl.loop(0, blocks)
         def _(i):
-            block_in(i).wait()
             at = pl.ds(pl.multiple_of(i * block, block), block)
-            values = held[i].reshape(block, width).astype(f32)
+            values = held[pl.ds(2 * i, 2)].reshape(block, width).astype(f32)
             mean = jnp.mean(values * values, axis=1, keepdims=True)
-            low = (values * lax.rsqrt(mean + NORM_EPSILON) * gain[...]).astype(bf16)
+            low = (values * lax.rsqrt(mean + NORM_EPSILON) * gains[0:1]).astype(bf16)
             normed[at] = low
             linear = inner(low, wide_ref[...])
             unit[at] = linear[:, : 2 * share]
@@ -1498,7 +1528,6 @@
             remote(sums, landed.at[col], send.at[0], recv.at[col], place.at(0, 1 - place.blk)).wait_recv()
             exchange(step).wait_send()
 
-        others.begin()
         total = landed[0]
         for col in range(1, 8):
             total = total + landed[col]
@@ -1519,7 +1548,15 @@
 
         out_copies = [
             pltpu.make_async_copy(src, dst, stores.at[n])
-            for n, (src, dst) in enumerate(((normed, normed_out), (unit, unit_out), (qkv, row_out)))
+            for n, (src, dst) in enumerate(
+                (
+                    (unit, unit_out),
+                    (qkv, row_out),
+                    (wide_ref, wide_out),
+                    (tall_ref, tall_out),
+                    (small_held, small_out),
+                )
+            )
         ]
         for copy in out_copies:
             copy.start()
@@ -1548,10 +1585,18 @@
             rows_here = inner(context[at], tall_ref[...]).astype(bf16)
             part[pl.ds(2 * i, 2)] = rows_here.reshape(2, tok_rows, width)
 
-        last = pltpu.make_async_copy(context, context_out, stores.at[3])
-        last.start()
         flow.begin()
         others.along(2)
+        for i in range(blocks):
+            at = slice(i * block, (i + 1) * block)
+            normed_t[:, at] = jnp.transpose(normed[at])
+            context_t[:, at] = jnp.transpose(context[at])
+        last = [
+            pltpu.make_async_copy(normed_t, normed_out, stores.at[5]),
+            pltpu.make_async_copy(context_t, context_out, stores.at[6]),
+        ]
+        for copy in last:
+            copy.start()
         flow.stage3(0)
         flow.stage3(1)
         flow.chain(0)
@@ -1568,23 +1613,28 @@
         others.corner(2)
         others.corner(3)
         others.finish()
-        for copy in out_copies + [last]:
+        for copy in out_copies + last:
             copy.wait()
 
     shapes = [
-        jax.ShapeDtypeStruct((rows, width), bf16),
+        jax.ShapeDtypeStruct((width, rows), bf16),
         jax.ShapeDtypeStruct((rows, 2 * share), f32),
         jax.ShapeDtypeStruct((rows, 3 * share), bf16),
-        jax.ShapeDtypeStruct((rows, share), bf16),
+        jax.ShapeDtypeStruct((share, rows), bf16),
         jax.ShapeDtypeStruct((rows, 8), f32),
         jax.ShapeDtypeStruct((rows, 8), f32),
         jax.ShapeDtypeStruct((tok_rows, width), f32),
-        jax.ShapeDtypeStruct(gathered.shape, gathered.dtype),
+        jax.ShapeDtypeStruct((32,) + small.shape, bf16),
+        jax.ShapeDtypeStruct((32,) + cotangent.shape, bf16),
+        jax.ShapeDtypeStruct((width, 3 * share), bf16),
+        jax.ShapeDtypeStruct((share, width), bf16),
+        jax.ShapeDtypeStruct((4, width), f32),
+        jax.ShapeDtypeStruct((experts, 32, tok_rows), jnp.int32),
     ]
     scratch = [
-        pltpu.VMEM((blocks, 2, tok_rows, width), bf16),
-        pltpu.VMEM(wide.shape, bf16),
-        pltpu.VMEM(tall.shape, bf16),
+        pltpu.VMEM((8, tok_rows, width), bf16),
+        pltpu.VMEM((width, 3 * share), bf16),
+        pltpu.VMEM((share, width), bf16),
         pltpu.VMEM((rows, width), bf16),
         pltpu.VMEM((rows, 2 * share), f32),
         pltpu.VMEM((rows, 3 * share), bf16),
@@ -1592,15 +1642,22 @@
         pltpu.VMEM((8, tok_rows, width), bf16),
         pltpu.VMEM((8, rows), f32),
         pltpu.VMEM((8, 8, rows), f32),
-        pltpu.SemaphoreType.DMA((blocks + 2,)),
-        pltpu.SemaphoreType.DMA((4,)),
+        pltpu.VMEM((32,) + small.shape, bf16),
+        pltpu.VMEM((experts, 32, tok_rows), f32),
+        pltpu.VMEM((width, rows), bf16),
+        pltpu.VMEM((share, rows), bf16),
+        pltpu.SemaphoreType.DMA((7,)),
         pltpu.SemaphoreType.DMA((8,)),
         pltpu.SemaphoreType.DMA((8,)),
     ]
-    args = (tokens_all, gains, wide, tall, head_gains, cosine, sine, cotangent, gathered)
-    return hbm_call(
-        kernel, shapes, scratch + line + gather_sems(), "attention", 5, args, {8: 7}, (1, 4, 5, 6), (4, 5)
-    )
+    scratch += line + gather_sems() * 3 + plane_sems(1)
+    scratch += [
+        pltpu.SemaphoreType.DMA((ColumnsFlow.SENDS,)),
+        pltpu.SemaphoreType.DMA((ColumnsFlow.RECVS,)),
+        pltpu.SemaphoreType.DMA((ColumnsFlow.LOCALS,)),
+    ]
+    args = (tokens, small, cotangent, query_weight, key_weight, value_weight, output_weight, cosine, sine)
+    return hbm_call(kernel, shapes, scratch, "attention", 5, args, (7, 8), (4, 5, 11, 12))
 
 
 def run_units(work, first, last):
@@ -1664,32 +1721,44 @@
     ]
     scratch = gather_sems() * 2 + PickWork.scratch(cotangent_all, down_weight, per)
     return hbm_call(
-        kernel, shapes, scratch, "features", 6, (features, probs, places, cotangent_all, down_weight), None, (2,)
-    )
-
-
-def experts_back_call(part, dealt, places, hidden, weight):
-    sums = ScatterFlow.scratch(part.shape[1], part.shape[2], part.dtype, True)
-    out_shape = jax.ShapeDtypeStruct((places.shape[0], places.shape[2], part.shape[2]), part.dtype)
-
-    def kernel(part_ref, dealt_ref, place_ref, hidden_ref, weight_ref, out, dealt_out, mixed, *scratch):
+        kernel, shapes, scratch, "features", 6, (features, probs, places, cotangent_all, down_weight), (2,)
+    )
+
+
+def experts_back_call(input_rows, row_grads, places, hidden, weight, tok_rows):
+    width = input_rows.shape[2]
+    pairs, experts, pair_rows = places.shape
+    per = input_rows.shape[1] // pairs
+    sums = ScatterFlow.scratch(tok_rows, width, input_rows.dtype, True)
+    out_shape = jax.ShapeDtypeStruct((pairs, pair_rows, width), input_rows.dtype)
+    dealt = jax.ShapeDtypeStruct((2 * pairs, 8, tok_rows), jnp.float32)
+    put_scratch = PutWork.scratch(input_rows, per)
+
+    def kernel(source, grad_ref, place_ref, hidden_ref, weight_ref, out, dealt_out, mixed, *scratch):
         place = Place()
         entry_barrier(place, "all")
-        deal = DealFlow(place, dealt_ref, dealt_out, *scratch[:3])
-        flow = ScatterFlow(place, part_ref, out, scratch[3 : 3 + len(sums)], True)
-        work = OutputWork(place_ref, hidden_ref, weight_ref, mixed, scratch[3 + len(sums) :])
-        deal.begin()
-        flow.begin()
+        stage, deals = scratch[:2]
+        rest = scratch[2 + len(put_scratch) + 3 :]
+        deal = DealFlow(place, deals, dealt_out, *scratch[2 + len(put_scratch) :][:3])
+        flow = MadeFlow(place, out, rest[: len(sums)], stage)
+        put = PutWork(place, place_ref, source, grad_ref, flow, deals, scratch[2 : 2 + len(put_scratch)])
+        work = OutputWork(place_ref, hidden_ref, weight_ref, mixed, rest[len(sums) :])
+        put.load(3, 0, 0).start()
         work.begin()
+        deals[...] = jnp.zeros_like(deals)
+        put.column(3)
+        put.column(2)
         for i in range(4):
             flow.stage1(i)
-        run_units(work, 0, 8)
+        put.column(1)
+        put.column(0)
+        deal.begin()
         flow.stage2(0)
         flow.stage2(1)
-        run_units(work, 8, 12)
+        run_units(work, 0, 8)
         flow.stage2(2)
         flow.stage2(3)
-        run_units(work, 12, 16)
+        run_units(work, 8, 16)
         flow.stage3(0)
         flow.stage3(1)
         flow.chain(0)
@@ -1703,14 +1772,14 @@
         work.finish()
         deal.finish()
 
-    shapes = [
-        jax.ShapeDtypeStruct(part.shape[1:], jnp.float32),
-        jax.ShapeDtypeStruct(dealt.shape, dealt.dtype),
-        out_shape,
+    shapes = [jax.ShapeDtypeStruct((tok_rows, width), jnp.float32), dealt, out_shape]
+    scratch = [
+        pltpu.VMEM((2, 4, tok_rows, width), input_rows.dtype),
+        pltpu.VMEM(dealt.shape, jnp.float32),
     ]
-    scratch = DealFlow.scratch() + sums + OutputWork.scratch(hidden, weight, out_shape)
+    scratch += put_scratch + DealFlow.scratch() + sums + OutputWork.scratch(hidden, weight, out_shape)
     return hbm_call(
-        kernel, shapes, scratch, "experts_back", 3, (part, dealt, places, hidden, weight), None, (2,)
+        kernel, shapes, scratch, "experts_back", 3, (input_rows, row_grads, places, hidden, weight), (1, 2)
     )
 
 
@@ -1718,7 +1787,7 @@
     grad, logit_grad, out_part, tokens, gain, feature_row, wide, tall, head_gains, cosine, sine, kept
 ):
     tok_rows, width = grad.shape
-    rows = kept[0].shape[0]
+    rows = kept[0].shape[1]
     share = tall.shape[0]
     heads = share // HEAD_DIM
     own_rows = width // 32
@@ -1730,8 +1799,8 @@
     bf16, f32 = jnp.bfloat16, jnp.float32
     line = ScatterFlow.scratch(tok_rows, width, bf16, False)
     mixed = ScatterFlow.scratch(height, width, bf16, True)
-    sums = SumsFlow.scratch((band_rows, 3 * share), (share // 4, width))
-    flow_scratch = line + mixed + mixed[-3:] + sums + DealFlow.scratch() + gather_sems() * 2
+    sums = SumsFlow.scratch(((band_rows, 2 * share), (share // 4, width), (band_rows, share)))
+    flow_scratch = line + mixed + mixed[-5:] + sums + DealFlow.scratch() + gather_sems() * 2
     flow_scratch += [pltpu.SemaphoreType.REGULAR]
 
     def kernel(*refs):
@@ -1751,7 +1820,7 @@
 
         place = Place()
         entry_barrier(place, "all")
-        line_scratch, mixed_scratch, more = take(len(line)), take(len(mixed)), take(3)
+        line_scratch, mixed_scratch, more = take(len(line)), take(len(mixed)), take(5)
         weights = SumsFlow(place, wide_out, tall_out, take(len(sums)))
         deal = DealFlow(place, deals, dealt, *take(3))
         gather = GatherFlow(place, grad_ref, grads, *take(2), False)
@@ -1760,7 +1829,7 @@
         flow = ScatterFlow(place, grads, normed_grad, line_scratch, False)
         first = ScatterFlow(place, part_ref, first_out, mixed_scratch, True, (0, height))
         second = ScatterFlow(
-            place, part_ref, second_out, mixed_scratch[:-3] + more, True, (height, height)
+            place, part_ref, second_out, mixed_scratch[:-5] + more, True, (height, height)
         )
         gather.begin()
         logits.begin()
@@ -1798,6 +1867,10 @@
         gather.finish()
         for copy in loads:
             copy.wait()
+        first.stage3(2)
+        first.chain(1)
+        first.stage3(3)
+        tell_partners(place, freed)
 
         @pl.loop(0, blocks)
         def _(i):
@@ -1805,22 +1878,23 @@
             values = grads[pl.ds(2 * i, 2)].reshape(block, width)
             context_grad[at] = inner(values, tall_ref[...], 1, 1).astype(bf16)
 
-        first.stage3(2)
-        first.chain(1)
+        wait_partners(place, freed)
+        first.leave_all()
+        second.begin((3, 2, 1))
         first.chain(2)
-        first.stage3(3)
 
         @pl.loop(0, 4)
         def _(i):
             lanes = pl.ds(pl.multiple_of(i * band_rows, band_rows), band_rows)
             values = grads[:, :, lanes].reshape(rows, band_rows)
-            tall_grad[:, lanes] = inner(context[...], values, 0, 0).astype(bf16)
+            tall_grad[:, lanes] = inner(context[...], values).astype(bf16)
 
         for k in range(4):
             at = pl.ds(pl.multiple_of(place.column(k) * own_rows, own_rows), own_rows)
             weights.acc[1][k] = tall_grad[at]
+        weights.corners(1)
         first.final()
-        tell_partners(place, freed)
+        second.begin((0,))
 
         def back_block(h, i):
             seen = (i + 1) * block
@@ -1847,28 +1921,34 @@
                 grad_v[:seen, lanes] += value_part
 
         back_block(0, 3)
-        wait_partners(place, freed)
-        second.begin()
-        weights.corners(1)
         back_block(0, 2)
-        for i in range(4):
-            second.stage1(i)
+        second.stage1(0)
+        second.stage1(1)
         back_block(0, 1)
         back_block(0, 0)
+        second.stage1(2)
+        second.stage1(3)
         back_block(1, 3)
+        back_block(1, 2)
+        weights.sides(1)
         second.stage2(0)
-        weights.sides(1)
-        back_block(1, 2)
+        back_block(1, 1)
+        back_block(1, 0)
+        low_grads[:, 2 * share :] = grad_v[...].astype(bf16)
+
+        def band_grad(which, k):
+            band = pl.ds(pl.multiple_of(place.column(k) * band_rows, band_rows), band_rows)
+            lanes = slice(2 * share, 3 * share) if which == 2 else slice(0, 2 * share)
+            weights.acc[which][k] = inner(normed[band], low_grads[:, lanes]).astype(bf16)
+
+        for k in (3, 2, 1, 0):
+            band_grad(2, k)
+
         second.stage2(1)
-        back_block(1, 1)
-        second.stage2(2)
-        back_block(1, 0)
-        second.stage2(3)
 
         @pl.loop(0, blocks)
         def _(i):
             at = pl.ds(pl.multiple_of(i * block, block), block)
-            low_grads[at, 2 * share :] = grad_v[at].astype(bf16)
             for n, grad_n in enumerate((grad_q, grad_k)):
                 total = jnp.zeros((block, 1), f32)
                 for h in range(heads):
@@ -1898,7 +1978,6 @@
             exchange(step).start()
 
         landed[place.col] = dots[...]
-        second.stage3(0)
 
         @pl.loop(1, 8)
         def _(step):
@@ -1915,11 +1994,8 @@
             low = scale_ref[:, n : n + 1] * (grad_n[...] - mine * columns[:, n : n + 1])
             low_grads[:, n * share : (n + 1) * share] = low.astype(bf16)
 
-        def wide_grad(k):
-            lanes = pl.ds(pl.multiple_of(place.column(k) * band_rows, band_rows), band_rows)
-            weights.acc[0][k] = inner(normed[:, lanes], low_grads[...], 0, 0).astype(bf16)
-
-        wide_grad(3)
+        weights.corners(2)
+        band_grad(0, 3)
         weights.corners(0)
 
         @pl.loop(0, blocks)
@@ -1929,25 +2005,30 @@
             grads[pl.ds(2 * i, 2)] = values.reshape(2, tok_rows, width)
 
         flow.begin()
-        wide_grad(2)
-        wide_grad(1)
-        second.stage3(1)
-        second.chain(0)
+        weights.sides(2)
+        band_grad(0, 2)
+        band_grad(0, 1)
         flow.stage3(0)
         weights.sides(0)
         flow.stage3(1)
-        wide_grad(0)
+        band_grad(0, 0)
+        second.stage2(2)
         flow.chain(0)
+        weights.total(2)
+        weights.hand_out((2,))
+        second.stage2(3)
+        flow.stage3(2)
+        flow.chain(1)
+        weights.total(0)
+        weights.hand_out((0, 1))
+        second.stage3(0)
+        second.stage3(1)
+        flow.chain(2)
+        flow.stage3(3)
+        second.chain(0)
         second.stage3(2)
         second.chain(1)
         second.chain(2)
-        flow.stage3(2)
-        flow.chain(1)
-        weights.total(0)
-        weights.hand_out_wide()
-        flow.chain(2)
-        flow.stage3(3)
-        second.stage3(3)
         weights.total(1)
         weights.hand_out_tall()
         flow.final()
@@ -1960,6 +2041,7 @@
             deals[to, 0:1, :own_rows] = attention_row[:, lanes]
             deals[to, 3:4, :own_rows] = feature_ref[:, lanes]
         deal.begin()
+        second.stage3(3)
         second.final()
         logits.finish()
         weights.finish()
@@ -1983,10 +2065,10 @@
         pltpu.VMEM((tok_rows, width), bf16),
         pltpu.VMEM(wide.shape, bf16),
         pltpu.VMEM(tall.shape, bf16),
-        pltpu.VMEM((rows, width), bf16),
+        pltpu.VMEM((width, rows), bf16),
         pltpu.VMEM((rows, 2 * share), f32),
         pltpu.VMEM((rows, 3 * share), bf16),
-        pltpu.VMEM((rows, share), bf16),
+        pltpu.VMEM((share, rows), bf16),
         pltpu.VMEM((rows, share), bf16),
         pltpu.VMEM((rows, share), f32),
         pltpu.VMEM((rows, share), f32),
@@ -2009,10 +2091,16 @@
         "attention_back",
         2,
         args + tuple(kept),
-        None,
         (4, 5, 8, 9, 10, 15, 16),
         (6,),
     )
+
+
+def turn_tables(count):
+    half = HEAD_DIM // 2
+    frequencies = np.exp(-math.log(ROPE_BASE) * 2.0 * np.arange(half) / HEAD_DIM).astype(np.float32)
+    angles = np.arange(count, dtype=np.float32)[:, None] * frequencies[None, :]
+    return np.cos(angles), np.sin(angles)
 
 
 def product(left, right, sums, batches=((), ()), out=jnp.float32):
@@ -2049,35 +2137,24 @@
     f32, bf16 = jnp.float32, jnp.bfloat16
 
     gains = jnp.stack([attention_gain, query_gain, key_gain, feature_gain])
-    named_here = routes.astype(bf16).reshape(own_rows, tok_rows * TOPK // own_rows)
-    filled = EXPERTS + named_here.shape[1]
-    small = jnp.concatenate([router_weight, named_here], axis=1)
-    small = jnp.concatenate([small, jnp.pad(gains, ((0, 28), (0, filled - own_rows)))], axis=0)
-    small = jnp.pad(small, ((0, 0), (0, 128 - filled)))
-    tokens_all, small_all, cotangent_all, wide_weight, tall_weight = opening_call(
-        tokens, small, cotangent, query_weight, key_weight, value_weight, output_weight
-    )
-    routes_all = small_all[:, :own_rows, EXPERTS:filled].astype(jnp.int32).reshape(devices, tok_rows, TOPK)
+    small = jnp.concatenate(
+        [
+            jnp.pad(router_weight, ((0, 0), (0, 128 - EXPERTS))),
+            jnp.pad(gains, ((0, 12), (0, 128 - own_rows))),
+            jnp.pad(routes.T.astype(bf16), ((0, 16 - TOPK), (0, 0))),
+        ],
+        axis=0,
+    )
+    half_cos, half_sin = turn_tables(seq_rows)
+    cosine = np.concatenate([half_cos, half_cos], axis=1)
+    sine = np.concatenate([-half_sin, half_sin], axis=1)
+    *kept, attended, small_all, cotangent_all, wide_weight, tall_weight, gain_all, slots = attention_call(
+        tokens, small, cotangent, query_weight, key_weight, value_weight, output_weight, cosine, sine, experts_here
+    )
     router_full = small_all[:, :own_rows, :EXPERTS].reshape(model_width, EXPERTS)
-    gain_all = small_all[:, own_rows : own_rows + 4, :own_rows].astype(f32)
-    gain_all = gain_all.transpose(1, 0, 2).reshape(4, model_width)
     gain_attention, gain_feature = gain_all[0], gain_all[3]
     head_gains = lax.dynamic_slice_in_dim(gain_all[1:3], column * share, share, axis=1)
 
-    half_cos, half_sin = rope_tables(jnp.arange(seq_rows, dtype=jnp.int32), HEAD_DIM)
-    cosine = jnp.concatenate([half_cos, half_cos], axis=1)
-    sine = jnp.concatenate([-half_sin, half_sin], axis=1)
-    *kept, attended, cotangent_all = attention_call(
-        tokens_all,
-        gain_attention[None],
-        wide_weight,
-        tall_weight,
-        head_gains,
-        cosine,
-        sine,
-        cotangent,
-        cotangent_all,
-    )
     tokens_f = tokens.astype(f32)
     residual = tokens_f + attended
     features_f, feature_pull = jax.vjp(norm_apply, residual, gain_feature)
@@ -2086,14 +2163,10 @@
     router_probs = jax.nn.softmax(logits, axis=-1)
 
     first_expert = (lax.axis_index(DP) * 4 + lax.axis_index(SP)) * experts_here
-    expert_ids = first_expert + jnp.arange(experts_here, dtype=jnp.int32)
-    named = jnp.any(routes_all[:, None] == expert_ids[None, :, None, None], axis=3)
-    earlier = (jnp.arange(tok_rows)[:, None] < jnp.arange(tok_rows)[None, :]).astype(bf16)
-    rank = product(named.astype(bf16), earlier, ((2,), (0,))).astype(jnp.int32)
     pairs, pair_rows, per = devices // 2, 2 * tok_rows, 2 * CAP
-    places = jnp.where(named, rank, -per).reshape(pairs, 2, experts_here, tok_rows)
-    places = places + CAP * jnp.arange(2, dtype=jnp.int32)[None, :, None, None]
-    places = places.transpose(0, 2, 1, 3).reshape(pairs, experts_here, pair_rows)
+    slots = slots.reshape(experts_here, pairs, 2, tok_rows).transpose(1, 0, 2, 3)
+    second = CAP * jnp.arange(2, dtype=jnp.int32)[None, None, :, None]
+    places = jnp.where(slots < 0, -1, slots + second).reshape(pairs, experts_here, pair_rows)
     cotangent_all = cotangent_all.reshape(pairs, pair_rows, model_width)
     features_all, probs_all, grad_rows, plain_grads = features_call(
         features, router_probs.T, places, cotangent_all, down_weight, per
@@ -2104,10 +2177,8 @@
     weighted_hidden, gate_grad, up_grad, input_rows, row_grads = run_experts(
         expert_rows, plain_grads, row_probs, gate_weight, up_weight
     )
-    input_part, token_grad = put_rows_back(places, input_rows, row_grads)
-    input_part = input_part.reshape(devices, tok_rows, model_width)
     input_grad, prob_parts, out_part = experts_back_call(
-        input_part, token_grad, places, weighted_hidden, down_weight
+        input_rows, row_grads, places, weighted_hidden, down_weight, tok_rows
     )
     out_part = out_part.reshape(devices, tok_rows, model_width)
 

time: 677 us -> 651 us (0.962)
  Pallas kernels: 631 us -> 611 us
    pallas_call x1 -> x0, Pallas kernels: 14.8 us -> none  [put_rows_back(): pl.pallas_call(kernel, out_shape=[jax.ShapeDtypeStruct((pairs, pair_rows,...]
    pallas_call x5 -> x4, Pallas kernels: 531 us -> 527 us  [hbm_call(): pl.pallas_call(kernel, out_shape=shapes, in_specs=[pl.BlockSpec(memory_sp...]
where the time goes in v4:
time: 651 us; the launch traced here: 642 us
  Pallas kernels  611 us (94%)
  other arithmetic  15 us (2%)
  local copies, waits for them, and re-layouts  9.34 us (1%)
    pallas_call x4, Pallas kernels, hbm_call(): pl.pallas_call(kernel, out_shape=shapes, in_specs=[pl.BlockSpec(memory_sp...  527 us
    pallas_call x1, Pallas kernels, expert_weight_grads(): pl.pallas_call(kernel, out_shape=[jax.ShapeDtypeStruct((experts, width, h...  35.4 us
    pallas_call x1, Pallas kernels, run_experts(): pl.pallas_call(kernel, out_shape=[narrow, narrow, narrow, jax.ShapeDtypeS...  34.4 us
    pallas_call x1, Pallas kernels, pick_rows(): pl.pallas_call(kernel, out_shape=[jax.ShapeDtypeStruct((experts, pairs *...  14.6 us

profile of v4, /device:TPU:0, one launch (start us, length us, event | category | flops | bytes accessed | tf_op | source)
XLA Modules:
  0.0 642.0 jit_solution(2475184291093324024)
XLA Ops:
  1.4 0.7 fusion.22
  2.1 1.3 fusion.12.sml
  3.4 166.9 %attention.1 = (bf16[2048,1024]{1,0:T(8,128)(2,1)}, f32[1024,512]{1,0:T(8,128)}, bf16[1024,768]{1,0:T(8,128)(2,1)}, bf16[256,1024]{1,0:T(8,128)(2,1)}, f32[1024,...) custom-call(bf16[128,2048]{1,0:T(8,128)(2,1)} %refs_3_.1, ...), custom_call_target="tpu_custom_call" | custom-call | tf_op jit(solution)/shard_map/attention/pallas_call | solution.py:1388
  170.3 1.6 multiply_reduce_fusion.2
  171.9 0.8 slice.40
  172.6 1.4 fusion.31
  174.7 0.9 fusion.7
  176.5 1.3 slice.37
  178.8 80.9 %features.1 = (bf16[32,128,2048]{2,1,0:T(8,128)(2,1)}, f32[32,64,128]{2,1,0:T(8,128)}, bf16[4,768,2048]{2,1,0:T(8,128)(2,1)}, f32[4,768,512]{2,1,0:T(8,128)}) custom-call(bf16[128,2048]{1,0:T(8,128)(2,1)} %copy-done.1, f32[64,128]{1,0:T(8,128)} %fusion.29.prob_ref, s32[16,4,256]{2,1,0:T(4,128)} %reshape.111.place_ref, bf16[16,256,2048]{2,1,0:T(8,128)(2,1)} %bitcast.48, ...), custom_call_target="tpu_custom_call" | custom-call | tf_op jit(solution)/shard_map/features/pallas_call | solution.py:1388
  259.7 1.6 constant_dynamic-slice_fusion.1.prob_ref
  261.3 14.6 %pick_rows.1 = (bf16[4,768,2048]{2,1,0:T(8,128)(2,1)}, f32[4,768,1]{2,1,0:T(8,128)}) custom-call(s32[16,4,256]{2,1,0:T(4,128)} %reshape.111.place_ref, f32[32,4,128]{2,1,0:T(4,128)} %constant_dynamic-slice_fusion.1.prob_ref, bf16[16,256,2048]{2,1,0:T(8,128)(2,1)} %bitcast.45), custom_call_target="tpu_custom_call" | custom-call | tf_op jit(solution)/shard_map/pick_rows/pallas_call | solution.py:723
  275.9 34.4 %run_experts.1 = (bf16[4,768,512]{2,1,0:T(8,128)(2,1)}, bf16[4,768,512]{2,1,0:T(8,128)(2,1)}, bf16[4,768,512]{2,1,0:T(8,128)(2,1)}, bf16[4,768,2048]{2,1,0:T(8,128)(2,1)}, f32[4,768,1]{2,1,0:T(8,128)}) custom-call(bf16[4,768,2048]{2,1,0:T(8,128)(2,1)} %get-tuple-element.58.x, f32[4,768,512]{2,1,0:T(8,128)} %get-tuple-element.59.plain_ref, ...), custom_call_target="tpu_custom_call" | custom-call | tf_op jit(solution)/shard_map/run_experts/pallas_call | solution.py:772
  310.3 90.4 %experts_back.1 = (f32[128,2048]{1,0:T(8,128)}, f32[32,8,128]{2,1,0:T(8,128)}, bf16[16,256,2048]{2,1,0:T(8,128)(2,1)}) custom-call(bf16[4,768,2048]{2,1,0:T(8,128)(2,1)} %get-tuple-element.61.source, f32[4,768,1]{2,1,0:T(8,128)} %get-tuple-element.62.grad_ref, s32[16,4,256]{2,1,0:T(4,128)} %reshape.111.place_ref, ...), custom_call_target="tpu_custom_call" | custom-call | tf_op jit(solution)/shard_map/experts_back/pallas_call | solution.py:1388
  400.7 0.9 slice_reduce_fusion
  401.7 2.3 multiply_reduce_fusion
  404.9 1.2 fusion.30.refs_0_
  406.0 188.6 %attention_back.1 = (bf16[32,64,128]{2,1,0:T(8,128)(2,1)}, f32[64,2048]{1,0:T(8,128)}, f32[64,2048]{1,0:T(8,128)}, f32[128,2048]{1,0:T(8,128)}, bf16[3,64,2048]{...) custom-call(bf16[128,2048]{1,0:T(8,128)(2,1)} %fusion.30.refs_0_, bf16[64,128]{1,0:T(8,128)(2,1)} %reshape.116.refs_1_, ...), custom_call_target="tpu_custom_call" | custom-call | tf_op jit(solution)/shard_map/attention_back/pallas_call | solution.py:1388
  594.7 1.6 fusion.2
  596.3 3.1 fusion.1
  600.0 0.8 convert_element_type.65
  600.8 1.6 reshape.119
  602.4 2.6 fusion.5
  605.0 1.2 bitcast_convert_fusion
  606.2 35.4 %expert_weight_grads.1 = (f32[4,2048,512]{2,1,0:T(8,128)}, f32[4,2048,512]{2,1,0:T(8,128)}, f32[4,512,2048]{2,1,0:T(8,128)}) custom-call(bf16[4,768,2048]{2,1,0:T(8,128)(2,1)} %get-tuple-element.58.x, bf16[4,768,2048]{2,1,0:T(8,128)(2,1)} %get-tuple-element.82.c, bf16[4,768,512]{2,1,0:T(8,128)(2,1)} %get-tuple-element.63.hidden_ref.low, ...), custom_call_target="tpu_custom_call" | custom-call | flops 19327352832 | bytes 100663296 | tf_op jit(solution)/shard_map/expert_weight_grads/pallas_call | solution.py:1040
  (30 shorter events, 4.6 us)
Async XLA Ops:
  176.5 2.3 copy-start.1
  310.3 94.6 %copy-start.2 = (bf16[128,2048]{1,0:T(8,128)(2,1)S(1)}, bf16[128,2048]{1,0:T(8,128)(2,1)}, u32[]{:S(2)}) copy-start(bf16[128,2048]{1,0:T(8,128)(2,1)} %cot.1) | copy-start | bytes 1572868
  406.0 188.6 %copy-start = (bf16[128,2048]{1,0:T(8,128)(2,1)S(1)}, bf16[128,2048]{1,0:T(8,128)(2,1)}, u32[]{:S(2)}) copy-start(bf16[128,2048]{1,0:T(8,128)(2,1)} %refs_3_.1) | copy-start | bytes 1572868
  406.0 188.6 %copy-start.5 = (f32[1,2048]{1,0:T(1,128)S(1)}, f32[1,2048]{1,0:T(1,128)}, u32[]{:S(2)}) copy-start(f32[1,2048]{1,0:T(1,128)} %get-tuple-element.99.refs_4_) | copy-start | bytes 24580
  594.6 4.8 copy-start.6
  594.6 5.3 copy-start.4
  594.7 10.4 %copy-start.3 = (bf16[3,64,2048]{2,1,0:T(8,128)(2,1)S(1)}, bf16[3,64,2048]{2,1,0:T(8,128)(2,1)}, u32[]{:S(2)}) copy-start(bf16[3,64,2048]{2,1,0:T(8,128)(2,1)} %get-tuple-element.78) | copy-start | bytes 2359300

commit v5 on v4

--- a/solution.py
+++ b/solution.py
@@ -708,7 +708,7 @@
 def pick_rows(places, probs, features, per):
     pairs, experts, pair_rows = places.shape
     width = features.shape[-1]
-    step = 2
+    step = 4
 
     def kernel(place_ref, prob_ref, feature_ref, row_ref, row_prob_ref):
         for i in range(step):
@@ -1425,9 +1425,9 @@
     line = ScatterFlow.scratch(tok_rows, width, bf16, False)
 
     def kernel(tok, sml, cot, wq, wk, wv, wo, cos, sin, *refs):
-        outs, scratch = refs[:13], refs[13:]
+        outs, scratch = refs[:14], refs[14:]
         normed_out, unit_out, row_out, context_out, scale_out, log_out = outs[:6]
-        attended, small_out, gathered_out, wide_out, tall_out, gains, place_out = outs[6:]
+        attended, small_out, gathered_out, wide_out, tall_out, gains, place_out, head_out = outs[6:]
         held, wide_ref, tall_ref, normed, unit, qkv, context, part, sums, landed = scratch[:10]
         small_held, hits, normed_t, context_t, stores, send, recv = scratch[10:17]
         rest = list(scratch[17:])
@@ -1487,7 +1487,11 @@
         for e in range(experts):
             hit = hits[e]
             rank = inner(hit.astype(bf16), earlier)
-            place_out[e] = jnp.where(hit > 0.5, rank, -1.0).astype(jnp.int32)
+            shift = lax.broadcasted_iota(jnp.int32, hit.shape, 0) % 2 * CAP
+            slots = jnp.where(hit > 0.5, rank.astype(jnp.int32) + shift, -1)
+            for d in range(32):
+                lanes = slice(d % 2 * tok_rows, (d % 2 + 1) * tok_rows)
+                place_out[d // 2, e : e + 1, lanes] = slots[d : d + 1]
 
         tokens_in.along(3)
         plane.finish()
@@ -1495,6 +1499,7 @@
         tokens_in.finish()
         others.begin()
         head_gain = gains[1:3, pl.ds(pl.multiple_of(place.col * share, share), share)]
+        head_out[...] = head_gain
 
         @pl.loop(0, blocks)
         def _(i):
@@ -1629,7 +1634,8 @@
         jax.ShapeDtypeStruct((width, 3 * share), bf16),
         jax.ShapeDtypeStruct((share, width), bf16),
         jax.ShapeDtypeStruct((4, width), f32),
-        jax.ShapeDtypeStruct((experts, 32, tok_rows), jnp.int32),
+        jax.ShapeDtypeStruct((16, experts, 2 * tok_rows), jnp.int32),
+        jax.ShapeDtypeStruct((2, share), f32),
     ]
     scratch = [
         pltpu.VMEM((8, tok_rows, width), bf16),
@@ -1657,7 +1663,7 @@
         pltpu.SemaphoreType.DMA((ColumnsFlow.LOCALS,)),
     ]
     args = (tokens, small, cotangent, query_weight, key_weight, value_weight, output_weight, cosine, sine)
-    return hbm_call(kernel, shapes, scratch, "attention", 5, args, (7, 8), (4, 5, 11, 12))
+    return hbm_call(kernel, shapes, scratch, "attention", 5, args, (7, 8), (4, 5, 11, 12, 13))
 
 
 def run_units(work, first, last):
@@ -2148,12 +2154,21 @@
     half_cos, half_sin = turn_tables(seq_rows)
     cosine = np.concatenate([half_cos, half_cos], axis=1)
     sine = np.concatenate([-half_sin, half_sin], axis=1)
-    *kept, attended, small_all, cotangent_all, wide_weight, tall_weight, gain_all, slots = attention_call(
+    (
+        *kept,
+        attended,
+        small_all,
+        cotangent_all,
+        wide_weight,
+        tall_weight,
+        gain_all,
+        places,
+        head_gains,
+    ) = attention_call(
         tokens, small, cotangent, query_weight, key_weight, value_weight, output_weight, cosine, sine, experts_here
     )
     router_full = small_all[:, :own_rows, :EXPERTS].reshape(model_width, EXPERTS)
     gain_attention, gain_feature = gain_all[0], gain_all[3]
-    head_gains = lax.dynamic_slice_in_dim(gain_all[1:3], column * share, share, axis=1)
 
     tokens_f = tokens.astype(f32)
     residual = tokens_f + attended
@@ -2164,9 +2179,6 @@
 
     first_expert = (lax.axis_index(DP) * 4 + lax.axis_index(SP)) * experts_here
     pairs, pair_rows, per = devices // 2, 2 * tok_rows, 2 * CAP
-    slots = slots.reshape(experts_here, pairs, 2, tok_rows).transpose(1, 0, 2, 3)
-    second = CAP * jnp.arange(2, dtype=jnp.int32)[None, None, :, None]
-    places = jnp.where(slots < 0, -1, slots + second).reshape(pairs, experts_here, pair_rows)
     cotangent_all = cotangent_all.reshape(pairs, pair_rows, model_width)
     features_all, probs_all, grad_rows, plain_grads = features_call(
         features, router_probs.T, places, cotangent_all, down_weight, per

time: 651 us -> 645 us (level)
  no operation moved by 1% of the time
where the time goes in v5:
time: 645 us; the launch traced here: 636 us
  Pallas kernels  609 us (94%)
  other arithmetic  14 us (2%)
  local copies, waits for them, and re-layouts  7.3 us (1%)
    pallas_call x4, Pallas kernels, hbm_call(): pl.pallas_call(kernel, out_shape=shapes, in_specs=[pl.BlockSpec(memory_sp...  527 us
    pallas_call x1, Pallas kernels, expert_weight_grads(): pl.pallas_call(kernel, out_shape=[jax.ShapeDtypeStruct((experts, width, h...  35.4 us
    pallas_call x1, Pallas kernels, run_experts(): pl.pallas_call(kernel, out_shape=[narrow, narrow, narrow, jax.ShapeDtypeS...  34.4 us

profile of v5, /device:TPU:0, one launch (start us, length us, event | category | flops | bytes accessed | tf_op | source)
XLA Modules:
  0.0 636.4 jit_solution(9068421672611843929)
XLA Ops:
  0.7 0.7 convert_bitcast_fusion
  1.3 0.7 fusion.21
  2.1 1.3 fusion.11.sml
  3.4 166.8 %attention.1 = (bf16[2048,1024]{1,0:T(8,128)(2,1)}, f32[1024,512]{1,0:T(8,128)}, bf16[1024,768]{1,0:T(8,128)(2,1)}, bf16[256,1024]{1,0:T(8,128)(2,1)}, f32[1024,...) custom-call(bf16[128,2048]{1,0:T(8,128)(2,1)} %refs_3_.1, ...), custom_call_target="tpu_custom_call" | custom-call | tf_op jit(solution)/shard_map/attention/pallas_call | solution.py:1388
  170.2 1.6 multiply_reduce_fusion.2
  171.8 1.5 fusion.30
  173.4 1.3 slice.34
  175.7 80.9 %features.1 = (bf16[32,128,2048]{2,1,0:T(8,128)(2,1)}, f32[32,64,128]{2,1,0:T(8,128)}, bf16[4,768,2048]{2,1,0:T(8,128)(2,1)}, f32[4,768,512]{2,1,0:T(8,128)}) custom-call(bf16[128,2048]{1,0:T(8,128)(2,1)} %copy-done.1, f32[64,128]{1,0:T(8,128)} %fusion.28.prob_ref, s32[16,4,256]{2,1,0:T(4,128)} %get-tuple-element.55.place_ref, ...), custom_call_target="tpu_custom_call" | custom-call | tf_op jit(solution)/shard_map/features/pallas_call | solution.py:1388
  256.6 1.6 constant_dynamic-slice_fusion.prob_ref
  258.2 12.0 %pick_rows.1 = (bf16[4,768,2048]{2,1,0:T(8,128)(2,1)}, f32[4,768,1]{2,1,0:T(8,128)}) custom-call(s32[16,4,256]{2,1,0:T(4,128)} %get-tuple-element.55.place_ref, f32[32,4,128]{2,1,0:T(4,128)} %constant_dynamic-slice_fusion.prob_ref, bf16[16,256,2048]{2,1,0:T(8,128)(2,1)} %bitcast.42), custom_call_target="tpu_custom_call" | custom-call | tf_op jit(solution)/shard_map/pick_rows/pallas_call | solution.py:723
  270.2 34.4 %run_experts.1 = (bf16[4,768,512]{2,1,0:T(8,128)(2,1)}, bf16[4,768,512]{2,1,0:T(8,128)(2,1)}, bf16[4,768,512]{2,1,0:T(8,128)(2,1)}, bf16[4,768,2048]{2,1,0:T(8,128)(2,1)}, f32[4,768,1]{2,1,0:T(8,128)}) custom-call(bf16[4,768,2048]{2,1,0:T(8,128)(2,1)} %get-tuple-element.59.x, f32[4,768,512]{2,1,0:T(8,128)} %get-tuple-element.60.plain_ref, ...), custom_call_target="tpu_custom_call" | custom-call | tf_op jit(solution)/shard_map/run_experts/pallas_call | solution.py:772
  304.6 90.4 %experts_back.1 = (f32[128,2048]{1,0:T(8,128)}, f32[32,8,128]{2,1,0:T(8,128)}, bf16[16,256,2048]{2,1,0:T(8,128)(2,1)}) custom-call(bf16[4,768,2048]{2,1,0:T(8,128)(2,1)} %get-tuple-element.62.source, f32[4,768,1]{2,1,0:T(8,128)} %get-tuple-element.63.grad_ref, s32[16,4,256]{2,1,0:T(4,128)} %get-tuple-element.55.place_ref, ...), custom_call_target="tpu_custom_call" | custom-call | tf_op jit(solution)/shard_map/experts_back/pallas_call | solution.py:1388
  395.0 0.9 slice_reduce_fusion
  396.0 2.4 multiply_reduce_fusion
  398.5 0.7 reshape.103.refs_1_
  399.2 1.2 fusion.29.refs_0_
  400.4 188.6 %attention_back.1 = (bf16[32,64,128]{2,1,0:T(8,128)(2,1)}, f32[64,2048]{1,0:T(8,128)}, f32[64,2048]{1,0:T(8,128)}, f32[128,2048]{1,0:T(8,128)}, bf16[3,64,2048]{...) custom-call(bf16[128,2048]{1,0:T(8,128)(2,1)} %fusion.29.refs_0_, bf16[64,128]{1,0:T(8,128)(2,1)} %reshape.103.refs_1_, ...), custom_call_target="tpu_custom_call" | custom-call | tf_op jit(solution)/shard_map/attention_back/pallas_call | solution.py:1388
  589.0 1.6 fusion.2
  590.6 3.1 fusion.1
  594.3 0.8 convert_element_type.65
  595.1 1.6 reshape.106
  596.7 2.6 fusion.5
  599.3 1.2 bitcast_convert_fusion
  600.5 35.4 %expert_weight_grads.1 = (f32[4,2048,512]{2,1,0:T(8,128)}, f32[4,2048,512]{2,1,0:T(8,128)}, f32[4,512,2048]{2,1,0:T(8,128)}) custom-call(bf16[4,768,2048]{2,1,0:T(8,128)(2,1)} %get-tuple-element.59.x, bf16[4,768,2048]{2,1,0:T(8,128)(2,1)} %get-tuple-element.84.c, bf16[4,768,512]{2,1,0:T(8,128)(2,1)} %get-tuple-element.64.hidden_ref.low, ...), custom_call_target="tpu_custom_call" | custom-call | flops 19327352832 | bytes 100663296 | tf_op jit(solution)/shard_map/expert_weight_grads/pallas_call | solution.py:1040
  (25 shorter events, 1.9 us)
Async XLA Ops:
  173.4 2.3 copy-start.1
  304.6 94.6 %copy-start.2 = (bf16[128,2048]{1,0:T(8,128)(2,1)S(1)}, bf16[128,2048]{1,0:T(8,128)(2,1)}, u32[]{:S(2)}) copy-start(bf16[128,2048]{1,0:T(8,128)(2,1)} %cot.1) | copy-start | bytes 1572868
  400.4 188.6 %copy-start = (bf16[128,2048]{1,0:T(8,128)(2,1)S(1)}, bf16[128,2048]{1,0:T(8,128)(2,1)}, u32[]{:S(2)}) copy-start(bf16[128,2048]{1,0:T(8,128)(2,1)} %refs_3_.1) | copy-start | bytes 1572868
  400.4 188.6 %copy-start.5 = (f32[1,2048]{1,0:T(1,128)S(1)}, f32[1,2048]{1,0:T(1,128)}, u32[]{:S(2)}) copy-start(f32[1,2048]{1,0:T(1,128)} %get-tuple-element.101.refs_4_) | copy-start | bytes 24580
  588.9 4.8 copy-start.6
  589.0 5.3 copy-start.4
  589.0 10.4 %copy-start.3 = (bf16[3,64,2048]{2,1,0:T(8,128)(2,1)S(1)}, bf16[3,64,2048]{2,1,0:T(8,128)(2,1)}, u32[]{:S(2)}) copy-start(bf16[3,64,2048]{2,1,0:T(8,128)(2,1)} %get-tuple-element.80) | copy-start | bytes 2359300

commit v6 on v5

--- a/solution.py
+++ b/solution.py
@@ -1025,7 +1025,7 @@
 def expert_weight_grads(rows, grads, weighted, gate_back, up_back):
     experts, slots, width = rows.shape
     hidden = weighted.shape[2]
-    parts = 4
+    parts = 2
     part = width // parts
 
     def kernel(x, c, low, gate, up, gate_out, up_out, down_out):

time: 645 us -> 644 us (level)
  no operation moved by 1% of the time
where the time goes in v6:
time: 644 us; the launch traced here: 636 us
  Pallas kernels  608 us (94%)
  other arithmetic  14 us (2%)
  local copies, waits for them, and re-layouts  7.3 us (1%)
    pallas_call x4, Pallas kernels, hbm_call(): pl.pallas_call(kernel, out_shape=shapes, in_specs=[pl.BlockSpec(memory_sp...  527 us
    pallas_call x1, Pallas kernels, expert_weight_grads(): pl.pallas_call(kernel, out_shape=[jax.ShapeDtypeStruct((experts, width, h...  34.6 us
    pallas_call x1, Pallas kernels, run_experts(): pl.pallas_call(kernel, out_shape=[narrow, narrow, narrow, jax.ShapeDtypeS...  34.4 us

profile of v6, /device:TPU:0, one launch (start us, length us, event | category | flops | bytes accessed | tf_op | source)
XLA Modules:
  0.0 635.5 jit_solution(2013144256958909674)
XLA Ops:
  0.7 0.7 convert_bitcast_fusion
  1.3 0.7 fusion.21
  2.1 1.3 fusion.11.sml
  3.4 166.8 %attention.1 = (bf16[2048,1024]{1,0:T(8,128)(2,1)}, f32[1024,512]{1,0:T(8,128)}, bf16[1024,768]{1,0:T(8,128)(2,1)}, bf16[256,1024]{1,0:T(8,128)(2,1)}, f32[1024,...) custom-call(bf16[128,2048]{1,0:T(8,128)(2,1)} %refs_3_.1, ...), custom_call_target="tpu_custom_call" | custom-call | tf_op jit(solution)/shard_map/attention/pallas_call | solution.py:1388
  170.2 1.6 multiply_reduce_fusion.2
  171.8 1.5 fusion.30
  173.4 1.3 slice.34
  175.7 80.9 %features.1 = (bf16[32,128,2048]{2,1,0:T(8,128)(2,1)}, f32[32,64,128]{2,1,0:T(8,128)}, bf16[4,768,2048]{2,1,0:T(8,128)(2,1)}, f32[4,768,512]{2,1,0:T(8,128)}) custom-call(bf16[128,2048]{1,0:T(8,128)(2,1)} %copy-done.1, f32[64,128]{1,0:T(8,128)} %fusion.28.prob_ref, s32[16,4,256]{2,1,0:T(4,128)} %get-tuple-element.55.place_ref, ...), custom_call_target="tpu_custom_call" | custom-call | tf_op jit(solution)/shard_map/features/pallas_call | solution.py:1388
  256.6 1.6 constant_dynamic-slice_fusion.prob_ref
  258.2 12.0 %pick_rows.1 = (bf16[4,768,2048]{2,1,0:T(8,128)(2,1)}, f32[4,768,1]{2,1,0:T(8,128)}) custom-call(s32[16,4,256]{2,1,0:T(4,128)} %get-tuple-element.55.place_ref, f32[32,4,128]{2,1,0:T(4,128)} %constant_dynamic-slice_fusion.prob_ref, bf16[16,256,2048]{2,1,0:T(8,128)(2,1)} %bitcast.42), custom_call_target="tpu_custom_call" | custom-call | tf_op jit(solution)/shard_map/pick_rows/pallas_call | solution.py:723
  270.2 34.4 %run_experts.1 = (bf16[4,768,512]{2,1,0:T(8,128)(2,1)}, bf16[4,768,512]{2,1,0:T(8,128)(2,1)}, bf16[4,768,512]{2,1,0:T(8,128)(2,1)}, bf16[4,768,2048]{2,1,0:T(8,128)(2,1)}, f32[4,768,1]{2,1,0:T(8,128)}) custom-call(bf16[4,768,2048]{2,1,0:T(8,128)(2,1)} %get-tuple-element.59.x, f32[4,768,512]{2,1,0:T(8,128)} %get-tuple-element.60.plain_ref, ...), custom_call_target="tpu_custom_call" | custom-call | tf_op jit(solution)/shard_map/run_experts/pallas_call | solution.py:772
  304.6 90.4 %experts_back.1 = (f32[128,2048]{1,0:T(8,128)}, f32[32,8,128]{2,1,0:T(8,128)}, bf16[16,256,2048]{2,1,0:T(8,128)(2,1)}) custom-call(bf16[4,768,2048]{2,1,0:T(8,128)(2,1)} %get-tuple-element.62.source, f32[4,768,1]{2,1,0:T(8,128)} %get-tuple-element.63.grad_ref, s32[16,4,256]{2,1,0:T(4,128)} %get-tuple-element.55.place_ref, ...), custom_call_target="tpu_custom_call" | custom-call | tf_op jit(solution)/shard_map/experts_back/pallas_call | solution.py:1388
  395.0 0.9 slice_reduce_fusion
  396.0 2.4 multiply_reduce_fusion
  398.5 0.7 reshape.103.refs_1_
  399.2 1.2 fusion.29.refs_0_
  400.4 188.6 %attention_back.1 = (bf16[32,64,128]{2,1,0:T(8,128)(2,1)}, f32[64,2048]{1,0:T(8,128)}, f32[64,2048]{1,0:T(8,128)}, f32[128,2048]{1,0:T(8,128)}, bf16[3,64,2048]{...) custom-call(bf16[128,2048]{1,0:T(8,128)(2,1)} %fusion.29.refs_0_, bf16[64,128]{1,0:T(8,128)(2,1)} %reshape.103.refs_1_, ...), custom_call_target="tpu_custom_call" | custom-call | tf_op jit(solution)/shard_map/attention_back/pallas_call | solution.py:1388
  589.0 1.6 fusion.2
  590.6 3.1 fusion.1
  594.3 0.8 convert_element_type.65
  595.1 1.6 reshape.106
  596.7 2.6 fusion.5
  599.3 1.2 bitcast_convert_fusion
  600.5 34.6 %expert_weight_grads.1 = (f32[4,2048,512]{2,1,0:T(8,128)}, f32[4,2048,512]{2,1,0:T(8,128)}, f32[4,512,2048]{2,1,0:T(8,128)}) custom-call(bf16[4,768,2048]{2,1,0:T(8,128)(2,1)} %get-tuple-element.59.x, bf16[4,768,2048]{2,1,0:T(8,128)(2,1)} %get-tuple-element.84.c, bf16[4,768,512]{2,1,0:T(8,128)(2,1)} %get-tuple-element.64.hidden_ref.low, ...), custom_call_target="tpu_custom_call" | custom-call | flops 19327352832 | bytes 100663296 | tf_op jit(solution)/shard_map/expert_weight_grads/pallas_call | solution.py:1040
  (25 shorter events, 1.9 us)
Async XLA Ops:
  173.4 2.3 copy-start.1
  304.6 94.6 %copy-start.2 = (bf16[128,2048]{1,0:T(8,128)(2,1)S(1)}, bf16[128,2048]{1,0:T(8,128)(2,1)}, u32[]{:S(2)}) copy-start(bf16[128,2048]{1,0:T(8,128)(2,1)} %cot.1) | copy-start | bytes 1572868
  400.4 188.6 %copy-start = (bf16[128,2048]{1,0:T(8,128)(2,1)S(1)}, bf16[128,2048]{1,0:T(8,128)(2,1)}, u32[]{:S(2)}) copy-start(bf16[128,2048]{1,0:T(8,128)(2,1)} %refs_3_.1) | copy-start | bytes 1572868
  400.4 188.6 %copy-start.5 = (f32[1,2048]{1,0:T(1,128)S(1)}, f32[1,2048]{1,0:T(1,128)}, u32[]{:S(2)}) copy-start(f32[1,2048]{1,0:T(1,128)} %get-tuple-element.101.refs_4_) | copy-start | bytes 24580
  588.9 4.8 copy-start.6
  589.0 5.3 copy-start.4
  589.0 10.4 %copy-start.3 = (bf16[3,64,2048]{2,1,0:T(8,128)(2,1)S(1)}, bf16[3,64,2048]{2,1,0:T(8,128)(2,1)}, u32[]{:S(2)}) copy-start(bf16[3,64,2048]{2,1,0:T(8,128)(2,1)} %get-tuple-element.80) | copy-start | bytes 2359300
